TPU v7x, 32 devices: a whole 2x2x4 slice. The times are simulated.
32 devices in a mesh: dp: 4 (over y, core), seq: 4 (over z), mp: 2 (over x).
Axes of the slice: x: 2, y: 2, z: 4, core: 2. Of those that a mesh axis runs over, the one named last changes fastest.
Arguments:
- trunk_in: bfloat16 [12, 1536, 1536], P('dp', 'seq'), may hold values from -6 to 6
- norm1_gain: float32 [1536], replicated, may hold values from 0.5 to 1.5
- norm1_bias: float32 [1536], replicated, may hold values from -1.75 to 1.75
- w_query: bfloat16 [1536, 512], P(None, 'mp'), may hold values from -0.15625 to 0.15625
- w_key: bfloat16 [1536, 512], P(None, 'mp'), may hold values from -0.15625 to 0.15625
- w_value: bfloat16 [1536, 1536], P(None, 'mp'), may hold values from -0.15625 to 0.15625
- w_rel: bfloat16 [192, 512], P(None, 'mp'), may hold values from -0.4375 to 0.4375
- content_bias: float32 [8, 64], P('mp'), may hold values from -1.25 to 1.25
- pos_bias: float32 [8, 64], P('mp'), may hold values from -1.25 to 1.25
- w_out: bfloat16 [1536, 1536], P('mp'), may hold values from -4 to 4
- b_out: float32 [1536], replicated, may hold values from -1.75 to 1.75
- norm2_gain: float32 [1536], replicated, may hold values from 0.5 to 1.5
- norm2_bias: float32 [1536], replicated, may hold values from -1.75 to 1.75
- w_in: bfloat16 [1536, 3072], P(None, 'mp'), may hold values from -0.15625 to 0.15625
- b_in: float32 [3072], P('mp'), may hold values from -1.75 to 1.75
- w_hid: bfloat16 [3072, 1536], P('mp'), may hold values from -0.109375 to 0.109375
- b_hid: float32 [1536], replicated, may hold values from -1.75 to 1.75
- head_human: bfloat16 [1536, 5313], P('mp'), may hold values from -0.15625 to 0.15625
- bias_human: float32 [5313], replicated, may hold values from -3 to 3
- head_mouse: bfloat16 [1536, 1643], P('mp'), may hold values from -0.15625 to 0.15625
- bias_mouse: float32 [1643], replicated, may hold values from -3 to 3
- species: int32 [12], P('dp'), may hold values from 0 to 1
- targets_human: int32 [12, 1536, 5313], P('dp', 'seq'), may hold values from 0 to 5
- targets_mouse: int32 [12, 1536, 1643], P('dp', 'seq'), may hold values from 0 to 5
Outputs:
- trunk_out: float32 [12, 1536, 1536], P('dp', 'seq')
- loss: float32 [], replicated
- grad_trunk_in: float32 [12, 1536, 1536], P('dp', 'seq')
- grad_norm1_gain: float32 [1536], P(('dp', 'seq'))
- grad_norm1_bias: float32 [1536], P(('dp', 'seq'))
- grad_w_query: float32 [1536, 512], P(('dp', 'seq'), 'mp')
- grad_w_key: float32 [1536, 512], P(('dp', 'seq'), 'mp')
- grad_w_value: float32 [1536, 1536], P(('dp', 'seq'), 'mp')
- grad_w_rel: float32 [192, 512], P(('dp', 'seq'), 'mp')
- grad_content_bias: float32 [8, 64], P('mp', ('dp', 'seq'))
- grad_pos_bias: float32 [8, 64], P('mp', ('dp', 'seq'))
- grad_w_out: float32 [1536, 1536], P('mp', ('dp', 'seq'))
- grad_b_out: float32 [1536], P(('dp', 'seq'))
- grad_norm2_gain: float32 [1536], P(('dp', 'seq'))
- grad_norm2_bias: float32 [1536], P(('dp', 'seq'))
- grad_w_in: float32 [1536, 3072], P(('dp', 'seq'), 'mp')
- grad_b_in: float32 [3072], P('mp')
- grad_w_hid: float32 [3072, 1536], P('mp', ('dp', 'seq'))
- grad_b_hid: float32 [1536], P(('dp', 'seq'))
- grad_head_human: float32 [1536, 5313], P('mp')
- grad_bias_human: float32 [5313], replicated
- grad_head_mouse: float32 [1536, 1643], P('mp')
- grad_bias_mouse: float32 [1643], replicated
Inputs may be any that keep to these rules, and one draw needn't show every extreme that they name: `species`: 0 selects the human head, 1 the mouse head. `targets_human`: only the central 896 bins of a window are scored. `targets_mouse`: only the central 896 bins of a window are scored.
All inputs are finite; a program needn't handle non-finite values.
Results may differ from a plain program's by a relative error of at most 0.012.
The roundings to bfloat16 on the way count: a program that leaves them out, or rounds other values in their place, can miss the bound.
Values may be sent and summed in bfloat16 or wider, within the bound.
No kernel may reach another device: no remote copies, remote signals or barrier semaphores. Data moves between devices by JAX's collectives and lax.ppermute only.
A program may use at most 448 MiB of HBM per device.

v0:
```python
import math

import jax
import jax.numpy as jnp
from jax import lax
from jax.sharding import PartitionSpec as P

KD = 64
VD = 192
FEAT = 192
BINS = 1536
CROP = 896


norm_eps = 1e-05
log_eps = 1e-07
exact_mode = lax.Precision.HIGHEST


def rel_basis():
    per_class = FEAT // 6
    distance = jnp.arange(-(BINS - 1), BINS).astype(jnp.float32)
    magnitude = jnp.abs(distance)[:, None]
    half_life = (2.0 ** jnp.linspace(3.0, math.log2(BINS), per_class)).astype(jnp.float32)
    decays = jnp.exp(-math.log(2.0) / half_life[None, :] * magnitude)
    widths = (2.0 ** jnp.arange(1, per_class + 1)).astype(jnp.float32) - 1.0
    central = (widths[None, :] > magnitude).astype(jnp.float32)
    spread = BINS / (2.0 * per_class)
    centre = jnp.linspace(BINS / per_class, BINS, per_class).astype(jnp.float32)
    concentration = (centre / spread) ** 2
    rate_param = centre / spread**2
    peak_at = (concentration - 1.0) / rate_param
    log_ratio = (concentration - 1.0) * (
        jnp.log(jnp.maximum(magnitude, 1e-20)) - jnp.log(peak_at)
    ) - rate_param * (magnitude - peak_at)
    density = jnp.exp(log_ratio)
    gammas = density / jnp.max(density, axis=0, keepdims=True)
    symmetric = jnp.concatenate([decays, central, gammas], axis=1)
    return jnp.concatenate([symmetric, jnp.sign(distance)[:, None] * symmetric], axis=1)


def rel_shift(logits, key_count):
    query_count = logits.shape[-2]
    span_width = logits.shape[-1]
    leading = logits.shape[:-2]
    padded = jnp.pad(logits, [(0, 0)] * len(leading) + [(0, 0), (0, 1)])
    flattened = padded.reshape(leading + (query_count * (span_width + 1),))
    flattened = flattened[..., query_count - 1 : query_count - 1 + query_count * span_width]
    return flattened.reshape(leading + (query_count, span_width))[..., :key_count]


def norm_forward(values, norm_gain, norm_bias):
    centred = values - jnp.mean(values, axis=-1, keepdims=True)
    inverse = lax.rsqrt(jnp.mean(centred * centred, axis=-1, keepdims=True) + norm_eps)
    scaled = centred * inverse
    return (scaled * norm_gain + norm_bias, scaled, inverse)


def norm_backward(grad_output, scaled, inverse, norm_gain):
    grad_scaled = grad_output * norm_gain
    mean_grad = jnp.mean(grad_scaled, axis=-1, keepdims=True)
    mean_proj = jnp.mean(grad_scaled * scaled, axis=-1, keepdims=True)
    grad_input = inverse * (grad_scaled - mean_grad - scaled * mean_proj)
    return (grad_input, jnp.sum(grad_output * scaled, axis=0), jnp.sum(grad_output, axis=0))


def soft_plus(logits):
    return jnp.maximum(logits, 0.0) + jnp.log1p(jnp.exp(-jnp.abs(logits)))


def head_loss(logits, counts, row_weight):
    predicted = soft_plus(logits)
    shifted = predicted + log_eps
    loss_rows = jnp.sum(predicted - counts * jnp.log(shifted), axis=-1)
    sigma_val = 1.0 / (1.0 + jnp.exp(-logits))
    grad_logits = row_weight[:, None] * (sigma_val - counts * sigma_val / shifted)
    return (jnp.sum(row_weight * loss_rows), grad_logits)


def contract(left_arr, right_arr, left_dim, right_dim):
    return lax.dot_general(
        left_arr,
        right_arr,
        (((left_dim,), (right_dim,)), ((), ())),
        preferred_element_type=jnp.float32,
    )


def on_device(
    trunk_in,
    norm1_gain,
    norm1_bias,
    w_query,
    w_key,
    w_value,
    w_rel,
    content_bias,
    pos_bias,
    w_out,
    b_out,
    norm2_gain,
    norm2_bias,
    w_in,
    b_in,
    w_hid,
    b_hid,
    head_human,
    bias_human,
    head_mouse,
    bias_mouse,
    species,
    targets_human,
    targets_mouse,
):
    windows_here, bins_here, model_width = trunk_in.shape
    row_count = windows_here * bins_here
    heads_here = content_bias.shape[0]
    seq_index = lax.axis_index("seq")
    model_index = lax.axis_index("mp")
    query_start = seq_index * bins_here
    key_scale = KD ** (-0.5)
    loss_scale = 1.0 / math.sqrt(windows_here * lax.axis_size("dp") * CROP)
    crop_start = (BINS - CROP) // 2
    feature_share = head_human.shape[0]
    track_human = head_human.shape[1]
    track_mouse = head_mouse.shape[1]
    trunk = trunk_in.astype(jnp.float32).reshape(row_count, model_width)
    normed1, scaled1, inverse1 = norm_forward(trunk, norm1_gain, norm1_bias)
    normed1_low = normed1.astype(jnp.bfloat16)
    query_raw = jnp.dot(normed1_low, w_query, preferred_element_type=jnp.float32)
    key_local = (
        jnp.dot(normed1_low, w_key, preferred_element_type=jnp.float32)
        .astype(jnp.bfloat16)
        .reshape(windows_here, bins_here, heads_here, KD)
    )
    value_local = (
        jnp.dot(normed1_low, w_value, preferred_element_type=jnp.float32)
        .astype(jnp.bfloat16)
        .reshape(windows_here, bins_here, heads_here, VD)
    )
    query_scaled = query_raw.reshape(windows_here, bins_here, heads_here, KD) * key_scale
    query_content = (query_scaled + content_bias).astype(jnp.bfloat16)
    query_pos = (query_scaled + pos_bias).astype(jnp.bfloat16)
    basis = rel_basis()
    span_rows = bins_here + BINS - 1
    row_first = BINS - bins_here - query_start
    basis_piece = lax.dynamic_slice_in_dim(basis, row_first, span_rows, 0)
    relative = (
        jnp.dot(basis_piece, w_rel.astype(jnp.float32), precision=exact_mode)
        .astype(jnp.bfloat16)
        .reshape(span_rows, heads_here, KD)
    )
    keys_all, values_all = (
        lax.all_gather(key_local, "seq", axis=1, tiled=True),
        lax.all_gather(value_local, "seq", axis=1, tiled=True),
    )
    content = jnp.einsum(
        "wqhd,wkhd->whqk", query_content, keys_all, preferred_element_type=jnp.float32
    )
    position = jnp.einsum("wqhd,rhd->whqr", query_pos, relative, preferred_element_type=jnp.float32)
    scores = content + rel_shift(position, BINS)
    exps = jnp.exp(scores - jnp.max(scores, axis=-1, keepdims=True))
    probs = exps / jnp.sum(exps, axis=-1, keepdims=True)
    probs_low = probs.astype(jnp.bfloat16)
    attended = jnp.einsum(
        "whqk,wkhd->wqhd", probs_low, values_all, preferred_element_type=jnp.float32
    )
    attended_low = attended.reshape(row_count, heads_here * VD).astype(jnp.bfloat16)
    attn_term = jnp.dot(attended_low, w_out, preferred_element_type=jnp.float32)
    mid = trunk + lax.psum(attn_term, "mp") + b_out
    normed2, scaled2, inverse2 = norm_forward(mid, norm2_gain, norm2_bias)
    normed2_low = normed2.astype(jnp.bfloat16)
    preact = jnp.dot(normed2_low, w_in, preferred_element_type=jnp.float32) + b_in
    active = jnp.maximum(preact, 0.0).astype(jnp.bfloat16)
    mlp_out = lax.psum(jnp.dot(active, w_hid, preferred_element_type=jnp.float32), "mp") + b_hid
    trunk_out = mid + mlp_out
    trunk_low = trunk_out.astype(jnp.bfloat16)
    bin_place = query_start + jnp.arange(bins_here)
    in_crop = ((bin_place >= crop_start) & (bin_place < crop_start + CROP)).astype(jnp.float32)
    row_weight = in_crop * loss_scale
    has_crop = (query_start + bins_here > crop_start) & (query_start < crop_start + CROP)
    trunk_windows = trunk_low.reshape(windows_here, bins_here, model_width)
    slice_windows = lax.dynamic_slice_in_dim(
        trunk_windows, model_index * feature_share, feature_share, 2
    )
    full_human, full_mouse = (
        lax.all_gather(head_human, "mp", axis=0, tiled=True),
        lax.all_gather(head_mouse, "mp", axis=0, tiled=True),
    )
    totals = (
        jnp.zeros((), jnp.float32),
        jnp.zeros((feature_share, track_human), jnp.float32),
        jnp.zeros((feature_share, track_mouse), jnp.float32),
        jnp.zeros((track_human,), jnp.float32),
        jnp.zeros((track_mouse,), jnp.float32),
    )
    grad_pieces = []
    for window in range(windows_here):
        rows_low = trunk_windows[window]
        rows_slice = slice_windows[window]
        counts_h = targets_human[window].astype(jnp.float32)
        counts_m = targets_mouse[window].astype(jnp.float32)

        def human_case(carry):
            logit_h = jnp.dot(rows_low, full_human, preferred_element_type=jnp.float32) + bias_human
            loss_h, grad_h = head_loss(logit_h, counts_h, row_weight)
            grad_h_low = grad_h.astype(jnp.bfloat16)
            updated = (
                carry[0] + loss_h,
                carry[1] + contract(rows_slice, grad_h_low, 0, 0),
                carry[2],
                carry[3] + jnp.sum(grad_h, axis=0),
                carry[4],
            )
            return (updated, contract(grad_h_low, full_human, 1, 1))

        def mouse_case(carry):
            logit_m = jnp.dot(rows_low, full_mouse, preferred_element_type=jnp.float32) + bias_mouse
            loss_m, grad_m = head_loss(logit_m, counts_m, row_weight)
            grad_m_low = grad_m.astype(jnp.bfloat16)
            updated = (
                carry[0] + loss_m,
                carry[1],
                carry[2] + contract(rows_slice, grad_m_low, 0, 0),
                carry[3],
                carry[4] + jnp.sum(grad_m, axis=0),
            )
            return (updated, contract(grad_m_low, full_mouse, 1, 1))

        def skip_case(carry):
            return (carry, jnp.zeros((bins_here, model_width), jnp.float32))

        selector = jnp.where(has_crop, species[window], 2)
        totals, grad_rows = lax.switch(selector, [human_case, mouse_case, skip_case], totals)
        grad_pieces.append(grad_rows)
    loss_local, dhead_human, dhead_mouse, dbias_human, dbias_mouse = totals
    grad_trunk = jnp.concatenate(grad_pieces, axis=0)
    db_hid = jnp.sum(grad_trunk, axis=0)
    grad_out_low = grad_trunk.astype(jnp.bfloat16)
    dw_hid = contract(active, grad_out_low, 0, 0)
    grad_preact = jnp.where(preact > 0.0, contract(grad_out_low, w_hid, 1, 1), 0.0)
    db_in = jnp.sum(grad_preact, axis=0)
    grad_pre_low = grad_preact.astype(jnp.bfloat16)
    dw_in = contract(normed2_low, grad_pre_low, 0, 0)
    normed2_term = contract(grad_pre_low, w_in, 1, 1)
    grad_normed2 = lax.psum(normed2_term.astype(jnp.bfloat16), "mp").astype(jnp.float32)
    grad_mid_norm, dgain2, dbias2 = norm_backward(grad_normed2, scaled2, inverse2, norm2_gain)
    grad_mid = grad_trunk + grad_mid_norm
    db_out = jnp.sum(grad_mid, axis=0)
    grad_mid_low = grad_mid.astype(jnp.bfloat16)
    dw_out = contract(attended_low, grad_mid_low, 0, 0)
    grad_att_low = (
        contract(grad_mid_low, w_out, 1, 1)
        .astype(jnp.bfloat16)
        .reshape(windows_here, bins_here, heads_here, VD)
    )
    grad_probs = jnp.einsum(
        "wqhd,wkhd->whqk", grad_att_low, values_all, preferred_element_type=jnp.float32
    )
    delta_sum = jnp.sum(grad_probs * probs, axis=-1, keepdims=True)
    grad_scores = (probs * (grad_probs - delta_sum)).astype(jnp.bfloat16)
    grad_qc = jnp.einsum(
        "whqk,wkhd->wqhd", grad_scores, keys_all, preferred_element_type=jnp.float32
    )
    key_terms = jnp.einsum(
        "whqk,wqhd->wkhd", grad_scores, query_content, preferred_element_type=jnp.float32
    )
    value_terms = jnp.einsum(
        "whqk,wqhd->wkhd", probs_low, grad_att_low, preferred_element_type=jnp.float32
    )
    unused_out, unshift = jax.vjp(lambda shifted_in: rel_shift(shifted_in, BINS), position)
    grad_pos = unshift(grad_scores.astype(jnp.float32))[0].astype(jnp.bfloat16)
    grad_qp = jnp.einsum("whqr,rhd->wqhd", grad_pos, relative, preferred_element_type=jnp.float32)
    grad_relative = jnp.einsum(
        "whqr,wqhd->rhd", grad_pos, query_pos, preferred_element_type=jnp.float32
    ).reshape(span_rows, heads_here * KD)
    dw_rel = lax.dot_general(
        basis_piece,
        grad_relative,
        (((0,), (0,)), ((), ())),
        precision=exact_mode,
        preferred_element_type=jnp.float32,
    )
    dcontent = jnp.sum(grad_qc, axis=(0, 1))
    dposition = jnp.sum(grad_qp, axis=(0, 1))
    grad_query = (
        ((grad_qc + grad_qp) * key_scale).reshape(row_count, heads_here * KD).astype(jnp.bfloat16)
    )
    key_grad, value_grad = (
        lax.psum_scatter(key_terms, "seq", scatter_dimension=1, tiled=True),
        lax.psum_scatter(value_terms, "seq", scatter_dimension=1, tiled=True),
    )
    key_grad_low = key_grad.reshape(row_count, heads_here * KD).astype(jnp.bfloat16)
    value_grad_low = value_grad.reshape(row_count, heads_here * VD).astype(jnp.bfloat16)
    dw_query = contract(normed1_low, grad_query, 0, 0)
    dw_key = contract(normed1_low, key_grad_low, 0, 0)
    dw_value = contract(normed1_low, value_grad_low, 0, 0)
    normed1_term = (
        contract(grad_query, w_query, 1, 1)
        + contract(key_grad_low, w_key, 1, 1)
        + contract(value_grad_low, w_value, 1, 1)
    )
    grad_normed1 = lax.psum(normed1_term.astype(jnp.bfloat16), "mp").astype(jnp.float32)
    grad_in_norm, dgain1, dbias1 = norm_backward(grad_normed1, scaled1, inverse1, norm1_gain)
    grad_input = grad_mid + grad_in_norm
    summed = (
        lax.psum_scatter(dgain1, ("dp", "seq"), scatter_dimension=0, tiled=True),
        lax.psum_scatter(dbias1, ("dp", "seq"), scatter_dimension=0, tiled=True),
        lax.psum_scatter(dw_query, ("dp", "seq"), scatter_dimension=0, tiled=True),
        lax.psum_scatter(dw_key, ("dp", "seq"), scatter_dimension=0, tiled=True),
        lax.psum_scatter(dw_value, ("dp", "seq"), scatter_dimension=0, tiled=True),
        lax.psum_scatter(dw_rel, ("dp", "seq"), scatter_dimension=0, tiled=True),
        lax.psum_scatter(dcontent, ("dp", "seq"), scatter_dimension=1, tiled=True),
        lax.psum_scatter(dposition, ("dp", "seq"), scatter_dimension=1, tiled=True),
        lax.psum_scatter(dw_out, ("dp", "seq"), scatter_dimension=1, tiled=True),
        lax.psum_scatter(db_out, ("dp", "seq"), scatter_dimension=0, tiled=True),
        lax.psum_scatter(dgain2, ("dp", "seq"), scatter_dimension=0, tiled=True),
        lax.psum_scatter(dbias2, ("dp", "seq"), scatter_dimension=0, tiled=True),
        lax.psum_scatter(dw_in, ("dp", "seq"), scatter_dimension=0, tiled=True),
        lax.psum_scatter(dw_hid, ("dp", "seq"), scatter_dimension=1, tiled=True),
        lax.psum_scatter(db_hid, ("dp", "seq"), scatter_dimension=0, tiled=True),
    )
    gain_one, offset_one, gain_two, offset_two = (summed[0], summed[1], summed[10], summed[11])
    head_totals = (
        lax.psum(dhead_human.astype(jnp.bfloat16), ("dp", "seq")).astype(jnp.float32),
        lax.psum(dhead_mouse.astype(jnp.bfloat16), ("dp", "seq")).astype(jnp.float32),
        lax.psum(dbias_human.astype(jnp.bfloat16), ("dp", "seq")).astype(jnp.float32),
        lax.psum(dbias_mouse.astype(jnp.bfloat16), ("dp", "seq")).astype(jnp.float32),
        lax.psum(db_in.astype(jnp.bfloat16), ("dp", "seq")).astype(jnp.float32),
        lax.psum(loss_local.astype(jnp.bfloat16), ("dp", "seq")).astype(jnp.float32),
    )
    return (
        trunk_out.reshape(windows_here, bins_here, model_width),
        head_totals[5],
        grad_input.reshape(windows_here, bins_here, model_width),
        gain_one,
        offset_one,
        summed[2],
        summed[3],
        summed[4],
        summed[5],
        summed[6],
        summed[7],
        summed[8],
        summed[9],
        gain_two,
        offset_two,
        summed[12],
        head_totals[4],
        summed[13],
        summed[14],
        head_totals[0],
        head_totals[2],
        head_totals[1],
        head_totals[3],
    )


def solution(mesh):
    in_specs = (
        P("dp", "seq", None),
        P(),
        P(),
        P(None, "mp"),
        P(None, "mp"),
        P(None, "mp"),
        P(None, "mp"),
        P("mp", None),
        P("mp", None),
        P("mp", None),
        P(),
        P(),
        P(),
        P(None, "mp"),
        P("mp"),
        P("mp", None),
        P(),
        P("mp", None),
        P(),
        P("mp", None),
        P(),
        P("dp"),
        P("dp", "seq", None),
        P("dp", "seq", None),
    )
    out_specs = (
        P("dp", "seq", None),
        P(),
        P("dp", "seq", None),
        P(("dp", "seq")),
        P(("dp", "seq")),
        P(("dp", "seq"), "mp"),
        P(("dp", "seq"), "mp"),
        P(("dp", "seq"), "mp"),
        P(("dp", "seq"), "mp"),
        P("mp", ("dp", "seq")),
        P("mp", ("dp", "seq")),
        P("mp", ("dp", "seq")),
        P(("dp", "seq")),
        P(("dp", "seq")),
        P(("dp", "seq")),
        P(("dp", "seq"), "mp"),
        P("mp"),
        P("mp", ("dp", "seq")),
        P(("dp", "seq")),
        P("mp", None),
        P(),
        P("mp", None),
        P(),
    )
    return jax.shard_map(
        on_device, mesh=mesh, in_specs=in_specs, out_specs=out_specs, check_vma=False
    )
```

profile of v0, /device:TPU:0, one launch (start us, length us, event | category | flops | bytes accessed | tf_op | source)
XLA Modules:
  0.0 2512.7 jit_solution(11781694178047609312)
XLA Ops:
  65.5 36.2 %copy.141 = f32[3,4,384,1919]{3,2,1,0:T(8,128)} copy(f32[3,4,384,1919]{2,3,0,1:T(8,128)} %convolution_bitcast_fusion.2) | data formatting | bytes 70742016
  101.8 25.9 %pad.17.clone = f32[3,4,384,1920]{3,2,1,0:T(8,128)} pad(f32[3,4,384,1919]{3,2,1,0:T(8,128)} %copy.141, f32[]{:T(128)} %constant.87.clone.1), padding=0_0x0_0x0_0x0_1 | pad | bytes 70760448 | tf_op jit(solution)/shard_map/jit(_pad)/pad | solution.py:46
  127.7 42.7 %reshape.393 = f32[3,4,737280]{2,1,0:T(4,128)} reshape(f32[3,4,384,1920]{3,2,1,0:T(8,128)} %pad.17.clone) | data formatting | bytes 70778880 | tf_op jit(solution)/shard_map/reshape | solution.py:47
  170.4 24.4 slice.73
  194.8 71.1 %reshape.394 = f32[3,4,384,1919]{3,2,1,0:T(8,128)} reshape(f32[3,4,736896]{2,1,0:T(4,128)} %slice.73) | data formatting | bytes 70742016 | tf_op jit(solution)/shard_map/reshape | solution.py:49
  266.0 24.5 fusion.154
  290.4 14.9 convert_bitcast_fusion
  322.2 172.9 %all-reduce.22.cloned.1.call-done = f32[1152,1536]{1,0:T(8,128)} async-done(((f32[1152,1536]{1,0:T(8,128)}), f32[1152,1536]{1,0:T(8,128)}) %all-reduce.22.cloned.1.call-update) | async-done | bytes 7077904 | tf_op jit(solution)/shard_map/psum | solution.py:170
  542.0 150.7 %all-reduce.24.cloned.1.call-done = f32[1152,1536]{1,0:T(8,128)} async-done(((f32[1152,1536]{1,0:T(8,128)}), f32[1152,1536]{1,0:T(8,128)}) %all-reduce.24.cloned.1.call-update) | async-done | bytes 7077904 | tf_op jit(solution)/shard_map/psum | solution.py:175
  706.0 55.9 %all-gather.11.cloned.1.call-done = bf16[1536,1643]{1,0:T(8,128)(2,1)} async-done(((bf16[768,1643]{1,0:T(8,128)(2,1)}), bf16[1536,1643]{1,0:T(8,128)(2,1)}) %all-gather.11.cloned.1.call-update) | async-done | bytes 5047312 | tf_op jit(solution)/shard_map/all_gather | solution.py:188
  761.8 197.9 %all-gather.9.cloned.1.call-done = bf16[1536,5313]{1,0:T(8,128)(2,1)} async-done(((bf16[768,5313]{1,0:T(8,128)(2,1)}), bf16[1536,5313]{1,0:T(8,128)(2,1)}) %all-gather.9.cloned.1.call-update) | async-done | bytes 16321552 | tf_op jit(solution)/shard_map/all_gather | solution.py:187
  959.8 40.4 %conditional.3 = (f32[]{:T(128)}, f32[768,5313]{0,1:T(8,128)}, f32[768,1643]{1,0:T(8,128)}, f32[5313]{0:T(1024)}, f32[1643]{0:T(1024)S(1)}, /*index=5*/f32[384,1536]{1,0:T(8,128)}) conditional(s32[]{:T(128)} %clamp.11, (bf16[384,1536]{1,0:T(8,128)(2,1)}, bf16[1536,5313]{1,0:T(8,128)(2,1)}, f32[5313]{0:T(1024)S(1)}, ...), branch_computations={%region_9.13_spmd, %region_13.17_spmd, %region_17.18_spmd} | conditional | flops 15707435008 | bytes 97278752 | solution.py:234
  1004.1 42.3 %conditional.4 = (f32[]{:T(128)}, f32[768,5313]{0,1:T(8,128)}, f32[768,1643]{1,0:T(8,128)}, f32[5313]{0:T(1024)}, f32[1643]{0:T(1024)S(1)}, /*index=5*/f32[384,1536]{1,0:T(8,128)}) conditional(s32[]{:T(128)} %clamp.10, (bf16[384,1536]{1,0:T(8,128)(2,1)}, bf16[1536,5313]{1,0:T(8,128)(2,1)}, f32[5313]{0:T(1024)}, ...), branch_computations={%region_18.22_spmd, %region_22.26_spmd, %region_26.27_spmd} | conditional | flops 15711520768 | bytes 106250864 | solution.py:234
  1050.5 63.8 %conditional.5 = (f32[]{:T(128)}, f32[768,5313]{0,1:T(8,128)}, f32[768,1643]{1,0:T(8,128)}, f32[5313]{0:T(1024)}, f32[1643]{0:T(1024)S(1)}, /*index=5*/f32[384,1536]{1,0:T(8,128)}) conditional(s32[]{:T(128)} %clamp.9, (bf16[384,1536]{1,0:T(8,128)(2,1)}, bf16[1536,5313]{1,0:T(8,128)(2,1)}, f32[5313]{0:T(1024)}, ...), branch_computations={%region_27.31_spmd, %region_31.35_spmd, %region_35.36_spmd} | conditional | flops 15711520768 | bytes 106250864 | solution.py:234
  1050.9 24.7 fusion.136
  1138.9 121.7 %all-reduce.26.cloned.1.call-done = bf16[1152,1536]{1,0:T(8,128)(2,1)} async-done(((bf16[1152,1536]{1,0:T(8,128)(2,1)}), bf16[1152,1536]{1,0:T(8,128)(2,1)}) %all-reduce.26.cloned.1.call-update) | async-done | bytes 3538960 | tf_op jit(solution)/shard_map/psum | solution.py:246
  1292.4 24.6 multiply_reduce_fusion.6
  1317.0 23.6 multiply_convert_fusion
  1350.6 18.0 fusion.88
  1396.9 53.0 %reshape.398 = bf16[3,4,736896]{2,1,0:T(4,128)(2,1)} reshape(bf16[3,4,384,1919]{3,2,1,0:T(8,128)(2,1)} %pad.18) | data formatting | bytes 35371008 | tf_op jit(solution)/shard_map/transpose(jvp())/reshape | solution.py:49
  1449.9 15.0 pad.19
  1464.9 27.9 %reshape.399 = bf16[3,4,384,1920]{3,2,1,0:T(8,128)(2,1)} reshape(bf16[3,4,737280]{2,1,0:T(4,128)(2,1)} %pad.19) | data formatting | bytes 35389440 | tf_op jit(solution)/shard_map/transpose(jvp())/reshape | solution.py:47
  1523.7 152.6 %reduce-scatter.15.cloned.1.call-done = f32[3,384,4,192]{1,3,2,0:T(8,128)} async-done(((f32[3,1536,4,192]{1,3,2,0:T(8,128)}), f32[3,384,4,192]{1,3,2,0:T(8,128)}) %reduce-scatter.15.cloned.1.call-update) | async-done | bytes 3538960 | tf_op jit(solution)/shard_map/reduce_scatter | solution.py:291
  1768.4 39.2 %fusion = f32[16,256]{1,0:T(8,128)S(1)} fusion(f32[192,256]{1,0:T(8,128)S(1)} %fusion.162), kind=kCustom, calls=%all-reduce-scatter | all-reduce-scatter fusion | flops 65537 | bytes 213504
  1819.6 60.4 %all-reduce.14 = (bf16[]{:T(256)}, bf16[1536]{0:T(1024)(128)(2,1)S(1)}, bf16[5313]{0:T(1024)(128)(2,1)S(1)}, bf16[1643]{0:T(1024)(128)(2,1)S(1)}) all-reduce(bf16[]{:T(256)S(6)} %convert_element_type.247, bf16[1536]{0:T(1024)(128)(2,1)S(1)} %copy-done.65, ...), channel_id=1, replica_groups=mesh['dp'=4,'seq'=4,'mp'=2] {'dp','seq'}, use_global_device_ids=true, to_apply=%region_36.37 | all-reduce | flops 8493 | bytes 33972 | tf_op jit(solution)/shard_map/psum | solution.py:330
  1905.0 82.7 %all-reduce.28.cloned.1.call-done = bf16[1152,1536]{1,0:T(8,128)(2,1)} async-done(((bf16[1152,1536]{1,0:T(8,128)(2,1)}), bf16[1152,1536]{1,0:T(8,128)(2,1)}) %all-reduce.28.cloned.1.call-update) | async-done | bytes 3538960 | tf_op jit(solution)/shard_map/psum | solution.py:303
  1993.4 62.0 %all-reduce.13 = (f32[1536]{0:T(1024)S(1)}, f32[1536]{0:T(1024)S(1)}, f32[4,64]{1,0:T(4,128)S(1)}, f32[4,64]{1,0:T(4,128)S(1)}, f32[1536]{0:T(1024)S(1)}, /*inde...) all-reduce(f32[1536]{0:T(1024)S(1)} %get-tuple-element.437, ...), channel_id=4, replica_groups=mesh['dp'=4,'seq'=4,'mp'=2] {'dp','seq'}, use_global_device_ids=true, to_apply=%region_47.48.clone | all-reduce | flops 9728 | bytes 77824
  2070.2 60.7 %reduce-scatter.23.cloned.1.call-done = f32[768,96]{0,1:T(8,128)} async-done(((f32[768,1536]{0,1:T(8,128)}), f32[768,96]{0,1:T(8,128)}) %reduce-scatter.23.cloned.1.call-update) | async-done | bytes 294928 | tf_op jit(solution)/shard_map/reduce_scatter | solution.py:315
  2130.9 115.0 %reduce-scatter.27.cloned.1.call-done = f32[1536,96]{0,1:T(8,128)} async-done(((f32[1536,1536]{0,1:T(8,128)}), f32[1536,96]{0,1:T(8,128)}) %reduce-scatter.27.cloned.1.call-update) | async-done | bytes 589840 | tf_op jit(solution)/shard_map/reduce_scatter | solution.py:320
  2245.9 116.2 %reduce-scatter.25.cloned.1.call-done = f32[96,1536]{1,0:T(8,128)} async-done(((f32[1536,1536]{1,0:T(8,128)}), f32[96,1536]{1,0:T(8,128)}) %reduce-scatter.25.cloned.1.call-update) | async-done | bytes 589840 | tf_op jit(solution)/shard_map/reduce_scatter | solution.py:319
  2362.1 63.4 %reduce-scatter.19.cloned.1.call-done = f32[96,256]{1,0:T(8,128)} async-done(((f32[1536,256]{1,0:T(8,128)}), f32[96,256]{1,0:T(8,128)}) %reduce-scatter.19.cloned.1.call-update) | async-done | bytes 98320 | tf_op jit(solution)/shard_map/reduce_scatter | solution.py:310
  2425.5 79.3 %reduce-scatter.21.cloned.1.call-done = f32[96,768]{1,0:T(8,128)} async-done(((f32[1536,768]{1,0:T(8,128)}), f32[96,768]{1,0:T(8,128)}) %reduce-scatter.21.cloned.1.call-update) | async-done | bytes 294928 | tf_op jit(solution)/shard_map/reduce_scatter | solution.py:311
  (325 shorter events, 503.1 us)
Async XLA Ops:
  7.2 308.5 %copy-start = (bf16[768,1536]{1,0:T(8,128)(2,1)S(1)}, bf16[768,1536]{1,0:T(8,128)(2,1)}, u32[]{:S(2)}) copy-start(bf16[768,1536]{1,0:T(8,128)(2,1)} %param.42) | copy-start | bytes 7077892
  7.2 258.7 %all-gather.7.cloned.1.call-start = ((), (), s32[]{:S(2)}) async-start(), calls=%async_computation.9 | async-start | bytes 2949120 | tf_op jit(solution)/shard_map/all_gather | solution.py:154
  22.8 267.7 %all-gather.5.cloned.1.call-start = ((), (), s32[]{:S(2)}) async-start(), calls=%async_computation.8 | async-start | bytes 8847360 | tf_op jit(solution)/shard_map/all_gather | solution.py:155
  40.9 454.2 %all-reduce.22.cloned.1.call-start = ((), (), s32[]{:S(2)}) async-start(), calls=%async_computation.10 | async-start | bytes 14155776 | tf_op jit(solution)/shard_map/psum | solution.py:170
  50.8 215.2 %copy-start.15 = (f32[3,384,4,64]{1,3,2,0:T(8,128)}, f32[3,384,4,64]{1,3,2,0:T(8,128)S(1)}, u32[]{:S(2)}) copy-start(f32[3,384,4,64]{1,3,2,0:T(8,128)S(1)} %get-tuple-element.508) | copy-start | bytes 3538948
  322.1 173.0 %copy-start.61 = (f32[1536]{0:T(1024)S(1)}, f32[1536]{0:T(1024)}, u32[]{:S(2)}) copy-start(f32[1536]{0:T(1024)} %param.43) | copy-start | bytes 18436
  322.1 370.6 %all-reduce.24.cloned.1.call-start = ((), (), s32[]{:S(2)}) async-start(), calls=%async_computation.11 | async-start | bytes 14155776 | tf_op jit(solution)/shard_map/psum | solution.py:175
  522.4 239.4 %all-gather.11.cloned.1.call-start = ((), (), s32[]{:S(2)}) async-start(), calls=%async_computation.13 | async-start | bytes 7667712 | tf_op jit(solution)/shard_map/all_gather | solution.py:188
  526.9 432.9 %all-gather.9.cloned.1.call-start = ((), (), s32[]{:S(2)}) async-start(), calls=%async_computation.12 | async-start | bytes 24772608 | tf_op jit(solution)/shard_map/all_gather | solution.py:187
  538.8 153.9 %copy-start.62 = (f32[1536]{0:T(1024)S(1)}, f32[1536]{0:T(1024)}, u32[]{:S(2)}) copy-start(f32[1536]{0:T(1024)} %param.49) | copy-start | bytes 18436
  538.8 721.8 %all-reduce.26.cloned.1.call-start = ((), (), s32[]{:S(2)}) async-start(), calls=%async_computation.14 | async-start | bytes 7077888 | tf_op jit(solution)/shard_map/psum | solution.py:246
  702.9 256.8 %copy-start.70 = (f32[5313]{0:T(1024)S(1)}, f32[5313]{0:T(1024)}, u32[]{:S(2)}) copy-start(f32[5313]{0:T(1024)} %param.51) | copy-start | bytes 63760
  1131.7 128.9 %copy-start.37 = (f32[1152]{0:T(1024)S(1)}, f32[1152]{0:T(1024)}, u32[]{:S(2)}) copy-start(f32[1152]{0:T(1024)} %copy-done.36) | copy-start | bytes 13828
  1131.7 128.9 %copy-start.46 = (f32[1152]{0:T(1024)S(1)}, f32[1152]{0:T(1024)}, u32[]{:S(2)}) copy-start(f32[1152]{0:T(1024)} %copy-done.45) | copy-start | bytes 13828
  1131.7 128.9 %copy-start.51 = (f32[1536]{0:T(1024)S(1)}, f32[1536]{0:T(1024)}, u32[]{:S(2)}) copy-start(f32[1536]{0:T(1024)} %param.44) | copy-start | bytes 18436
  1138.9 382.8 %reduce-scatter.13.cloned.1.call-start = ((), (), s32[]{:S(2)}) async-start(), calls=%async_computation.15 | async-start | bytes 5898240 | tf_op jit(solution)/shard_map/reduce_scatter | solution.py:290
  1350.5 325.7 %reduce-scatter.15.cloned.1.call-start = ((), (), s32[]{:S(2)}) async-start(), calls=%async_computation.16 | async-start | bytes 17694720 | tf_op jit(solution)/shard_map/reduce_scatter | solution.py:291
  1368.6 522.4 %all-reduce.30.cloned.1.call-start = ((), (), s32[]{:S(2)}) async-start(), calls=%async_computation.24 | async-start | bytes 21405696 | tf_op jit(solution)/shard_map/psum | solution.py:325
  1382.5 605.2 %all-reduce.28.cloned.1.call-start = ((), (), s32[]{:S(2)}) async-start(), calls=%async_computation.17 | async-start | bytes 7077888 | tf_op jit(solution)/shard_map/psum | solution.py:303
  1702.2 368.0 %reduce-scatter.17.cloned.1.call-start = ((), (), s32[]{:S(2)}) async-start(), calls=%async_computation.18 | async-start | bytes 1671168 | tf_op jit(solution)/shard_map/reduce_scatter | solution.py:309
  1706.7 424.2 %reduce-scatter.23.cloned.1.call-start = ((), (), s32[]{:S(2)}) async-start(), calls=%async_computation.21 | async-start | bytes 5013504 | tf_op jit(solution)/shard_map/reduce_scatter | solution.py:315
  1715.9 530.0 %reduce-scatter.27.cloned.1.call-start = ((), (), s32[]{:S(2)}) async-start(), calls=%async_computation.23 | async-start | bytes 10027008 | tf_op jit(solution)/shard_map/reduce_scatter | solution.py:320
  1729.3 632.8 %reduce-scatter.25.cloned.1.call-start = ((), (), s32[]{:S(2)}) async-start(), calls=%async_computation.22 | async-start | bytes 10027008 | tf_op jit(solution)/shard_map/reduce_scatter | solution.py:319
  1742.5 683.0 %reduce-scatter.19.cloned.1.call-start = ((), (), s32[]{:S(2)}) async-start(), calls=%async_computation.19 | async-start | bytes 1671168 | tf_op jit(solution)/shard_map/reduce_scatter | solution.py:310
  1747.1 757.8 %reduce-scatter.21.cloned.1.call-start = ((), (), s32[]{:S(2)}) async-start(), calls=%async_computation.20 | async-start | bytes 5013504 | tf_op jit(solution)/shard_map/reduce_scatter | solution.py:311
  1807.6 74.9 %collective-permute-start = (f32[16,256]{1,0:T(8,128)S(1)}, f32[16,256]{1,0:T(8,128)S(1)}, u32[]{:S(2)}, u32[]{:S(2)}) collective-permute-start(f32[16,256]{1,0:T(8,128)S(1)} %fusion), channel_id=1, source_target_pairs={{0,2},{2,4},{4,6},{6,8},{8,10},{10,12},{12,14},{14,16},{16,18},{18... | collective-permute-start | bytes 49160
  1810.4 72.1 %collective-permute-start.1 = (f32[16,256]{1,0:T(8,128)S(1)}, f32[16,256]{1,0:T(8,128)S(1)}, u32[]{:S(2)}, u32[]{:S(2)}) collective-permute-start(f32[16,256]{1,0:T(8,128)S(1)} %fusion), channel_id=1, source_target_pairs={{0,4},{2,6},{4,8},{6,10},{8,12},{10,14},{12,16},{14,18},{16,20},{1... | collective-permute-start | bytes 49160
  1811.7 70.9 %collective-permute-start.2 = (f32[16,256]{1,0:T(8,128)S(1)}, f32[16,256]{1,0:T(8,128)S(1)}, u32[]{:S(2)}, u32[]{:S(2)}) collective-permute-start(f32[16,256]{1,0:T(8,128)S(1)} %fusion), channel_id=1, source_target_pairs={{0,6},{2,8},{4,10},{6,12},{8,14},{10,16},{12,18},{14,20},{16,22},{... | collective-permute-start | bytes 49160
  1814.5 68.0 %collective-permute-start.3 = (f32[12,256]{1,0:T(8,128)S(1)}, f32[12,256]{1,0:T(8,128)S(1)}, u32[]{:S(2)}, u32[]{:S(2)}) collective-permute-start(f32[12,256]{1,0:T(8,128)S(1)} %slice.78), channel_id=1, source_target_pairs={{0,8},{2,10},{4,12},{6,14},{8,16},{10,18},{12,20},{14,22},{16,24},... | collective-permute-start | bytes 36872
  1905.0 88.3 %copy-start.55 = (f32[1536]{0:T(1024)S(1)}, f32[1536]{0:T(1024)}, u32[]{:S(2)}) copy-start(f32[1536]{0:T(1024)} %get-tuple-element.435) | copy-start | bytes 18436
  1905.0 88.3 %copy-start.56 = (f32[1536]{0:T(1024)S(1)}, f32[1536]{0:T(1024)}, u32[]{:S(2)}) copy-start(f32[1536]{0:T(1024)} %get-tuple-element.441) | copy-start | bytes 18436
  1905.0 88.3 %copy-start.57 = (f32[1536]{0:T(1024)S(1)}, f32[1536]{0:T(1024)}, u32[]{:S(2)}) copy-start(f32[1536]{0:T(1024)} %get-tuple-element.469) | copy-start | bytes 18436
  (65 other events, 1053.1 us)
Sparse Core Ops, SparseCore 0:
  22.9 52.9 all-gather.6
  78.1 126.9 all-gather.4
  322.2 172.7 all-reduce.21
  522.5 170.1 all-reduce.23
  694.7 67.0 all-gather.10
  763.8 195.8 all-gather.8
  1139.0 121.5 all-reduce.25
  1350.7 85.2 reduce-scatter.12
  1438.4 237.7 reduce-scatter.14
  1680.4 210.5 all-reduce.29
  1893.4 94.3 all-reduce.27
  1991.8 59.5 reduce-scatter.16
  2056.3 74.5 reduce-scatter.22
  2135.5 110.3 reduce-scatter.26
  2251.0 111.0 reduce-scatter.24
  2366.2 59.2 reduce-scatter.18
  2430.2 74.5 reduce-scatter.20
where the time goes:
time: 2510 us
  waiting for transfers between devices  1380 us (55%)
  local copies, waits for them, and re-layouts  434 us (17%)
  matrix products  352 us (14%)
  blocking collectives  162 us (6%)
  other arithmetic  124 us (5%)
  loops' own time  31.5 us (1%)
    all_gather x1, waiting for transfers between devices, on_device(): lax.all_gather(head_human, 'mp', axis=0, tiled=True)  198 us
    psum x1, waiting for transfers between devices, on_device(): mid = trunk + lax.psum(attn_term, 'mp') + b_out  173 us
    reduce_scatter x1, waiting for transfers between devices, on_device(): lax.psum_scatter(value_terms, 'seq', scatter_dimension=1, tiled=True)  153 us
    psum x1, waiting for transfers between devices, on_device(): lax.psum(jnp.dot(active, w_hid, preferred_element_type=jnp.float32), 'mp')  151 us
    dot_general x18, matrix products, contract(): lax.dot_general(left_arr, right_arr, (((left_dim,), (right_dim,)), ((), (...  134 us
    reshape x2, local copies, waits for them, and re-layouts, rel_shift(): flattened.reshape(leading + (query_count, span_width))[..., :key_count]  124 us
    psum x1, waiting for transfers between devices, on_device(): lax.psum(normed2_term.astype(jnp.bfloat16), 'mp').astype(jnp.float32)  122 us
    reduce_scatter x1, waiting for transfers between devices, on_device(): lax.psum_scatter(dw_in, ('dp', 'seq'), scatter_dimension=0, tiled=True)  116 us
  transfers between devices with their start and end apart: 21, of which 13 were waited for; matrix products, arithmetic and copies ran while one was open for 25% of the time, Pallas kernels for 0%

commit v1 on v0

v1 whole, which is shorter than its diff:
```python
import math

import jax
import jax.numpy as jnp
from jax import lax
from jax.experimental import pallas as pl
from jax.experimental.pallas import tpu as pltpu
from jax.sharding import PartitionSpec as P

KD = 64
VD = 192
FEAT = 192
BINS = 1536
CROP = 896


norm_eps = 1e-05
log_eps = 1e-07
exact_mode = lax.Precision.HIGHEST


def rel_basis():
    per_class = FEAT // 6
    distance = jnp.arange(-(BINS - 1), BINS).astype(jnp.float32)
    magnitude = jnp.abs(distance)[:, None]
    half_life = (2.0 ** jnp.linspace(3.0, math.log2(BINS), per_class)).astype(jnp.float32)
    decays = jnp.exp(-math.log(2.0) / half_life[None, :] * magnitude)
    widths = (2.0 ** jnp.arange(1, per_class + 1)).astype(jnp.float32) - 1.0
    central = (widths[None, :] > magnitude).astype(jnp.float32)
    spread = BINS / (2.0 * per_class)
    centre = jnp.linspace(BINS / per_class, BINS, per_class).astype(jnp.float32)
    concentration = (centre / spread) ** 2
    rate_param = centre / spread**2
    peak_at = (concentration - 1.0) / rate_param
    log_ratio = (concentration - 1.0) * (
        jnp.log(jnp.maximum(magnitude, 1e-20)) - jnp.log(peak_at)
    ) - rate_param * (magnitude - peak_at)
    density = jnp.exp(log_ratio)
    gammas = density / jnp.max(density, axis=0, keepdims=True)
    symmetric = jnp.concatenate([decays, central, gammas], axis=1)
    return jnp.concatenate([symmetric, jnp.sign(distance)[:, None] * symmetric], axis=1)


PACK = VD + 3 * KD
GRAD_PACK = VD + 2 * KD
TILE = 896
NN = (((1,), (0,)), ((), ()))
NT = (((1,), (1,)), ((), ()))
TN = (((0,), (0,)), ((), ()))


def mxu(left_arr, right_arr, dims, precision=None):
    return lax.dot_general(
        left_arr, right_arr, dims, precision=precision, preferred_element_type=jnp.float32
    )


def query_block(bins):
    for block in (384, 256, 128):
        if bins % block == 0:
            return block
    return bins


def attend_forward_kernel(block, bins, pack_ref, rel_ref, out_ref, probs_ref):
    step = pl.program_id(0)
    span = bins + block
    query = pack_ref[pl.ds(pl.multiple_of(step * block, block), block), VD + KD :]
    base = pl.multiple_of(bins - block - step * block, block)
    content = mxu(query[:, :KD], pack_ref[:, VD : VD + KD], NT)
    position = mxu(query[:, KD:], rel_ref[pl.ds(base, span), :], NT)
    position = pltpu.roll(position, span - (block - 1), 1, stride=1, stride_axis=0)
    scores = content + position[:, :bins]
    exps = jnp.exp(scores - jnp.max(scores, axis=1, keepdims=True))
    probs = (exps * (1.0 / jnp.sum(exps, axis=1, keepdims=True))).astype(jnp.bfloat16)
    probs_ref[...] = probs
    out_ref[0] = mxu(probs, pack_ref[:, :VD], NN).T.astype(jnp.bfloat16)


def attend_forward(pack, rel):
    bins = pack.shape[0]
    block = query_block(bins)
    steps = bins // block
    return pl.pallas_call(
        lambda *refs: attend_forward_kernel(block, bins, *refs),
        grid=(steps,),
        in_specs=[
            pl.BlockSpec((bins, PACK), lambda i: (0, 0)),
            pl.BlockSpec((2 * bins, KD), lambda i: (0, 0)),
        ],
        out_specs=[
            pl.BlockSpec((1, VD, block), lambda i: (i, 0, 0)),
            pl.BlockSpec((block, bins), lambda i: (i, 0)),
        ],
        out_shape=[
            jax.ShapeDtypeStruct((steps, VD, block), jnp.bfloat16),
            jax.ShapeDtypeStruct((bins, bins), jnp.bfloat16),
        ],
        compiler_params=pltpu.CompilerParams(vmem_limit_bytes=48 << 20),
        cost_estimate=pl.CostEstimate(
            flops=2 * bins * bins * 1024, bytes_accessed=2 * bins * bins, transcendentals=bins * bins
        ),
        name="attend_forward",
    )(pack, rel)


def attend_backward_kernel(
    block, bins, pack_ref, rel_ref, probs_ref, grad_ref, out_ref, drel_ref, stat_ref, acc_ref
):
    step = pl.program_id(0)
    steps = bins // block
    span = bins + block

    @pl.when(step == 0)
    def _():
        acc_ref[...] = jnp.zeros_like(acc_ref)
        drel_ref[...] = jnp.zeros_like(drel_ref)
        stat_ref[...] = jnp.zeros_like(stat_ref)

    query = pack_ref[pl.ds(pl.multiple_of(step * block, block), block), VD + KD :]
    base = pl.multiple_of(bins - block - step * block, block)
    grad_t = grad_ref[0]
    probs = probs_ref[...]
    acc_ref[:VD, :] += mxu(grad_t, probs, NN)
    grad_probs = mxu(grad_t.T, pack_ref[:, :VD], NT)
    wide = probs.astype(jnp.float32)
    scaled = wide * grad_probs
    delta = jnp.sum(scaled, axis=1, keepdims=True)
    grad_scores = (scaled - wide * delta).astype(jnp.bfloat16)
    grad_qc = mxu(grad_scores, pack_ref[:, VD : VD + KD], NN)
    query_t = query.T
    acc_ref[VD:, :] += mxu(query_t[:KD], grad_scores, NN)
    row = lax.broadcasted_iota(jnp.int32, (block, block), 0)
    col = lax.broadcasted_iota(jnp.int32, (block, block), 1)
    flip = (row + col == block - 1).astype(jnp.bfloat16)
    turned = mxu(flip, grad_scores, NN)
    turned = jnp.concatenate([turned, jnp.zeros((block, block), jnp.float32)], axis=1)
    turned = pltpu.roll(turned, 0, 1, stride=1, stride_axis=0).astype(jnp.bfloat16)
    grad_qp = mxu(
        flip.astype(jnp.float32),
        mxu(turned, rel_ref[pl.ds(base, span), :], NN),
        NN,
        exact_mode,
    )
    pos_turned = mxu(query_t[KD:], flip, NN).astype(jnp.bfloat16)
    drel_ref[:, pl.ds(base, span)] += mxu(pos_turned, turned, NN)
    stat_ref[0:1, :KD] += jnp.sum(grad_qc, axis=0, keepdims=True)
    stat_ref[1:2, :KD] += jnp.sum(grad_qp, axis=0, keepdims=True)
    out_ref[pl.ds(step, 1), VD + KD :, :] = (
        ((grad_qc + grad_qp) * (KD**-0.5)).T.astype(jnp.bfloat16)[None]
    )

    @pl.when(step == steps - 1)
    def _():
        for part in range(steps):
            out_ref[part, : VD + KD, :] = acc_ref[:, part * block : (part + 1) * block].astype(
                jnp.bfloat16
            )


def attend_backward(pack, rel, probs, grad):
    bins = pack.shape[0]
    block = query_block(bins)
    steps = bins // block
    return pl.pallas_call(
        lambda *refs: attend_backward_kernel(block, bins, *refs),
        grid=(steps,),
        in_specs=[
            pl.BlockSpec((bins, PACK), lambda i: (0, 0)),
            pl.BlockSpec((2 * bins, KD), lambda i: (0, 0)),
            pl.BlockSpec((block, bins), lambda i: (i, 0)),
            pl.BlockSpec((1, VD, block), lambda i: (i, 0, 0)),
        ],
        out_specs=[
            pl.BlockSpec((steps, GRAD_PACK, block), lambda i: (0, 0, 0)),
            pl.BlockSpec((KD, 2 * bins), lambda i: (0, 0)),
            pl.BlockSpec((8, 128), lambda i: (0, 0)),
        ],
        out_shape=[
            jax.ShapeDtypeStruct((steps, GRAD_PACK, block), jnp.bfloat16),
            jax.ShapeDtypeStruct((KD, 2 * bins), jnp.float32),
            jax.ShapeDtypeStruct((8, 128), jnp.float32),
        ],
        scratch_shapes=[pltpu.VMEM((VD + KD, bins), jnp.float32)],
        compiler_params=pltpu.CompilerParams(vmem_limit_bytes=48 << 20),
        cost_estimate=pl.CostEstimate(
            flops=2 * bins * bins * 2048, bytes_accessed=2 * bins * bins, transcendentals=0
        ),
        name="attend_backward",
    )(pack, rel, probs, grad)


def heads_kernel(
    track_human,
    track_mouse,
    tiles_human,
    pick_ref,
    rows_ref,
    weight_ref,
    human_own_ref,
    human_oth_ref,
    mouse_own_ref,
    mouse_oth_ref,
    bias_ref,
    count_human_ref,
    count_mouse_ref,
    grad_ref,
    dtrunk_ref,
    dbias_ref,
    loss_ref,
):
    step = pl.program_id(0)
    kind = pick_ref[0]
    swapped = pick_ref[1] == 1
    on_human = jnp.logical_and(step < tiles_human, kind == 0)
    on_mouse = jnp.logical_and(step >= tiles_human, kind == 1)

    @pl.when(step == 0)
    def _():
        dtrunk_ref[...] = jnp.zeros_like(dtrunk_ref)
        loss_ref[...] = jnp.zeros_like(loss_ref)

    def score(own_ref, oth_ref, count_ref, first, tracks):
        track = lax.broadcasted_iota(jnp.int32, (TILE, 1), 0) + first * TILE
        valid = track < tracks
        own = jnp.where(valid, own_ref[...], 0.0).astype(jnp.bfloat16)
        oth = jnp.where(valid, oth_ref[...], 0.0).astype(jnp.bfloat16)
        head = jnp.concatenate(
            [jnp.where(swapped, oth, own), jnp.where(swapped, own, oth)], axis=1
        )
        logits = mxu(head, rows_ref[...], NT) + bias_ref[...]
        counts = count_ref[0].astype(jnp.float32)
        small = jnp.exp(-jnp.abs(logits))
        above = 1.0 + small
        log_above = jnp.log(above) + (small - (above - 1.0)) / above
        shifted = jnp.maximum(logits, 0.0) + log_above
        predicted = shifted
        shifted = shifted + log_eps
        sigma = jnp.where(logits >= 0.0, 1.0, small) / above
        weight = weight_ref[0:1, :]
        rows_loss = weight * (predicted - counts * jnp.log(shifted))
        grad = weight * (sigma - counts * sigma / shifted)
        rows_loss = jnp.where(valid, rows_loss, 0.0)
        grad = jnp.where(valid, grad, 0.0)
        loss_ref[...] += jnp.sum(rows_loss.reshape(TILE // 8, 8, -1), axis=0)
        dbias_ref[...] = jnp.sum(grad, axis=1, keepdims=True)
        grad_low = grad.astype(jnp.bfloat16)
        grad_ref[...] = grad_low
        dtrunk_ref[...] += mxu(grad_low.T, head, NN)

    @pl.when(on_human)
    def _():
        score(human_own_ref, human_oth_ref, count_human_ref, step, track_human)

    @pl.when(on_mouse)
    def _():
        score(mouse_own_ref, mouse_oth_ref, count_mouse_ref, step - tiles_human, track_mouse)

    @pl.when(jnp.logical_not(jnp.logical_or(on_human, on_mouse)))
    def _():
        dbias_ref[...] = jnp.zeros_like(dbias_ref)


def score_heads(window, pick, rows, weight, human, mouse, bias, count_human, count_mouse):
    bins, width = rows.shape
    share = human[0].shape[1]
    rest = width - share
    track_human, track_mouse = count_human.shape[1], count_mouse.shape[1]
    tiles_human, tiles_mouse = pl.cdiv(track_human, TILE), pl.cdiv(track_mouse, TILE)
    tiles = tiles_human + tiles_mouse

    def human_tile(t, p):
        return jnp.where(p[0] == 0, jnp.minimum(t, tiles_human - 1), 0)

    def mouse_tile(t, p):
        return jnp.where(p[0] == 1, jnp.maximum(t - tiles_human, 0), 0)

    whole = lambda t, p: (0, 0)
    along = lambda t, p: (t, 0)
    return pl.pallas_call(
        lambda *refs: heads_kernel(track_human, track_mouse, tiles_human, *refs),
        grid_spec=pltpu.PrefetchScalarGridSpec(
            num_scalar_prefetch=1,
            grid=(tiles,),
            in_specs=[
                pl.BlockSpec((bins, width), whole),
                pl.BlockSpec((8, bins), whole),
                pl.BlockSpec((TILE, share), lambda t, p: (human_tile(t, p), 0)),
                pl.BlockSpec((TILE, rest), lambda t, p: (human_tile(t, p), 0)),
                pl.BlockSpec((TILE, share), lambda t, p: (mouse_tile(t, p), 0)),
                pl.BlockSpec((TILE, rest), lambda t, p: (mouse_tile(t, p), 0)),
                pl.BlockSpec((TILE, 1), along),
                pl.BlockSpec((1, TILE, bins), lambda t, p: (window, human_tile(t, p), 0)),
                pl.BlockSpec((1, TILE, bins), lambda t, p: (window, mouse_tile(t, p), 0)),
            ],
            out_specs=[
                pl.BlockSpec((TILE, bins), along),
                pl.BlockSpec((bins, width), whole),
                pl.BlockSpec((TILE, 1), along),
                pl.BlockSpec((8, bins), whole),
            ],
        ),
        out_shape=[
            jax.ShapeDtypeStruct((tiles * TILE, bins), jnp.bfloat16),
            jax.ShapeDtypeStruct((bins, width), jnp.float32),
            jax.ShapeDtypeStruct((tiles * TILE, 1), jnp.float32),
            jax.ShapeDtypeStruct((8, bins), jnp.float32),
        ],
        compiler_params=pltpu.CompilerParams(vmem_limit_bytes=56 << 20),
        cost_estimate=pl.CostEstimate(
            flops=4 * bins * width * track_human,
            bytes_accessed=4 * width * track_human,
            transcendentals=4 * bins * track_human,
        ),
        name="score_heads",
    )(pick, rows, weight, *human, *mouse, bias, count_human, count_mouse)


def head_grads_kernel(windows, tiles_human, pick_ref, *refs):
    grads, rows, out_ref, acc_ref = refs[:windows], refs[windows], refs[windows + 1], refs[-1]
    step = pl.program_id(0)
    mine = jnp.where(step < tiles_human, 0, 1)
    acc_ref[...] = jnp.zeros_like(acc_ref)
    for window in range(windows):

        @pl.when(pick_ref[window] == mine)
        def _():
            acc_ref[...] += mxu(grads[window][...], rows[window], NN)

    out_ref[...] = acc_ref[...].astype(jnp.bfloat16)


def head_grads(pick, grads, rows, tiles_human):
    windows, bins, share = rows.shape
    tiles = grads[0].shape[0] // TILE

    def tile_of(window):
        def index(t, p):
            first = jnp.where(p[window] == 0, jnp.minimum(t, tiles_human - 1), 0)
            return (jnp.where(p[window] == 1, jnp.maximum(t, tiles_human), first), 0)

        return index

    return pl.pallas_call(
        lambda *refs: head_grads_kernel(windows, tiles_human, *refs),
        grid_spec=pltpu.PrefetchScalarGridSpec(
            num_scalar_prefetch=1,
            grid=(tiles,),
            in_specs=[pl.BlockSpec((TILE, bins), tile_of(w)) for w in range(windows)]
            + [pl.BlockSpec((windows, bins, share), lambda t, p: (0, 0, 0))],
            out_specs=pl.BlockSpec((TILE, share), lambda t, p: (t, 0)),
            scratch_shapes=[pltpu.VMEM((TILE, share), jnp.float32)],
        ),
        out_shape=jax.ShapeDtypeStruct((tiles * TILE, share), jnp.bfloat16),
        compiler_params=pltpu.CompilerParams(vmem_limit_bytes=40 << 20),
        cost_estimate=pl.CostEstimate(
            flops=2 * windows * bins * share * tiles * TILE,
            bytes_accessed=4 * tiles * TILE * share,
            transcendentals=0,
        ),
        name="head_grads",
    )(pick, *grads, rows)


def norm_stats(values):
    mean = jnp.mean(values, axis=-1, keepdims=True)
    centred = values - mean
    inverse = lax.rsqrt(jnp.mean(centred * centred, axis=-1, keepdims=True) + norm_eps)
    return mean, inverse


def norm_backward(grad_output, scaled, inverse, norm_gain):
    grad_scaled = grad_output * norm_gain
    mean_grad = jnp.mean(grad_scaled, axis=-1, keepdims=True)
    mean_proj = jnp.mean(grad_scaled * scaled, axis=-1, keepdims=True)
    grad_input = inverse * (grad_scaled - mean_grad - scaled * mean_proj)
    return (grad_input, jnp.sum(grad_output * scaled, axis=0), jnp.sum(grad_output, axis=0))


def sum_over_model(partial):
    low = partial.astype(jnp.bfloat16)
    if lax.axis_size("mp") == 2:
        other = lax.ppermute(low, "mp", [(0, 1), (1, 0)])
        return low.astype(jnp.float32) + other.astype(jnp.float32)
    return lax.psum(low, "mp").astype(jnp.float32)


def in_model_order(own, dim):
    if lax.axis_size("mp") == 2:
        first = lax.axis_index("mp") == 0
        other = lax.ppermute(own, "mp", [(0, 1), (1, 0)])
        return jnp.concatenate(
            [jnp.where(first, own, other), jnp.where(first, other, own)], axis=dim
        )
    return lax.all_gather(own, "mp", axis=dim, tiled=True)


def other_rows(own, chunk):
    count = lax.axis_size("dp") * lax.axis_size("seq")
    place = lax.axis_index("dp") * lax.axis_size("seq") + lax.axis_index("seq")
    rows = own.shape[0]
    start = jnp.minimum(place * chunk, rows - chunk)
    part = lax.dynamic_slice_in_dim(own, start, chunk, 0)
    if count * chunk != rows:
        part = lax.dynamic_slice_in_dim(
            jnp.concatenate([part, part], axis=0),
            jnp.minimum(place * chunk - start, chunk),
            chunk,
            0,
        )
    part = lax.ppermute(part, "mp", [(0, 1), (1, 0)])
    return lax.all_gather(part, ("dp", "seq"), axis=0, tiled=True)


def swap_pairs(axis, step):
    return [(i, i ^ step) for i in range(lax.axis_size(axis))]


def sum_everywhere(vector):
    for axis in ("dp", "seq"):
        step = 1
        while step < lax.axis_size(axis):
            vector = vector + lax.ppermute(vector, axis, swap_pairs(axis, step))
            step *= 2
    return vector


def scatter_sum(full):
    dp_size, seq_size = lax.axis_size("dp"), lax.axis_size("seq")
    dp_index, seq_index = lax.axis_index("dp"), lax.axis_index("seq")
    rows = full.shape[0] // (dp_size * seq_size)
    cols = full.shape[1]
    kept = full.astype(jnp.bfloat16)
    step = 1
    while step < dp_size:
        bit = (dp_index // step) % 2
        split = kept.reshape(-1, 2, seq_size * rows, cols)
        mine = lax.dynamic_index_in_dim(split, bit, 1, keepdims=False)
        theirs = lax.dynamic_index_in_dim(split, 1 - bit, 1, keepdims=False)
        got = lax.ppermute(theirs, "dp", swap_pairs("dp", step))
        kept = (mine.astype(jnp.float32) + got.astype(jnp.float32)).astype(jnp.bfloat16)
        step *= 2
    parts = kept.reshape(seq_size, rows, cols)

    def part(index):
        return lax.dynamic_index_in_dim(parts, index % seq_size, 0, keepdims=False)

    ring = [(i, (i + 1) % seq_size) for i in range(seq_size)]
    moving = part(seq_index - 1 + seq_size)
    for step in range(seq_size - 1):
        got = lax.ppermute(moving, "seq", ring)
        total = got.astype(jnp.float32) + part(seq_index - 2 - step + 2 * seq_size).astype(
            jnp.float32
        )
        moving = total.astype(jnp.bfloat16)
    return total


def on_device(
    trunk_in,
    norm1_gain,
    norm1_bias,
    w_query,
    w_key,
    w_value,
    w_rel,
    content_bias,
    pos_bias,
    w_out,
    b_out,
    norm2_gain,
    norm2_bias,
    w_in,
    b_in,
    w_hid,
    b_hid,
    head_human,
    bias_human,
    head_mouse,
    bias_mouse,
    species,
    targets_human,
    targets_mouse,
):
    windows, bins, width = trunk_in.shape
    heads = content_bias.shape[0]
    dp_size, seq_size, mp_size = (lax.axis_size(axis) for axis in ("dp", "seq", "mp"))
    seq_index, mp_index = lax.axis_index("seq"), lax.axis_index("mp")
    place = lax.axis_index("dp") * seq_size + seq_index
    places = dp_size * seq_size
    all_bins = bins * seq_size
    block = query_block(all_bins)
    query_start = seq_index * bins
    key_scale = KD ** (-0.5)
    loss_scale = 1.0 / math.sqrt(windows * dp_size * CROP)
    crop_start = (all_bins - CROP) // 2
    bf16 = jnp.bfloat16

    if heads % seq_size == 0:
        groups = [[w] for w in range(windows)]
    else:
        groups = [list(range(windows))]
    group_size = len(groups[0])
    pairs = heads * group_size
    pairs_here = -(-pairs // seq_size)
    pair_heads = [
        jnp.minimum((seq_index * pairs_here + j) // group_size, heads - 1)
        for j in range(pairs_here)
    ]

    def spread(array):
        short = seq_size * pairs_here - pairs
        if short:
            array = jnp.pad(array, [(0, short)] + [(0, 0)] * (array.ndim - 1))
        return exchange(array.reshape((seq_size, pairs_here) + array.shape[1:]))

    def exchange(array):
        return lax.all_to_all(array, "seq", split_axis=0, concat_axis=0, tiled=True)

    def bins_last(array):
        if bins == block:
            return array
        depth = array.shape[1]
        array = array.transpose(1, 0, 2).reshape(depth, all_bins // block, block)
        return array.transpose(1, 0, 2)

    def owners_first(array):
        if bins == block:
            return array
        depth = array.shape[1]
        array = array.transpose(1, 0, 2).reshape(depth, seq_size, bins)
        return array.transpose(1, 0, 2)

    def collect(arrays):
        depth = arrays[0].shape[1]
        stacked = jnp.stack([owners_first(a) for a in arrays], axis=1)
        stacked = exchange(stacked).reshape(seq_size * pairs_here, depth, bins)[:pairs]
        stacked = stacked.reshape(heads, group_size, depth, bins).transpose(0, 2, 1, 3)
        return stacked.reshape(heads, depth, group_size * bins)

    def all_rows(own, chunk):
        if mp_size != 2:
            full = lax.all_gather(own, "mp", axis=1, tiled=True)
            half = full.shape[1] // 2
            return (full[:, :half], full[:, half:])
        return (own, other_rows(own, chunk))

    def chunk_of(rows):
        return -(-rows // (places * 16)) * 16

    if mp_size == 2:
        out_oth = other_rows(w_out, w_out.shape[0] // places)
        first = mp_index == 0
        w_out_all = jnp.concatenate(
            [jnp.where(first, w_out, out_oth), jnp.where(first, out_oth, w_out)], axis=0
        )
    else:
        w_out_all = lax.all_gather(w_out, "mp", axis=0, tiled=True)
    track_human, track_mouse = head_human.shape[1], head_mouse.shape[1]
    human = all_rows(head_human.T, chunk_of(track_human))
    mouse = all_rows(head_mouse.T, chunk_of(track_mouse))

    def per_head(weight, size):
        return weight.reshape(width, heads, size)

    value_w, key_w, query_w = per_head(w_value, VD), per_head(w_key, KD), per_head(w_query, KD)
    w_pack = jnp.concatenate([value_w, key_w, query_w, query_w], axis=2).reshape(
        width, heads * PACK
    )
    w_grad = jnp.concatenate([value_w, key_w, query_w], axis=2).reshape(width, heads * GRAD_PACK)
    pack_scale = jnp.concatenate(
        [jnp.ones((VD + KD,), jnp.float32), jnp.full((2 * KD,), key_scale, jnp.float32)]
    )
    pack_scale = jnp.tile(pack_scale, heads)
    pack_bias = jnp.concatenate(
        [jnp.zeros((heads, VD + KD), jnp.float32), content_bias, pos_bias], axis=1
    ).reshape(-1)

    basis = jnp.pad(rel_basis(), [(0, 1), (0, 0)])
    w_rel_heads = w_rel.reshape(FEAT, heads, KD)
    rels = [
        mxu(
            basis,
            lax.dynamic_index_in_dim(w_rel_heads, head, 1, keepdims=False).astype(jnp.float32),
            NN,
            exact_mode,
        ).astype(bf16)
        for head in pair_heads
    ]

    trunk, stats1, normed1, packs = [], [], [], []
    for group in groups:
        rows = group_size * bins
        values = trunk_in[group[0] : group[-1] + 1].reshape(rows, width).astype(jnp.float32)
        mean, inverse = norm_stats(values)
        normed = ((values - mean) * inverse * norm1_gain + norm1_bias).astype(bf16)
        pack = (mxu(normed, w_pack, NN) * pack_scale + pack_bias).astype(bf16)
        pack = pack.reshape(group_size, bins, heads, PACK).transpose(2, 0, 1, 3)
        pack = spread(pack.reshape(pairs, bins, PACK))
        trunk.append(values)
        stats1.append((mean, inverse))
        normed1.append(normed)
        packs.append([pack[:, j].reshape(all_bins, PACK) for j in range(pairs_here)])

    probs, attended, mids, stats2, normed2, preacts, actives, trunk_out, trunk_low = (
        [] for _ in range(9)
    )
    for g, group in enumerate(groups):
        outs, kept = [], []
        for j in range(pairs_here):
            out, prob = attend_forward(packs[g][j], rels[j])
            outs.append(out)
            kept.append(prob)
        probs.append(kept)
        att = collect(outs).reshape(heads * VD, group_size * bins)
        attended.append(att)
        att_all = in_model_order(att, 0)
        mid = trunk[g] + mxu(att_all, w_out_all, TN) + b_out
        mean, inverse = norm_stats(mid)
        normed = ((mid - mean) * inverse * norm2_gain + norm2_bias).astype(bf16)
        preact = mxu(normed, w_in, NN) + b_in
        active = jnp.maximum(preact, 0.0).astype(bf16)
        out = mid + (sum_over_model(mxu(active, w_hid, NN)) + b_hid)
        mids.append(mid)
        stats2.append((mean, inverse))
        normed2.append(normed)
        preacts.append(preact > 0.0)
        actives.append(active)
        trunk_out.append(out)
        trunk_low.append(out.astype(bf16))

    bin_place = query_start + jnp.arange(bins)
    in_crop = ((bin_place >= crop_start) & (bin_place < crop_start + CROP)).astype(jnp.float32)
    weight = jnp.broadcast_to((in_crop * loss_scale)[None, :], (8, bins))
    has_crop = (query_start + bins > crop_start) & (query_start < crop_start + CROP)
    picks = jnp.where(has_crop, species, 2)
    count_human = targets_human.transpose(0, 2, 1)
    count_mouse = targets_mouse.transpose(0, 2, 1)
    tiles_human, tiles_mouse = pl.cdiv(track_human, TILE), pl.cdiv(track_mouse, TILE)
    bias_all = jnp.concatenate(
        [
            jnp.pad(bias_human, (0, tiles_human * TILE - track_human)),
            jnp.pad(bias_mouse, (0, tiles_mouse * TILE - track_mouse)),
        ]
    )[:, None]
    order = mp_index if mp_size == 2 else 0
    grad_rows, logit_grads, track_sums, losses = [], [], [], []
    low_windows = [
        trunk_low[g][i * bins : (i + 1) * bins] for g in range(len(groups)) for i in range(group_size)
    ]
    for window in range(windows):
        pick = jnp.stack([picks[window], jnp.int32(0) + order])
        grad_low, grad_out, track_sum, loss = score_heads(
            window, pick, low_windows[window], weight, human, mouse, bias_all, count_human, count_mouse
        )
        logit_grads.append(grad_low)
        grad_rows.append(grad_out)
        track_sums.append(track_sum)
        losses.append(jnp.sum(loss))
    share = head_human.shape[0]
    own_rows = jnp.stack(
        [lax.dynamic_slice_in_dim(rows, mp_index * share, share, 1) for rows in low_windows]
    )
    dheads = head_grads(picks, logit_grads, own_rows, tiles_human)
    dheads = lax.psum(dheads, ("dp", "seq")).astype(jnp.float32)
    dtracks = sum(track_sums)[:, 0]

    grad_mids, grad_outs, grad_pres, grad_mid_lows, packed_grads = [], [], [], [], []
    sums = [0.0] * 5
    drels = [0.0] * pairs_here
    dstats = [0.0] * pairs_here
    for g, group in enumerate(groups):
        grad_trunk = jnp.concatenate([grad_rows[w] for w in group], axis=0)
        grad_out = grad_trunk.astype(bf16)
        grad_preact = jnp.where(preacts[g], mxu(grad_out, w_hid, NT), 0.0)
        grad_pre = grad_preact.astype(bf16)
        grad_normed = sum_over_model(mxu(grad_pre, w_in, NT))
        mean, inverse = stats2[g]
        grad_norm, dgain, dbias = norm_backward(
            grad_normed, (mids[g] - mean) * inverse, inverse, norm2_gain
        )
        grad_mid = grad_trunk + grad_norm
        grad_mid_low = grad_mid.astype(bf16)
        parts = (
            dgain,
            dbias,
            jnp.sum(grad_mid, axis=0),
            jnp.sum(grad_trunk, axis=0),
            jnp.sum(grad_preact, axis=0),
        )
        sums = [old + new for old, new in zip(sums, parts)]
        grad_outs.append(grad_out)
        grad_pres.append(grad_pre)
        grad_mids.append(grad_mid)
        grad_mid_lows.append(grad_mid_low)
        grad_att = mxu(w_out, grad_mid_low, NT).astype(bf16)
        grad_att = grad_att.reshape(heads, VD, group_size, bins).transpose(0, 2, 1, 3)
        grad_att = spread(grad_att.reshape(pairs, VD, bins))
        outs = []
        for j in range(pairs_here):
            out, drel, stat = attend_backward(
                packs[g][j], rels[j], probs[g][j], bins_last(grad_att[:, j])
            )
            outs.append(out)
            drels[j] = drels[j] + drel
            dstats[j] = dstats[j] + stat
        packed_grads.append(collect(outs).reshape(heads * GRAD_PACK, group_size * bins))

    join = lambda arrays: jnp.concatenate(arrays, axis=0)
    dtrunk_weights = jnp.concatenate(
        [
            mxu(join(normed2), join(grad_pres), TN).astype(bf16),
            mxu(join(grad_outs), join(actives), TN).astype(bf16),
            lax.dot_general(
                join(grad_mid_lows),
                jnp.concatenate(attended, axis=1),
                (((0,), (1,)), ((), ())),
                preferred_element_type=jnp.float32,
            ).astype(bf16),
        ],
        axis=1,
    )
    trunk_summed = scatter_sum(dtrunk_weights)

    grad_inputs = []
    sums1 = [0.0, 0.0]
    for g, group in enumerate(groups):
        grad_normed = sum_over_model(
            lax.dot_general(
                packed_grads[g],
                w_grad,
                (((0,), (1,)), ((), ())),
                preferred_element_type=jnp.float32,
            )
        )
        mean, inverse = stats1[g]
        grad_norm, dgain, dbias = norm_backward(
            grad_normed, (trunk[g] - mean) * inverse, inverse, norm1_gain
        )
        sums1 = [sums1[0] + dgain, sums1[1] + dbias]
        grad_inputs.append((grad_mids[g] + grad_norm).reshape(group_size, bins, width))
    dpack = lax.dot_general(
        join(normed1),
        jnp.concatenate(packed_grads, axis=1),
        (((0,), (1,)), ((), ())),
        preferred_element_type=jnp.float32,
    ).astype(bf16)
    pack_summed = scatter_sum(dpack).reshape(-1, heads, GRAD_PACK)

    dw_rel = jnp.zeros((heads, FEAT, KD), jnp.float32)
    dstat = jnp.zeros((heads, 2, KD), jnp.float32)
    for j, head in enumerate(pair_heads):
        mine = (jnp.arange(heads) == head).astype(jnp.float32)[:, None, None]
        part = lax.dot_general(
            basis,
            drels[j],
            (((0,), (1,)), ((), ())),
            precision=exact_mode,
            preferred_element_type=jnp.float32,
        )
        dw_rel = dw_rel + mine * part
        dstat = dstat + mine * dstats[j][None, :2, :KD]

    def sum_parts(parts):
        sizes = [part.size for part in parts]
        flat = [part.reshape(-1) for part in parts]
        flat = [jnp.pad(part, (0, -part.size % 128)) for part in flat]
        total = sum_everywhere(jnp.concatenate(flat).reshape(-1, 128)).reshape(-1)
        results, start = [], 0
        for part, size in zip(parts, sizes):
            results.append(total[start : start + size].reshape(part.shape))
            start += -(-size // 128) * 128
        return results

    dgain2, dbias2, db_out, db_hid, db_in, dtracks, loss = sum_parts(
        list(sums) + [dtracks, sum(losses)[None]]
    )
    dgain1, dbias1, dstat, dw_rel = sum_parts(list(sums1) + [dstat, dw_rel])

    def own(array, dim=0):
        size = array.shape[dim] // places
        return lax.dynamic_slice_in_dim(array, place * size, size, dim)

    rel_rows = own(dw_rel, 1).transpose(1, 0, 2).reshape(-1, heads * KD)
    hidden = w_in.shape[1]
    pack_rows = pack_summed.shape[0]
    shape3 = (windows, bins, width)
    return (
        join(trunk_out).reshape(shape3),
        loss[0],
        join(grad_inputs).reshape(shape3),
        own(dgain1),
        own(dbias1),
        pack_summed[:, :, VD + KD :].reshape(pack_rows, heads * KD),
        pack_summed[:, :, VD : VD + KD].reshape(pack_rows, heads * KD),
        pack_summed[:, :, :VD].reshape(pack_rows, heads * VD),
        rel_rows,
        own(dstat[:, 0], 1),
        own(dstat[:, 1], 1),
        trunk_summed[:, 2 * hidden :].T,
        own(db_out),
        own(dgain2),
        own(dbias2),
        trunk_summed[:, :hidden],
        db_in,
        trunk_summed[:, hidden : 2 * hidden].T,
        own(db_hid),
        dheads[:track_human].T,
        dtracks[:track_human],
        dheads[tiles_human * TILE : tiles_human * TILE + track_mouse].T,
        dtracks[tiles_human * TILE : tiles_human * TILE + track_mouse],
    )


def solution(mesh):
    in_specs = (
        P("dp", "seq", None),
        P(),
        P(),
        P(None, "mp"),
        P(None, "mp"),
        P(None, "mp"),
        P(None, "mp"),
        P("mp", None),
        P("mp", None),
        P("mp", None),
        P(),
        P(),
        P(),
        P(None, "mp"),
        P("mp"),
        P("mp", None),
        P(),
        P("mp", None),
        P(),
        P("mp", None),
        P(),
        P("dp"),
        P("dp", "seq", None),
        P("dp", "seq", None),
    )
    out_specs = (
        P("dp", "seq", None),
        P(),
        P("dp", "seq", None),
        P(("dp", "seq")),
        P(("dp", "seq")),
        P(("dp", "seq"), "mp"),
        P(("dp", "seq"), "mp"),
        P(("dp", "seq"), "mp"),
        P(("dp", "seq"), "mp"),
        P("mp", ("dp", "seq")),
        P("mp", ("dp", "seq")),
        P("mp", ("dp", "seq")),
        P(("dp", "seq")),
        P(("dp", "seq")),
        P(("dp", "seq")),
        P(("dp", "seq"), "mp"),
        P("mp"),
        P("mp", ("dp", "seq")),
        P(("dp", "seq")),
        P("mp", None),
        P(),
        P("mp", None),
        P(),
    )
    return jax.shard_map(
        on_device, mesh=mesh, in_specs=in_specs, out_specs=out_specs, check_vma=False
    )
```

time: 2510 us -> 1150 us (0.46)
  waiting for transfers between devices: 1380 us -> 362 us
  local copies, waits for them, and re-layouts: 434 us -> 207 us
  matrix products: 352 us -> 126 us
  Pallas kernels: 0 us -> 195 us
  blocking collectives: 162 us -> 0 us
  starting transfers between devices: 12.3 us -> 84.2 us
  loops' own time: 31.5 us -> 0 us
    reduce_scatter x8 -> x0, waiting for transfers between devices: 587 us -> none  [the longest x1 153 us: on_device(): lax.psum_scatter(value_terms, 'seq', scatter_dimension=1, tiled=True)]
    psum x5 -> x1, waiting for transfers between devices: 535 us -> 0.01 us  [on_device(): dheads = lax.psum(dheads, ('dp', 'seq')).astype(jnp.float32)]
    all_gather x4 -> x3, waiting for transfers between devices: 254 us -> 0.01 us  [other_rows(): return lax.all_gather(part, ('dp', 'seq'), axis=0, tiled=True)]
    ppermute x0 -> x33, waiting for transfers between devices: none -> 253 us  [the longest x9 145 us: sum_over_model(): other = lax.ppermute(low, 'mp', [(0, 1), (1, 0)])]
    dot_general x37 -> x30, matrix products: 327 us -> 126 us  [the longest x24 96.3 us: mxu(): lax.dot_general(left_arr, right_arr, dims, precision=precision, preferred...]
    pallas_call x0 -> x10, Pallas kernels: none -> 195 us  [the longest x3 90.7 us: score_heads(): pl.pallas_call(lambda *refs: heads_kernel(track_human, track_mouse, tiles...]
    reshape x10 -> x11, local copies, waits for them, and re-layouts: 221 us -> 35.5 us  [the longest x1 24.1 us: scatter_sum(): split = kept.reshape(-1, 2, seq_size * rows, cols)]
    all_to_all x0 -> x12, waiting for transfers between devices: none -> 108 us  [exchange(): return lax.all_to_all(array, 'seq', split_axis=0, concat_axis=0, tiled=True)]
  transfers between devices with their start and end apart: 21 -> 49, of which waited for: 13 -> 27; matrix products, arithmetic and copies ran while one was open for 25% -> 37% of each run, Pallas kernels for 0% -> 14%
where the time goes in v1:
time: 1150 us; the launch traced here: 1140 us
  waiting for transfers between devices  362 us (31%)
  local copies, waits for them, and re-layouts  207 us (18%)
  Pallas kernels  195 us (17%)
  other arithmetic  145 us (13%)
  matrix products  126 us (11%)
  starting transfers between devices  84.2 us (7%)
  between operations  17.9 us (2%)
    ppermute x9, waiting for transfers between devices, sum_over_model(): other = lax.ppermute(low, 'mp', [(0, 1), (1, 0)])  145 us
    all_to_all x12, waiting for transfers between devices, exchange(): return lax.all_to_all(array, 'seq', split_axis=0, concat_axis=0, tiled=True)  108 us
    dot_general x24, matrix products, mxu(): lax.dot_general(left_arr, right_arr, dims, precision=precision, preferred...  96.3 us
    pallas_call x3, Pallas kernels, score_heads(): pl.pallas_call(lambda *refs: heads_kernel(track_human, track_mouse, tiles...  90.7 us
    unnamed x330, local copies, waits for them, and re-layouts  88.5 us
    pallas_call x3, Pallas kernels, attend_backward(): pl.pallas_call(lambda *refs: attend_backward_kernel(block, bins, *refs),...  56.1 us
    all_to_all x12, starting transfers between devices, exchange(): return lax.all_to_all(array, 'seq', split_axis=0, concat_axis=0, tiled=True)  54 us
    ppermute x4, waiting for transfers between devices, scatter_sum(): got = lax.ppermute(theirs, 'dp', swap_pairs('dp', step))  50.8 us
  transfers between devices with their start and end apart: 49, of which 27 were waited for; matrix products, arithmetic and copies ran while one was open for 37% of the time, Pallas kernels for 14%

profile of v1, /device:TPU:0, one launch (start us, length us, event | category | flops | bytes accessed | tf_op | source)
XLA Modules:
  0.0 1137.7 jit_solution(3837161283704584421)
XLA Ops:
  48.7 29.1 %all-to-all-done.4 = bf16[4,1,384,384]{3,2,1,0:T(8,128)(2,1)S(1)} async-done(((bf16[4,1,384,384]{3,2,1,0:T(8,128)(2,1)}), bf16[4,1,384,384]{3,2,1,0:T(8,128)(2,1)S(1)}, u32[]{:S(2)}, u32[]{:S(2)}) %all-to-all-start.4) | async-done | bytes 1179680 | tf_op jit(solution)/shard_map/all_to_all | solution.py:518
  93.1 22.1 %all-to-all-done = bf16[4,1,384,384]{3,2,1,0:T(8,128)(2,1)S(1)} async-done(((bf16[4,1,384,384]{3,2,1,0:T(8,128)(2,1)}), bf16[4,1,384,384]{3,2,1,0:T(8,128)(2,1)S(1)}, u32[]{:S(2)}, u32[]{:S(2)}) %all-to-all-start) | async-done | bytes 1179680 | tf_op jit(solution)/shard_map/all_to_all | solution.py:518
  126.6 10.2 attend_forward.3
  138.5 17.0 %all-to-all-done.2 = bf16[4,1,384,384]{3,2,1,0:T(8,128)(2,1)S(1)} async-done(((bf16[4,1,384,384]{3,2,1,0:T(8,128)(2,1)}), bf16[4,1,384,384]{3,2,1,0:T(8,128)(2,1)S(1)}, u32[]{:S(2)}, u32[]{:S(2)}) %all-to-all-start.2) | async-done | bytes 1179680 | tf_op jit(solution)/shard_map/all_to_all | solution.py:518
  164.0 10.4 attend_forward.4
  180.9 10.4 attend_forward.5
  202.5 23.8 %all-to-all-done.5 = bf16[4,1,192,384]{3,2,1,0:T(8,128)(2,1)} async-done(((bf16[4,1,192,384]{3,2,1,0:T(8,128)(2,1)}), bf16[4,1,192,384]{3,2,1,0:T(8,128)(2,1)}, u32[]{:S(2)}, u32[]{:S(2)}) %all-to-all-start.5) | async-done | bytes 589856 | tf_op jit(solution)/shard_map/all_to_all | solution.py:518
  229.9 11.7 %collective-permute-done.5 = bf16[768,384]{1,0:T(8,128)(2,1)} collective-permute-done((bf16[768,384]{1,0:T(8,128)(2,1)}, bf16[768,384]{1,0:T(8,128)(2,1)}, u32[]{:S(2)}, u32[]{:S(2)}) %collective-permute-start.5) | collective-permute-done | bytes 589856 | tf_op jit(solution)/shard_map/ppermute | solution.py:391
  297.9 25.2 %collective-permute-done.4 = bf16[384,1536]{1,0:T(8,128)(2,1)} collective-permute-done((bf16[384,1536]{1,0:T(8,128)(2,1)}, bf16[384,1536]{1,0:T(8,128)(2,1)}, u32[]{:S(2)}, u32[]{:S(2)}) %collective-permute-start.4) | collective-permute-done | bytes 1179680 | tf_op jit(solution)/shard_map/ppermute | solution.py:383
  323.0 23.2 %collective-permute-done.6 = bf16[384,1536]{1,0:T(8,128)(2,1)} collective-permute-done((bf16[384,1536]{1,0:T(8,128)(2,1)}, bf16[384,1536]{1,0:T(8,128)(2,1)}, u32[]{:S(2)}, u32[]{:S(2)}) %collective-permute-start.6) | collective-permute-done | bytes 1179680 | tf_op jit(solution)/shard_map/ppermute | solution.py:383
  363.3 35.2 %score_heads.5 = (bf16[7168,384]{1,0:T(8,128)(2,1)}, f32[384,1536]{1,0:T(8,128)}, f32[7168,1]{1,0:T(8,128)}, f32[8,384]{1,0:T(8,128)}) custom-call(s32[2]{0:T(128)} %pad_add_fusion.2.refs_0_, bf16[384,1536]{1,0:T(8,128)(2,1)} %get-tuple-element.312.refs_1_, f32[8,384]{1,0:T(8,128)} %broadcast_in_dim.20.refs_2_, bf16[5313,768]{1,0:T(8,128)(2,1)} %bitcast.339, ...), custom_call_target="tpu_custom_call" | custom-call | flops 12534939648 | bytes 32643072 | tf_op jit(solution)/shard_map/score_heads/pallas_call | solution.py:280
  412.9 35.4 %score_heads.4 = (bf16[7168,384]{1,0:T(8,128)(2,1)}, f32[384,1536]{1,0:T(8,128)}, f32[7168,1]{1,0:T(8,128)}, f32[8,384]{1,0:T(8,128)}) custom-call(s32[2]{0:T(128)} %get-tuple-element.336.refs_0_, bf16[384,1536]{1,0:T(8,128)(2,1)} %get-tuple-element.310.refs_1_, f32[8,384]{1,0:T(8,128)} %broadcast_in_dim.20.refs_2_, bf16[5313,768]{1,0:T(8,128)(2,1)} %bitcast.340, ...), custom_call_target="tpu_custom_call" | custom-call | flops 12534939648 | bytes 32643072 | tf_op jit(solution)/shard_map/score_heads/pallas_call | solution.py:280
  460.5 20.1 %score_heads.3 = (bf16[7168,384]{1,0:T(8,128)(2,1)}, f32[384,1536]{1,0:T(8,128)}, f32[7168,1]{1,0:T(8,128)}, f32[8,384]{1,0:T(8,128)}) custom-call(s32[2]{0:T(128)} %get-tuple-element.335.refs_0_, bf16[384,1536]{1,0:T(8,128)(2,1)} %get-tuple-element.240.refs_1_, f32[8,384]{1,0:T(8,128)} %broadcast_in_dim.20.refs_2_, bf16[5313,768]{1,0:T(8,128)(2,1)} %bitcast.341, ...), custom_call_target="tpu_custom_call" | custom-call | flops 12534939648 | bytes 32643072 | tf_op jit(solution)/shard_map/score_heads/pallas_call | solution.py:280
  515.5 11.5 %collective-permute-done.9 = bf16[384,1536]{1,0:T(8,128)(2,1)S(1)} collective-permute-done((bf16[384,1536]{1,0:T(8,128)(2,1)S(1)}, bf16[384,1536]{1,0:T(8,128)(2,1)S(1)}, u32[]{:S(2)}, u32[]{:S(2)}) %collective-permute-start.9) | collective-permute-done | bytes 1179680 | tf_op jit(solution)/shard_map/ppermute | solution.py:383
  527.0 12.6 %collective-permute-done.10 = bf16[384,1536]{1,0:T(8,128)(2,1)S(1)} collective-permute-done((bf16[384,1536]{1,0:T(8,128)(2,1)S(1)}, bf16[384,1536]{1,0:T(8,128)(2,1)S(1)}, u32[]{:S(2)}, u32[]{:S(2)}) %collective-permute-start.10) | collective-permute-done | bytes 1179680 | tf_op jit(solution)/shard_map/ppermute | solution.py:383
  582.5 17.6 %head_grads.1 = bf16[7168,768]{1,0:T(8,128)(2,1)} custom-call(s32[3]{0:T(128)S(1)} %broadcast_select_fusion.8.refs_0_, bf16[7168,384]{1,0:T(8,128)(2,1)S(1)} %copy-done.6, bf16[7168,384]{1,0:T(8,128)(2,1)S(1)} %copy-done.5, bf16[7168,384]{1,0:T(8,128)(2,1)} %get-tuple-element.76.refs_3_, bf16[3,384,768]{2,1,0:T(8,128)(2,1)S(1)} %pad_maximum_fusion.6.refs_4_), custom_call_target="tpu_custom_call" | custom-call | flops 12683575296 | bytes 22020096 | tf_op jit(solution)/shard_map/head_grads/pallas_call | solution.py:344
  621.7 18.7 %attend_backward.4 = (bf16[4,320,384]{2,1,0:T(8,128)(2,1)}, f32[64,3072]{1,0:T(8,128)S(1)}, f32[8,128]{1,0:T(8,128)S(1)}) custom-call(bf16[1536,384]{1,0:T(8,128)(2,1)S(1)} %bitcast.333, bf16[3072,64]{1,0:T(8,128)(2,1)S(1)} %copy-done.15, bf16[1536,1536]{1,0:T(8,128)(2,1)} %get-tuple-element.64.refs_2_, bf16[4,192,384]{2,1,0:T(8,128)(2,1)} %bitcast.52.refs_3_), custom_call_target="tpu_custom_call" | custom-call | flops 9663676416 | bytes 4718592 | tf_op jit(solution)/shard_map/attend_backward/pallas_call | solution.py:165
  655.8 18.7 %attend_backward.5 = (bf16[4,320,384]{2,1,0:T(8,128)(2,1)}, f32[64,3072]{1,0:T(8,128)S(1)}, f32[8,128]{1,0:T(8,128)S(1)}) custom-call(bf16[1536,384]{1,0:T(8,128)(2,1)S(1)} %bitcast.329, bf16[3072,64]{1,0:T(8,128)(2,1)S(1)} %copy-done.15, bf16[1536,1536]{1,0:T(8,128)(2,1)} %get-tuple-element.66.refs_2_, bf16[4,192,384]{2,1,0:T(8,128)(2,1)} %bitcast.60.refs_3_), custom_call_target="tpu_custom_call" | custom-call | flops 9663676416 | bytes 4718592 | tf_op jit(solution)/shard_map/attend_backward/pallas_call | solution.py:165
  685.8 9.9 pad_maximum_fusion
  695.7 24.1 %reshape.549 = bf16[2,2,384,3840]{2,1,0,3:T(2,128)(2,1)} reshape(bf16[1536,3840]{0,1:T(8,128)(2,1)} %pad_maximum_fusion) | data formatting | bytes 23592960 | tf_op jit(solution)/shard_map/reshape | solution.py:437
  719.8 18.7 %attend_backward.3 = (bf16[4,320,384]{2,1,0:T(8,128)(2,1)}, f32[64,3072]{1,0:T(8,128)S(1)}, f32[8,128]{1,0:T(8,128)S(1)}) custom-call(bf16[1536,384]{1,0:T(8,128)(2,1)S(1)} %bitcast.331, bf16[3072,64]{1,0:T(8,128)(2,1)S(1)} %copy-done.15, bf16[1536,1536]{1,0:T(8,128)(2,1)} %get-tuple-element.62.refs_2_, bf16[4,192,384]{2,1,0:T(8,128)(2,1)S(1)} %bitcast.334), custom_call_target="tpu_custom_call" | custom-call | flops 9663676416 | bytes 4718592 | tf_op jit(solution)/shard_map/attend_backward/pallas_call | solution.py:165
  744.8 27.7 %constant_dynamic-slice_fusion.2 = (bf16[2,1,384,3840]{2,1,0,3:T(2,128)(2,1)}, bf16[2,1,384,3840]{2,1,0,3:T(2,128)(2,1)}) fusion(bf16[2,2,384,3840]{2,1,0,3:T(2,128)(2,1)} %reshape.549, s32[]{:T(128)S(6)} %select_n.205, s32[]{:T(128)S(6)} %select_n.206), kind=kLoop, calls=%fused_computation.320 | loop fusion | bytes 23592968 | tf_op jit(solution)/shard_map/jit(dynamic_index_in_dim)/dynamic_slice | solution.py:438
  775.6 23.7 %copy.210 = bf16[2,1,384,3840]{3,2,0,1:T(8,128)(2,1)} copy(bf16[2,1,384,3840]{2,1,0,3:T(2,128)(2,1)} %get-tuple-element.249) | data formatting | bytes 11796480
  799.3 23.8 %copy.211 = bf16[2,1,384,3840]{3,2,0,1:T(8,128)(2,1)} copy(bf16[2,1,384,3840]{2,1,0,3:T(2,128)(2,1)} %get-tuple-element.250) | data formatting | bytes 11796480
  844.4 21.6 %collective-permute-done.16 = bf16[384,1536]{1,0:T(8,128)(2,1)} collective-permute-done((bf16[384,1536]{1,0:T(8,128)(2,1)}, bf16[384,1536]{1,0:T(8,128)(2,1)}, u32[]{:S(2)}, u32[]{:S(2)}) %collective-permute-start.16) | collective-permute-done | bytes 1179680 | tf_op jit(solution)/shard_map/ppermute | solution.py:383
  866.1 25.3 %collective-permute-done.17 = bf16[384,1536]{1,0:T(8,128)(2,1)} collective-permute-done((bf16[384,1536]{1,0:T(8,128)(2,1)}, bf16[384,1536]{1,0:T(8,128)(2,1)}, u32[]{:S(2)}, u32[]{:S(2)}) %collective-permute-start.17) | collective-permute-done | bytes 1179680 | tf_op jit(solution)/shard_map/ppermute | solution.py:383
  891.3 25.0 %collective-permute-done.18 = bf16[384,1536]{1,0:T(8,128)(2,1)} collective-permute-done((bf16[384,1536]{1,0:T(8,128)(2,1)S(1)}, bf16[384,1536]{1,0:T(8,128)(2,1)}, u32[]{:S(2)}, u32[]{:S(2)}) %collective-permute-start.18) | collective-permute-done | bytes 1179680 | tf_op jit(solution)/shard_map/ppermute | solution.py:383
  963.8 12.9 %convert_element_type.497 = f32[7168,768]{1,0:T(8,128)} convert(bf16[7168,768]{1,0:T(8,128)(2,1)} %all-reduce.6.cloned.1.call-done) | non-fusion elementwise | flops 5505024 | bytes 33030144 | tf_op jit(solution)/shard_map/convert_element_type | solution.py:665
  990.9 11.3 slice_bitcast_fusion
  1011.7 50.8 %collective-permute-done.29 = bf16[1,384,3840]{2,1,0:T(8,128)(2,1)} collective-permute-done((bf16[1,384,3840]{2,1,0:T(8,128)(2,1)}, bf16[1,384,3840]{2,1,0:T(8,128)(2,1)}, u32[]{:S(2)}, u32[]{:S(2)}) %collective-permute-start.29) | collective-permute-done | bytes 2949152 | tf_op jit(solution)/shard_map/ppermute | solution.py:440
  1073.9 14.5 %collective-permute-done.30 = bf16[96,3840]{1,0:T(8,128)(2,1)} collective-permute-done((bf16[96,3840]{1,0:T(8,128)(2,1)}, bf16[96,3840]{1,0:T(8,128)(2,1)}, u32[]{:S(2)}, u32[]{:S(2)}) %collective-permute-start.30) | collective-permute-done | bytes 737312 | tf_op jit(solution)/shard_map/ppermute | solution.py:451
  1097.2 14.9 %collective-permute-done.31 = bf16[96,3840]{1,0:T(8,128)(2,1)} collective-permute-done((bf16[96,3840]{1,0:T(8,128)(2,1)}, bf16[96,3840]{1,0:T(8,128)(2,1)}, u32[]{:S(2)}, u32[]{:S(2)}) %collective-permute-start.31) | collective-permute-done | bytes 737312 | tf_op jit(solution)/shard_map/ppermute | solution.py:451
  (613 shorter events, 462.6 us)
Async XLA Ops:
  7.2 237.5 %all-gather.4.cloned.1.call-start = ((), (), s32[]{:S(2)}) async-start(), calls=%async_computation.12 | async-start | bytes 2506752 | tf_op jit(solution)/shard_map/all_gather | solution.py:412
  34.4 43.4 %all-to-all-start.4 = ((bf16[4,1,384,384]{3,2,1,0:T(8,128)(2,1)}), bf16[4,1,384,384]{3,2,1,0:T(8,128)(2,1)S(1)}, u32[]{:S(2)}, u32[]{:S(2)}) async-start(bf16[4,1,384,384]{3,2,1,0:T(8,128)(2,1)} %bitcast.325), calls=%async_computation.4 | async-start | bytes 2359296 | tf_op jit(solution)/shard_map/all_to_all | solution.py:518
  39.4 323.3 %all-gather.8.cloned.1.call-start = ((), (), s32[]{:S(2)}) async-start(), calls=%async_computation.14 | async-start | bytes 2924544 | tf_op jit(solution)/shard_map/all_gather | solution.py:412
  77.8 37.4 %all-to-all-start = ((bf16[4,1,384,384]{3,2,1,0:T(8,128)(2,1)}), bf16[4,1,384,384]{3,2,1,0:T(8,128)(2,1)S(1)}, u32[]{:S(2)}, u32[]{:S(2)}) async-start(bf16[4,1,384,384]{3,2,1,0:T(8,128)(2,1)} %bitcast.327), calls=%async_computation | async-start | bytes 2359296 | tf_op jit(solution)/shard_map/all_to_all | solution.py:518
  115.2 40.3 %all-to-all-start.2 = ((bf16[4,1,384,384]{3,2,1,0:T(8,128)(2,1)}), bf16[4,1,384,384]{3,2,1,0:T(8,128)(2,1)S(1)}, u32[]{:S(2)}, u32[]{:S(2)}) async-start(bf16[4,1,384,384]{3,2,1,0:T(8,128)(2,1)} %bitcast.363), calls=%async_computation.2 | async-start | bytes 2359296 | tf_op jit(solution)/shard_map/all_to_all | solution.py:518
  180.2 182.5 %all-gather.6.cloned.1.call-start = ((), (), s32[]{:S(2)}) async-start(), calls=%async_computation.13 | async-start | bytes 8773632 | tf_op jit(solution)/shard_map/all_gather | solution.py:412
  195.7 30.5 %all-to-all-start.5 = ((bf16[4,1,192,384]{3,2,1,0:T(8,128)(2,1)}), bf16[4,1,192,384]{3,2,1,0:T(8,128)(2,1)}, u32[]{:S(2)}, u32[]{:S(2)}) async-start(bf16[4,1,192,384]{3,2,1,0:T(8,128)(2,1)} %bitcast.25), calls=%async_computation.5 | async-start | bytes 1179648 | tf_op jit(solution)/shard_map/all_to_all | solution.py:518
  200.4 27.3 %collective-permute-start = (bf16[768,384]{1,0:T(8,128)(2,1)}, bf16[768,384]{1,0:T(8,128)(2,1)S(1)}, u32[]{:S(2)}, u32[]{:S(2)}) collective-permute-start(bf16[768,384]{1,0:T(8,128)(2,1)} %bitcast.12), channel_id=1, source_target_pairs={{0,1},{1,0},{2,3},{3,2},{4,5},{5,4},{6,7},{7,6},{8,9},{9,8},{10,11... | collective-permute-start | bytes 1769480 | tf_op jit(solution)/shard_map/ppermute | solution.py:391
  201.9 27.9 %collective-permute-start.3 = (bf16[768,384]{1,0:T(8,128)(2,1)}, bf16[768,384]{1,0:T(8,128)(2,1)}, u32[]{:S(2)}, u32[]{:S(2)}) collective-permute-start(bf16[768,384]{1,0:T(8,128)(2,1)} %bitcast.19), channel_id=1, source_target_pairs={{0,1},{1,0},{2,3},{3,2},{4,5},{5,4},{6,7},{7,6},{8,9},{9,8},{10,11... | collective-permute-start | bytes 1769480 | tf_op jit(solution)/shard_map/ppermute | solution.py:391
  268.5 29.3 %collective-permute-start.2 = (bf16[384,1536]{1,0:T(8,128)(2,1)}, bf16[384,1536]{1,0:T(8,128)(2,1)}, u32[]{:S(2)}, u32[]{:S(2)}) collective-permute-start(bf16[384,1536]{1,0:T(8,128)(2,1)} %convolution_convert_fusion.9), channel_id=1, source_target_pairs={{0,1},{1,0},{2,3},{3,2},{4,5},{5,4},{6,7},{7,6},{8,9},{9,8},{10,11... | collective-permute-start | bytes 3538952 | tf_op jit(solution)/shard_map/ppermute | solution.py:383
  276.5 46.6 %collective-permute-start.4 = (bf16[384,1536]{1,0:T(8,128)(2,1)}, bf16[384,1536]{1,0:T(8,128)(2,1)}, u32[]{:S(2)}, u32[]{:S(2)}) collective-permute-start(bf16[384,1536]{1,0:T(8,128)(2,1)} %convolution_convert_fusion.8), channel_id=1, source_target_pairs={{0,1},{1,0},{2,3},{3,2},{4,5},{5,4},{6,7},{7,6},{8,9},{9,8},{10,11... | collective-permute-start | bytes 3538952 | tf_op jit(solution)/shard_map/ppermute | solution.py:383
  283.5 62.7 %collective-permute-start.6 = (bf16[384,1536]{1,0:T(8,128)(2,1)}, bf16[384,1536]{1,0:T(8,128)(2,1)}, u32[]{:S(2)}, u32[]{:S(2)}) collective-permute-start(bf16[384,1536]{1,0:T(8,128)(2,1)} %convolution_convert_fusion.7), channel_id=1, source_target_pairs={{0,1},{1,0},{2,3},{3,2},{4,5},{5,4},{6,7},{7,6},{8,9},{9,8},{10,11... | collective-permute-start | bytes 3538952 | tf_op jit(solution)/shard_map/ppermute | solution.py:383
  411.3 104.2 %collective-permute-start.11 = (bf16[384,1536]{1,0:T(8,128)(2,1)S(1)}, bf16[384,1536]{1,0:T(8,128)(2,1)S(1)}, u32[]{:S(2)}, u32[]{:S(2)}) collective-permute-start(bf16[384,1536]{1,0:T(8,128)(2,1)S(1)} %convolution_convert_fusion.4), channel_id=1, source_target_pairs={{0,1},{1,0},{2,3},{3,2},{4,5},{5,4},{6,7},{7,6},{8,9},{9,8},{10,11... | collective-permute-start | bytes 3538952 | tf_op jit(solution)/shard_map/ppermute | solution.py:383
  503.8 23.2 %collective-permute-start.9 = (bf16[384,1536]{1,0:T(8,128)(2,1)S(1)}, bf16[384,1536]{1,0:T(8,128)(2,1)S(1)}, u32[]{:S(2)}, u32[]{:S(2)}) collective-permute-start(bf16[384,1536]{1,0:T(8,128)(2,1)S(1)} %convolution_convert_fusion.6), channel_id=1, source_target_pairs={{0,1},{1,0},{2,3},{3,2},{4,5},{5,4},{6,7},{7,6},{8,9},{9,8},{10,11... | collective-permute-start | bytes 3538952 | tf_op jit(solution)/shard_map/ppermute | solution.py:383
  504.4 35.3 %collective-permute-start.10 = (bf16[384,1536]{1,0:T(8,128)(2,1)S(1)}, bf16[384,1536]{1,0:T(8,128)(2,1)S(1)}, u32[]{:S(2)}, u32[]{:S(2)}) collective-permute-start(bf16[384,1536]{1,0:T(8,128)(2,1)S(1)} %convolution_convert_fusion.5), channel_id=1, source_target_pairs={{0,1},{1,0},{2,3},{3,2},{4,5},{5,4},{6,7},{7,6},{8,9},{9,8},{10,11... | collective-permute-start | bytes 3538952 | tf_op jit(solution)/shard_map/ppermute | solution.py:383
  572.8 43.9 %all-to-all-start.8 = ((bf16[4,1,192,384]{3,2,1,0:T(8,128)(2,1)}), bf16[4,1,192,384]{3,2,1,0:T(8,128)(2,1)}, u32[]{:S(2)}, u32[]{:S(2)}) async-start(bf16[4,1,192,384]{3,2,1,0:T(8,128)(2,1)} %bitcast.372), calls=%async_computation.8 | async-start | bytes 1179648 | tf_op jit(solution)/shard_map/all_to_all | solution.py:518
  577.3 386.4 %all-reduce.6.cloned.1.call-start = ((), (), s32[]{:S(2)}) async-start(), calls=%async_computation.15 | async-start | bytes 22020096 | tf_op jit(solution)/shard_map/psum | solution.py:665
  616.7 27.5 %all-to-all-start.10 = ((bf16[4,1,192,384]{3,2,1,0:T(8,128)(2,1)}), bf16[4,1,192,384]{3,2,1,0:T(8,128)(2,1)}, u32[]{:S(2)}, u32[]{:S(2)}) async-start(bf16[4,1,192,384]{3,2,1,0:T(8,128)(2,1)} %bitcast.59), calls=%async_computation.10 | async-start | bytes 1179648 | tf_op jit(solution)/shard_map/all_to_all | solution.py:518
  644.2 36.1 %all-to-all-start.9 = ((bf16[4,1,320,384]{3,2,1,0:T(8,128)(2,1)}), bf16[4,1,320,384]{3,2,1,0:T(8,128)(2,1)S(1)}, u32[]{:S(2)}, u32[]{:S(2)}) async-start(bf16[4,1,320,384]{3,2,1,0:T(8,128)(2,1)} %bitcast.54), calls=%async_computation.9 | async-start | bytes 1966080 | tf_op jit(solution)/shard_map/all_to_all | solution.py:518
  680.3 59.1 %all-to-all-start.11 = ((bf16[4,1,320,384]{3,2,1,0:T(8,128)(2,1)}), bf16[4,1,320,384]{3,2,1,0:T(8,128)(2,1)}, u32[]{:S(2)}, u32[]{:S(2)}) async-start(bf16[4,1,320,384]{3,2,1,0:T(8,128)(2,1)} %bitcast.62), calls=%async_computation.11 | async-start | bytes 1966080 | tf_op jit(solution)/shard_map/all_to_all | solution.py:518
  739.3 92.2 %all-to-all-start.7 = ((bf16[4,1,320,384]{3,2,1,0:T(8,128)(2,1)}), bf16[4,1,320,384]{3,2,1,0:T(8,128)(2,1)}, u32[]{:S(2)}, u32[]{:S(2)}) async-start(bf16[4,1,320,384]{3,2,1,0:T(8,128)(2,1)} %bitcast.45), calls=%async_computation.7 | async-start | bytes 1966080 | tf_op jit(solution)/shard_map/all_to_all | solution.py:518
  823.1 156.6 %collective-permute-start.28 = (bf16[2,384,3840]{2,1,0:T(8,128)(2,1)}, bf16[2,384,3840]{2,1,0:T(8,128)(2,1)}, u32[]{:S(2)}, u32[]{:S(2)}) collective-permute-start(bf16[2,384,3840]{2,1,0:T(8,128)(2,1)} %bitcast.359), channel_id=1, source_target_pairs={{0,8},{8,0},{16,24},{24,16},{1,9},{9,1},{17,25},{25,17},{2,10},{10... | collective-permute-start | bytes 17694728 | tf_op jit(solution)/shard_map/ppermute | solution.py:440
  836.9 29.2 %collective-permute-start.16 = (bf16[384,1536]{1,0:T(8,128)(2,1)}, bf16[384,1536]{1,0:T(8,128)(2,1)}, u32[]{:S(2)}, u32[]{:S(2)}) collective-permute-start(bf16[384,1536]{1,0:T(8,128)(2,1)} %convolution_convert_fusion.12), channel_id=1, source_target_pairs={{0,1},{1,0},{2,3},{3,2},{4,5},{5,4},{6,7},{7,6},{8,9},{9,8},{10,11... | collective-permute-start | bytes 3538952 | tf_op jit(solution)/shard_map/ppermute | solution.py:383
  836.9 54.4 %collective-permute-start.17 = (bf16[384,1536]{1,0:T(8,128)(2,1)}, bf16[384,1536]{1,0:T(8,128)(2,1)}, u32[]{:S(2)}, u32[]{:S(2)}) collective-permute-start(bf16[384,1536]{1,0:T(8,128)(2,1)} %convolution_convert_fusion.11), channel_id=1, source_target_pairs={{0,1},{1,0},{2,3},{3,2},{4,5},{5,4},{6,7},{7,6},{8,9},{9,8},{10,11... | collective-permute-start | bytes 3538952 | tf_op jit(solution)/shard_map/ppermute | solution.py:383
  838.9 77.5 %collective-permute-start.18 = (bf16[384,1536]{1,0:T(8,128)(2,1)S(1)}, bf16[384,1536]{1,0:T(8,128)(2,1)}, u32[]{:S(2)}, u32[]{:S(2)}) collective-permute-start(bf16[384,1536]{1,0:T(8,128)(2,1)S(1)} %convolution_convert_fusion.10), channel_id=1, source_target_pairs={{0,1},{1,0},{2,3},{3,2},{4,5},{5,4},{6,7},{7,6},{8,9},{9,8},{10,11... | collective-permute-start | bytes 3538952 | tf_op jit(solution)/shard_map/ppermute | solution.py:383
  937.8 38.9 %collective-permute-start.23 = (bf16[2,384,1280]{2,1,0:T(8,128)(2,1)S(1)}, bf16[2,384,1280]{2,1,0:T(8,128)(2,1)}, u32[]{:S(2)}, u32[]{:S(2)}) collective-permute-start(bf16[2,384,1280]{2,1,0:T(8,128)(2,1)S(1)} %dynamic-slice_bitcast_fusion), channel_id=1, source_target_pairs={{0,8},{8,0},{16,24},{24,16},{1,9},{9,1},{17,25},{25,17},{2,10},{10... | collective-permute-start | bytes 5898248 | tf_op jit(solution)/shard_map/ppermute | solution.py:440
  962.4 45.0 %collective-permute-start.22 = (f32[412,128]{1,0:T(8,128)S(1)}, f32[412,128]{1,0:T(8,128)}, u32[]{:S(2)}, u32[]{:S(2)}) collective-permute-start(f32[412,128]{1,0:T(8,128)S(1)} %add.695), channel_id=1, source_target_pairs={{0,4},{2,6},{4,0},{6,2},{1,5},{3,7},{5,1},{7,3},{8,12},{10,14},{12... | collective-permute-start | bytes 632840 | tf_op jit(solution)/shard_map/ppermute | solution.py:423
  979.8 29.4 %collective-permute-start.24 = (bf16[1,384,1280]{2,1,0:T(8,128)(2,1)}, bf16[1,384,1280]{2,1,0:T(8,128)(2,1)S(1)}, u32[]{:S(2)}, u32[]{:S(2)}) collective-permute-start(bf16[1,384,1280]{2,1,0:T(8,128)(2,1)} %constant_dynamic-slice_fusion.9), channel_id=1, source_target_pairs={{0,16},{8,24},{16,0},{24,8},{1,17},{9,25},{17,1},{25,9},{2,18},{10... | collective-permute-start | bytes 2949128 | tf_op jit(solution)/shard_map/ppermute | solution.py:440
  988.9 73.6 %collective-permute-start.29 = (bf16[1,384,3840]{2,1,0:T(8,128)(2,1)}, bf16[1,384,3840]{2,1,0:T(8,128)(2,1)}, u32[]{:S(2)}, u32[]{:S(2)}) collective-permute-start(bf16[1,384,3840]{2,1,0:T(8,128)(2,1)} %constant_dynamic-slice_fusion), channel_id=1, source_target_pairs={{0,16},{8,24},{16,0},{24,8},{1,17},{9,25},{17,1},{25,9},{2,18},{10... | collective-permute-start | bytes 8847368 | tf_op jit(solution)/shard_map/ppermute | solution.py:440
  1011.2 59.1 %collective-permute-start.25 = (bf16[96,1280]{0,1:T(8,128)(2,1)}, bf16[96,1280]{0,1:T(8,128)(2,1)}, u32[]{:S(2)}, u32[]{:S(2)}) collective-permute-start(bf16[96,1280]{0,1:T(8,128)(2,1)} %bitcast.72), channel_id=1, source_target_pairs={{0,2},{2,4},{4,6},{6,0},{1,3},{3,5},{5,7},{7,1},{8,10},{10,12},{12... | collective-permute-start | bytes 737288 | tf_op jit(solution)/shard_map/ppermute | solution.py:451
  1072.1 23.3 %collective-permute-start.26 = (bf16[96,1280]{0,1:T(8,128)(2,1)}, bf16[96,1280]{0,1:T(8,128)(2,1)}, u32[]{:S(2)}, u32[]{:S(2)}) collective-permute-start(bf16[96,1280]{0,1:T(8,128)(2,1)} %fusion.169), channel_id=1, source_target_pairs={{0,2},{2,4},{4,6},{6,0},{1,3},{3,5},{5,7},{7,1},{8,10},{10,12},{12... | collective-permute-start | bytes 737288 | tf_op jit(solution)/shard_map/ppermute | solution.py:451
  1097.2 21.9 %collective-permute-start.27 = (bf16[96,1280]{0,1:T(8,128)(2,1)}, bf16[96,1280]{0,1:T(8,128)(2,1)}, u32[]{:S(2)}, u32[]{:S(2)}) collective-permute-start(bf16[96,1280]{0,1:T(8,128)(2,1)} %fusion.168), channel_id=1, source_target_pairs={{0,2},{2,4},{4,6},{6,0},{1,3},{3,5},{5,7},{7,1},{8,10},{10,12},{12... | collective-permute-start | bytes 737288 | tf_op jit(solution)/shard_map/ppermute | solution.py:451
  (176 other events, 2441.7 us)
Sparse Core Ops, SparseCore 0:
  22.6 54.9 all-gather.3
  79.9 62.2 all-gather.7
  183.3 86.5 all-gather.5
  603.4 271.7 all-reduce.5

commit v2 on v1

--- a/solution.py
+++ b/solution.py
@@ -425,34 +425,40 @@
     return vector
 
 
-def scatter_sum(full):
+def scatter_product(left, right):
     dp_size, seq_size = lax.axis_size("dp"), lax.axis_size("seq")
     dp_index, seq_index = lax.axis_index("dp"), lax.axis_index("seq")
-    rows = full.shape[0] // (dp_size * seq_size)
-    cols = full.shape[1]
-    kept = full.astype(jnp.bfloat16)
-    step = 1
-    while step < dp_size:
-        bit = (dp_index // step) % 2
-        split = kept.reshape(-1, 2, seq_size * rows, cols)
-        mine = lax.dynamic_index_in_dim(split, bit, 1, keepdims=False)
-        theirs = lax.dynamic_index_in_dim(split, 1 - bit, 1, keepdims=False)
-        got = lax.ppermute(theirs, "dp", swap_pairs("dp", step))
-        kept = (mine.astype(jnp.float32) + got.astype(jnp.float32)).astype(jnp.bfloat16)
-        step *= 2
-    parts = kept.reshape(seq_size, rows, cols)
-
-    def part(index):
-        return lax.dynamic_index_in_dim(parts, index % seq_size, 0, keepdims=False)
-
-    ring = [(i, (i + 1) % seq_size) for i in range(seq_size)]
-    moving = part(seq_index - 1 + seq_size)
-    for step in range(seq_size - 1):
-        got = lax.ppermute(moving, "seq", ring)
-        total = got.astype(jnp.float32) + part(seq_index - 2 - step + 2 * seq_size).astype(
-            jnp.float32
-        )
-        moving = total.astype(jnp.bfloat16)
+    width = left.shape[1]
+    slab = width // dp_size
+    rows = slab // seq_size
+
+    def half(parity):
+        return jnp.concatenate(
+            [left[:, i * slab : (i + 1) * slab] for i in range(parity, dp_size, 2)], axis=1
+        )
+
+    even = dp_index % 2 == 0
+    kept, sent = jnp.where(even, half(0), half(1)), jnp.where(even, half(1), half(0))
+    got = lax.ppermute(mxu(sent, right, TN).astype(jnp.bfloat16), "dp", swap_pairs("dp", 1))
+    kept = mxu(kept, right, TN) + got.astype(jnp.float32)
+    step = dp_size
+    while step > 2:
+        step //= 2
+        size = kept.shape[0] // 2
+        upper = (dp_index // step) % 2 == 1
+        low, high = kept[:size], kept[size:]
+        got = lax.ppermute(
+            jnp.where(upper, low, high).astype(jnp.bfloat16), "dp", swap_pairs("dp", step)
+        )
+        kept = jnp.where(upper, high, low) + got.astype(jnp.float32)
+    parts = kept.astype(jnp.bfloat16).reshape(seq_size, rows, -1)
+    total = lax.dynamic_index_in_dim(parts, seq_index, 0, keepdims=False).astype(jnp.float32)
+    for step in range(1, seq_size):
+        other = seq_index ^ step
+        got = lax.ppermute(
+            lax.dynamic_index_in_dim(parts, other, 0, keepdims=False), "seq", swap_pairs("seq", step)
+        )
+        total = total + got.astype(jnp.float32)
     return total
 
 
@@ -515,7 +521,13 @@
         return exchange(array.reshape((seq_size, pairs_here) + array.shape[1:]))
 
     def exchange(array):
-        return lax.all_to_all(array, "seq", split_axis=0, concat_axis=0, tiled=True)
+        result = array
+        for step in range(1, seq_size):
+            other = seq_index ^ step
+            block_out = lax.dynamic_index_in_dim(array, other, 0, keepdims=True)
+            block_in = lax.ppermute(block_out, "seq", swap_pairs("seq", step))
+            result = lax.dynamic_update_slice_in_dim(result, block_in, other, 0)
+        return result
 
     def bins_last(array):
         if bins == block:
@@ -662,7 +674,7 @@
         [lax.dynamic_slice_in_dim(rows, mp_index * share, share, 1) for rows in low_windows]
     )
     dheads = head_grads(picks, logit_grads, own_rows, tiles_human)
-    dheads = lax.psum(dheads, ("dp", "seq")).astype(jnp.float32)
+    dheads = lax.psum(dheads, ("dp", "seq"))
     dtracks = sum(track_sums)[:, 0]
 
     grad_mids, grad_outs, grad_pres, grad_mid_lows, packed_grads = [], [], [], [], []
@@ -707,20 +719,9 @@
         packed_grads.append(collect(outs).reshape(heads * GRAD_PACK, group_size * bins))
 
     join = lambda arrays: jnp.concatenate(arrays, axis=0)
-    dtrunk_weights = jnp.concatenate(
-        [
-            mxu(join(normed2), join(grad_pres), TN).astype(bf16),
-            mxu(join(grad_outs), join(actives), TN).astype(bf16),
-            lax.dot_general(
-                join(grad_mid_lows),
-                jnp.concatenate(attended, axis=1),
-                (((0,), (1,)), ((), ())),
-                preferred_element_type=jnp.float32,
-            ).astype(bf16),
-        ],
-        axis=1,
-    )
-    trunk_summed = scatter_sum(dtrunk_weights)
+    dw_in = scatter_product(join(normed2), join(grad_pres))
+    dw_hid = scatter_product(join(grad_outs), join(actives))
+    dw_out = scatter_product(join(grad_mid_lows), jnp.concatenate(attended, axis=1).T)
 
     grad_inputs = []
     sums1 = [0.0, 0.0]
@@ -739,13 +740,8 @@
         )
         sums1 = [sums1[0] + dgain, sums1[1] + dbias]
         grad_inputs.append((grad_mids[g] + grad_norm).reshape(group_size, bins, width))
-    dpack = lax.dot_general(
-        join(normed1),
-        jnp.concatenate(packed_grads, axis=1),
-        (((0,), (1,)), ((), ())),
-        preferred_element_type=jnp.float32,
-    ).astype(bf16)
-    pack_summed = scatter_sum(dpack).reshape(-1, heads, GRAD_PACK)
+    pack_summed = scatter_product(join(normed1), jnp.concatenate(packed_grads, axis=1).T)
+    pack_summed = pack_summed.reshape(-1, heads, GRAD_PACK)
 
     dw_rel = jnp.zeros((heads, FEAT, KD), jnp.float32)
     dstat = jnp.zeros((heads, 2, KD), jnp.float32)
@@ -782,8 +778,8 @@
         return lax.dynamic_slice_in_dim(array, place * size, size, dim)
 
     rel_rows = own(dw_rel, 1).transpose(1, 0, 2).reshape(-1, heads * KD)
-    hidden = w_in.shape[1]
     pack_rows = pack_summed.shape[0]
+    mouse_start = tiles_human * TILE
     shape3 = (windows, bins, width)
     return (
         join(trunk_out).reshape(shape3),
@@ -797,18 +793,18 @@
         rel_rows,
         own(dstat[:, 0], 1),
         own(dstat[:, 1], 1),
-        trunk_summed[:, 2 * hidden :].T,
+        dw_out.T,
         own(db_out),
         own(dgain2),
         own(dbias2),
-        trunk_summed[:, :hidden],
+        dw_in,
         db_in,
-        trunk_summed[:, hidden : 2 * hidden].T,
+        dw_hid.T,
         own(db_hid),
-        dheads[:track_human].T,
+        dheads[:track_human].astype(jnp.float32).T,
         dtracks[:track_human],
-        dheads[tiles_human * TILE : tiles_human * TILE + track_mouse].T,
-        dtracks[tiles_human * TILE : tiles_human * TILE + track_mouse],
+        dheads[mouse_start : mouse_start + track_mouse].astype(jnp.float32).T,
+        dtracks[mouse_start : mouse_start + track_mouse],
     )
 
 

time: 1150 us -> 995 us (0.87)
  local copies, waits for them, and re-layouts: 207 us -> 115 us
  waiting for transfers between devices: 362 us -> 302 us
  starting transfers between devices: 84.2 us -> 127 us
  matrix products: 126 us -> 108 us
  other arithmetic: 145 us -> 128 us
    all_to_all x12 -> x0, waiting for transfers between devices: 108 us -> none  [exchange(): return lax.all_to_all(array, 'seq', split_axis=0, concat_axis=0, tiled=True)]
    ppermute x10 -> x56, starting transfers between devices: 5.63 us -> 101 us  [the longest x36 75.9 us: exchange(): block_in = lax.ppermute(block_out, 'seq', swap_pairs('seq', step))]
    all_to_all x12 -> x0, starting transfers between devices: 54 us -> none  [exchange(): return lax.all_to_all(array, 'seq', split_axis=0, concat_axis=0, tiled=True)]
    ppermute x10 -> x56, waiting for transfers between devices: 86.1 us -> 137 us  [the longest x36 69.9 us: exchange(): block_in = lax.ppermute(block_out, 'seq', swap_pairs('seq', step))]
    unnamed x330 -> x425, local copies, waits for them, and re-layouts: 88.5 us -> 43.2 us
    reshape x1 -> x0, local copies, waits for them, and re-layouts: 24.1 us -> none  [scatter_sum(): split = kept.reshape(-1, 2, seq_size * rows, cols)]
    convert_element_type x9 -> x8, other arithmetic: 32.2 us -> 9 us  [the longest x4 5.42 us: scatter_product(): parts = kept.astype(jnp.bfloat16).reshape(seq_size, rows, -1)]
    dynamic_slice x3 -> x12, local copies, waits for them, and re-layouts: 29.4 us -> 10.9 us  [exchange(): block_out = lax.dynamic_index_in_dim(array, other, 0, keepdims=True)]
  transfers between devices with their start and end apart: 49 -> 83, of which waited for: 27 -> 32; matrix products, arithmetic and copies ran while one was open for 37% -> 30% of each run, Pallas kernels for 14% -> 9%
where the time goes in v2:
time: 995 us; the launch traced here: 993 us
  waiting for transfers between devices  302 us (30%)
  Pallas kernels  193 us (19%)
  other arithmetic  128 us (13%)
  starting transfers between devices  127 us (13%)
  local copies, waits for them, and re-layouts  115 us (12%)
  matrix products  108 us (11%)
  between operations  19 us (2%)
    ppermute x9, waiting for transfers between devices, sum_over_model(): other = lax.ppermute(low, 'mp', [(0, 1), (1, 0)])  131 us
    dot_general x30, matrix products, mxu(): lax.dot_general(left_arr, right_arr, dims, precision=precision, preferred...  98.8 us
    pallas_call x3, Pallas kernels, score_heads(): pl.pallas_call(lambda *refs: heads_kernel(track_human, track_mouse, tiles...  90.9 us
    ppermute x36, starting transfers between devices, exchange(): block_in = lax.ppermute(block_out, 'seq', swap_pairs('seq', step))  75.9 us
    ppermute x36, waiting for transfers between devices, exchange(): block_in = lax.ppermute(block_out, 'seq', swap_pairs('seq', step))  69.9 us
    ppermute x12, waiting for transfers between devices, scatter_product(): lax.ppermute(lax.dynamic_index_in_dim(parts, other, 0, keepdims=False), '...  55.1 us
    pallas_call x3, Pallas kernels, attend_backward(): pl.pallas_call(lambda *refs: attend_backward_kernel(block, bins, *refs),...  54.2 us
    unnamed x425, local copies, waits for them, and re-layouts  43.2 us
  transfers between devices with their start and end apart: 83, of which 32 were waited for; matrix products, arithmetic and copies ran while one was open for 30% of the time, Pallas kernels for 9%

profile of v2, /device:TPU:0, one launch (start us, length us, event | category | flops | bytes accessed | tf_op | source)
XLA Modules:
  0.0 992.5 jit_solution(10762527833804939646)
XLA Ops:
  98.8 10.2 %attend_forward.4 = (bf16[4,192,384]{2,1,0:T(8,128)(2,1)S(1)}, bf16[1536,1536]{1,0:T(8,128)(2,1)}) custom-call(bf16[1536,384]{1,0:T(8,128)(2,1)S(1)} %bitcast.403, bf16[3072,64]{1,0:T(8,128)(2,1)S(1)} %copy-done.29), custom_call_target="tpu_custom_call" | custom-call | flops 4831838208 | bytes 4718592 | tf_op jit(solution)/shard_map/attend_forward/pallas_call | solution.py:84
  113.1 10.3 %attend_forward.5 = (bf16[4,192,384]{2,1,0:T(8,128)(2,1)S(1)}, bf16[1536,1536]{1,0:T(8,128)(2,1)}) custom-call(bf16[1536,384]{1,0:T(8,128)(2,1)S(1)} %bitcast.406, bf16[3072,64]{1,0:T(8,128)(2,1)S(1)} %copy-done.29), custom_call_target="tpu_custom_call" | custom-call | flops 4831838208 | bytes 4718592 | tf_op jit(solution)/shard_map/attend_forward/pallas_call | solution.py:84
  134.2 16.1 %collective-permute-start.20 = (bf16[1,1,192,384]{3,2,0,1:T(8,128)(2,1)}, bf16[1,1,192,384]{3,2,0,1:T(8,128)(2,1)}, u32[]{:S(2)}, u32[]{:S(2)}) collective-permute-start(bf16[1,1,192,384]{3,2,0,1:T(8,128)(2,1)} %get-tuple-element.310), channel_id=1, source_target_pairs={{0,2},{2,0},{4,6},{6,4},{1,3},{3,1},{5,7},{7,5},{8,10},{10,8},{12,... | collective-permute-start | bytes 442376 | tf_op jit(solution)/shard_map/ppermute | solution.py:528
  151.8 10.2 %attend_forward.3 = (bf16[4,192,384]{2,1,0:T(8,128)(2,1)S(1)}, bf16[1536,1536]{1,0:T(8,128)(2,1)}) custom-call(bf16[1536,384]{1,0:T(8,128)(2,1)S(1)} %bitcast.409, bf16[3072,64]{1,0:T(8,128)(2,1)S(1)} %copy-done.30), custom_call_target="tpu_custom_call" | custom-call | flops 4831838208 | bytes 4718592 | tf_op jit(solution)/shard_map/attend_forward/pallas_call | solution.py:84
  174.1 20.0 %collective-permute-done.4 = bf16[1,1,192,384]{3,2,0,1:T(8,128)(2,1)S(1)} collective-permute-done((bf16[1,1,192,384]{3,2,0,1:T(8,128)(2,1)S(1)}, bf16[1,1,192,384]{3,2,0,1:T(8,128)(2,1)S(1)}, u32[]{:S(2)}, u32[]{:S(2)}) %collective-permute-start.4) | collective-permute-done | bytes 147488 | tf_op jit(solution)/shard_map/ppermute | solution.py:528
  200.6 20.6 %collective-permute-done.6 = bf16[768,384]{1,0:T(8,128)(2,1)S(1)} collective-permute-done((bf16[768,384]{1,0:T(8,128)(2,1)S(1)}, bf16[768,384]{1,0:T(8,128)(2,1)S(1)}, u32[]{:S(2)}, u32[]{:S(2)}) %collective-permute-start.6) | collective-permute-done | bytes 589856 | tf_op jit(solution)/shard_map/ppermute | solution.py:391
  271.1 11.0 %collective-permute-done.16 = bf16[384,1536]{1,0:T(8,128)(2,1)S(1)} collective-permute-done((bf16[384,1536]{1,0:T(8,128)(2,1)S(1)}, bf16[384,1536]{1,0:T(8,128)(2,1)S(1)}, u32[]{:S(2)}, u32[]{:S(2)}) %collective-permute-start.16) | collective-permute-done | bytes 1179680 | tf_op jit(solution)/shard_map/ppermute | solution.py:383
  283.2 24.2 %collective-permute-done.24 = bf16[384,1536]{1,0:T(8,128)(2,1)S(1)} collective-permute-done((bf16[384,1536]{1,0:T(8,128)(2,1)S(1)}, bf16[384,1536]{1,0:T(8,128)(2,1)S(1)}, u32[]{:S(2)}, u32[]{:S(2)}) %collective-permute-start.24) | collective-permute-done | bytes 1179680 | tf_op jit(solution)/shard_map/ppermute | solution.py:383
  308.4 17.0 %collective-permute-done.8 = bf16[384,1536]{1,0:T(8,128)(2,1)} collective-permute-done((bf16[384,1536]{1,0:T(8,128)(2,1)S(1)}, bf16[384,1536]{1,0:T(8,128)(2,1)}, u32[]{:S(2)}, u32[]{:S(2)}) %collective-permute-start.8) | collective-permute-done | bytes 1179680 | tf_op jit(solution)/shard_map/ppermute | solution.py:383
  325.4 8.9 fusion.198
  343.4 20.1 %score_heads.3 = (bf16[7168,384]{1,0:T(8,128)(2,1)}, f32[384,1536]{1,0:T(8,128)}, f32[7168,1]{1,0:T(8,128)}, f32[8,384]{1,0:T(8,128)}) custom-call(s32[2]{0:T(128)} %get-tuple-element.351.refs_0_, bf16[384,1536]{1,0:T(8,128)(2,1)} %get-tuple-element.194.refs_1_, f32[8,384]{1,0:T(8,128)} %broadcast_in_dim.20.refs_2_, bf16[5313,768]{1,0:T(8,128)(2,1)} %bitcast.444, ...), custom_call_target="tpu_custom_call" | custom-call | flops 12534939648 | bytes 32643072 | tf_op jit(solution)/shard_map/score_heads/pallas_call | solution.py:280
  363.4 35.3 %score_heads.4 = (bf16[7168,384]{1,0:T(8,128)(2,1)}, f32[384,1536]{1,0:T(8,128)}, f32[7168,1]{1,0:T(8,128)}, f32[8,384]{1,0:T(8,128)}) custom-call(s32[2]{0:T(128)} %get-tuple-element.352.refs_0_, bf16[384,1536]{1,0:T(8,128)(2,1)} %get-tuple-element.326.refs_1_, f32[8,384]{1,0:T(8,128)} %broadcast_in_dim.20.refs_2_, bf16[5313,768]{1,0:T(8,128)(2,1)} %bitcast.445, ...), custom_call_target="tpu_custom_call" | custom-call | flops 12534939648 | bytes 32643072 | tf_op jit(solution)/shard_map/score_heads/pallas_call | solution.py:280
  398.7 35.6 %score_heads.5 = (bf16[7168,384]{1,0:T(8,128)(2,1)}, f32[384,1536]{1,0:T(8,128)}, f32[7168,1]{1,0:T(8,128)}, f32[8,384]{1,0:T(8,128)}) custom-call(s32[2]{0:T(128)} %pad_add_fusion.2.refs_0_, bf16[384,1536]{1,0:T(8,128)(2,1)} %get-tuple-element.328.refs_1_, f32[8,384]{1,0:T(8,128)} %broadcast_in_dim.20.refs_2_, bf16[5313,768]{1,0:T(8,128)(2,1)} %bitcast.446, ...), custom_call_target="tpu_custom_call" | custom-call | flops 12534939648 | bytes 32643072 | tf_op jit(solution)/shard_map/score_heads/pallas_call | solution.py:280
  439.4 17.5 %head_grads.1 = bf16[7168,768]{1,0:T(8,128)(2,1)} custom-call(s32[3]{0:T(128)S(1)} %copy-done.26, bf16[7168,384]{1,0:T(8,128)(2,1)S(1)} %copy-done.27, bf16[7168,384]{1,0:T(8,128)(2,1)S(1)} %copy-done.28, bf16[7168,384]{1,0:T(8,128)(2,1)} %get-tuple-element.76.refs_3_, bf16[3,384,768]{2,1,0:T(8,128)(2,1)S(1)} %copy-done.14), custom_call_target="tpu_custom_call" | custom-call | flops 12683575296 | bytes 22020096 | tf_op jit(solution)/shard_map/head_grads/pallas_call | solution.py:344
  506.7 22.8 %collective-permute-done.29 = bf16[384,1536]{1,0:T(8,128)(2,1)} collective-permute-done((bf16[384,1536]{1,0:T(8,128)(2,1)}, bf16[384,1536]{1,0:T(8,128)(2,1)}, u32[]{:S(2)}, u32[]{:S(2)}) %collective-permute-start.29) | collective-permute-done | bytes 1179680 | tf_op jit(solution)/shard_map/ppermute | solution.py:383
  529.5 16.8 %collective-permute-done.28 = bf16[384,1536]{1,0:T(8,128)(2,1)} collective-permute-done((bf16[384,1536]{1,0:T(8,128)(2,1)}, bf16[384,1536]{1,0:T(8,128)(2,1)}, u32[]{:S(2)}, u32[]{:S(2)}) %collective-permute-start.28) | collective-permute-done | bytes 1179680 | tf_op jit(solution)/shard_map/ppermute | solution.py:383
  575.6 7.5 collective-permute-start.48
  617.0 17.9 %attend_backward.5 = (bf16[4,320,384]{2,1,0:T(8,128)(2,1)S(1)}, f32[64,3072]{1,0:T(8,128)S(1)}, f32[8,128]{1,0:T(8,128)S(1)}) custom-call(bf16[1536,384]{1,0:T(8,128)(2,1)S(1)} %bitcast.407, bf16[3072,64]{1,0:T(8,128)(2,1)S(1)} %copy-done.31, bf16[1536,1536]{1,0:T(8,128)(2,1)} %get-tuple-element.66.refs_2_, bf16[4,192,384]{2,1,0:T(8,128)(2,1)S(1)} %copy-done.13), custom_call_target="tpu_custom_call" | custom-call | flops 9663676416 | bytes 4718592 | tf_op jit(solution)/shard_map/attend_backward/pallas_call | solution.py:165
  639.7 18.0 %attend_backward.4 = (bf16[4,320,384]{2,1,0:T(8,128)(2,1)S(1)}, f32[64,3072]{1,0:T(8,128)S(1)}, f32[8,128]{1,0:T(8,128)S(1)}) custom-call(bf16[1536,384]{1,0:T(8,128)(2,1)S(1)} %bitcast.404, bf16[3072,64]{1,0:T(8,128)(2,1)S(1)} %copy-done.32, bf16[1536,1536]{1,0:T(8,128)(2,1)} %get-tuple-element.64.refs_2_, ...), custom_call_target="tpu_custom_call" | custom-call | flops 9663676416 | bytes 4718592 | tf_op jit(solution)/shard_map/attend_backward/pallas_call | solution.py:165
  663.3 18.3 %attend_backward.3 = (bf16[4,320,384]{2,1,0:T(8,128)(2,1)S(1)}, f32[64,3072]{1,0:T(8,128)S(1)}, f32[8,128]{1,0:T(8,128)S(1)}) custom-call(bf16[1536,384]{1,0:T(8,128)(2,1)S(1)} %bitcast.410, bf16[3072,64]{1,0:T(8,128)(2,1)S(1)} %copy-done.32, bf16[1536,1536]{1,0:T(8,128)(2,1)} %get-tuple-element.62.refs_2_, ...), custom_call_target="tpu_custom_call" | custom-call | flops 9663676416 | bytes 4718592 | tf_op jit(solution)/shard_map/attend_backward/pallas_call | solution.py:165
  696.8 7.0 collective-permute-done.44
  704.5 7.9 collective-permute-done.45
  731.9 15.0 %collective-permute-done.38 = bf16[1,1,320,384]{3,2,0,1:T(8,128)(2,1)S(1)} collective-permute-done((bf16[1,1,320,384]{3,2,0,1:T(8,128)(2,1)S(1)}, bf16[1,1,320,384]{3,2,0,1:T(8,128)(2,1)S(1)}, u32[]{:S(2)}, u32[]{:S(2)}) %collective-permute-start.38) | collective-permute-done | bytes 245792 | tf_op jit(solution)/shard_map/ppermute | solution.py:528
  776.7 21.5 %collective-permute-done.47 = bf16[384,1536]{1,0:T(8,128)(2,1)S(1)} collective-permute-done((bf16[384,1536]{1,0:T(8,128)(2,1)S(1)}, bf16[384,1536]{1,0:T(8,128)(2,1)S(1)}, u32[]{:S(2)}, u32[]{:S(2)}) %collective-permute-start.47) | collective-permute-done | bytes 1179680 | tf_op jit(solution)/shard_map/ppermute | solution.py:383
  798.2 12.6 %collective-permute-done.40 = bf16[384,1536]{1,0:T(8,128)(2,1)S(1)} collective-permute-done((bf16[384,1536]{1,0:T(8,128)(2,1)S(1)}, bf16[384,1536]{1,0:T(8,128)(2,1)S(1)}, u32[]{:S(2)}, u32[]{:S(2)}) %collective-permute-start.40) | collective-permute-done | bytes 1179680 | tf_op jit(solution)/shard_map/ppermute | solution.py:383
  857.7 6.4 collective-permute-done.68
  883.9 13.9 %collective-permute-done.76 = bf16[96,1536]{1,0:T(8,128)(2,1)} collective-permute-done((bf16[96,1536]{1,0:T(8,128)(2,1)}, bf16[96,1536]{1,0:T(8,128)(2,1)}, u32[]{:S(2)}, u32[]{:S(2)}) %collective-permute-start.76) | collective-permute-done | bytes 294944 | tf_op jit(solution)/shard_map/ppermute | solution.py:458
  902.8 20.3 %collective-permute-done.72 = bf16[96,1536]{1,0:T(8,128)(2,1)S(1)} collective-permute-done((bf16[96,1536]{1,0:T(8,128)(2,1)}, bf16[96,1536]{1,0:T(8,128)(2,1)S(1)}, u32[]{:S(2)}, u32[]{:S(2)}) %collective-permute-start.72) | collective-permute-done | bytes 294944 | tf_op jit(solution)/shard_map/ppermute | solution.py:458
  932.6 11.0 %convert_bitcast_fusion = f32[768,5313]{0,1:T(8,128)} fusion(bf16[7168,768]{1,0:T(8,128)(2,1)} %all-reduce.6.cloned.1.call-done), kind=kLoop, calls=%fused_computation | loop fusion | flops 4080384 | bytes 24482304 | tf_op jit(solution)/shard_map/transpose | solution.py:804
  943.5 11.7 %collective-permute-done.60 = bf16[384,1280]{1,0:T(8,128)(2,1)S(1)} collective-permute-done((bf16[384,1280]{1,0:T(8,128)(2,1)S(1)}, bf16[384,1280]{1,0:T(8,128)(2,1)S(1)}, u32[]{:S(2)}, u32[]{:S(2)}) %collective-permute-start.60) | collective-permute-done | bytes 983072 | tf_op jit(solution)/shard_map/ppermute | solution.py:450
  955.7 6.9 collective-permute-start.61
  971.8 11.2 %collective-permute-done.62 = bf16[96,1280]{1,0:T(8,128)(2,1)S(1)} collective-permute-done((bf16[96,1280]{1,0:T(8,128)(2,1)S(1)}, bf16[96,1280]{1,0:T(8,128)(2,1)S(1)}, u32[]{:S(2)}, u32[]{:S(2)}) %collective-permute-start.62) | collective-permute-done | bytes 245792 | tf_op jit(solution)/shard_map/ppermute | solution.py:458
  (834 shorter events, 470.0 us)
Async XLA Ops:
  7.2 221.9 %all-gather.4.cloned.1.call-start = ((), (), s32[]{:S(2)}) async-start(), calls=%async_computation | async-start | bytes 2506752 | tf_op jit(solution)/shard_map/all_gather | solution.py:412
  30.8 59.2 %collective-permute-start.9 = (bf16[1,1,384,384]{3,2,1,0:T(8,128)(2,1)}, bf16[1,1,384,384]{3,2,1,0:T(8,128)(2,1)}, u32[]{:S(2)}, u32[]{:S(2)}) collective-permute-start(bf16[1,1,384,384]{3,2,1,0:T(8,128)(2,1)} %get-tuple-element.266), channel_id=1, source_target_pairs={{0,2},{2,0},{4,6},{6,4},{1,3},{3,1},{5,7},{7,5},{8,10},{10,8},{12,... | collective-permute-start | bytes 884744 | tf_op jit(solution)/shard_map/ppermute | solution.py:528
  33.8 57.4 %collective-permute-start.10 = (bf16[1,1,384,384]{3,2,1,0:T(8,128)(2,1)}, bf16[1,1,384,384]{3,2,1,0:T(8,128)(2,1)}, u32[]{:S(2)}, u32[]{:S(2)}) collective-permute-start(bf16[1,1,384,384]{3,2,1,0:T(8,128)(2,1)} %get-tuple-element.265), channel_id=1, source_target_pairs={{0,4},{2,6},{4,0},{6,2},{1,5},{3,7},{5,1},{7,3},{8,12},{10,14},{12... | collective-permute-start | bytes 884744 | tf_op jit(solution)/shard_map/ppermute | solution.py:528
  36.4 56.3 %collective-permute-start.11 = (bf16[1,1,384,384]{3,2,1,0:T(8,128)(2,1)}, bf16[1,1,384,384]{3,2,1,0:T(8,128)(2,1)}, u32[]{:S(2)}, u32[]{:S(2)}) collective-permute-start(bf16[1,1,384,384]{3,2,1,0:T(8,128)(2,1)} %get-tuple-element.264), channel_id=1, source_target_pairs={{0,6},{2,4},{4,2},{6,0},{1,7},{3,5},{5,3},{7,1},{8,14},{10,12},{12... | collective-permute-start | bytes 884744 | tf_op jit(solution)/shard_map/ppermute | solution.py:528
  43.3 299.5 %all-gather.8.cloned.1.call-start = ((), (), s32[]{:S(2)}) async-start(), calls=%async_computation.2 | async-start | bytes 2924544 | tf_op jit(solution)/shard_map/all_gather | solution.py:412
  49.7 59.3 %collective-permute-start.17 = (bf16[1,1,384,384]{3,2,1,0:T(8,128)(2,1)}, bf16[1,1,384,384]{3,2,1,0:T(8,128)(2,1)}, u32[]{:S(2)}, u32[]{:S(2)}) collective-permute-start(bf16[1,1,384,384]{3,2,1,0:T(8,128)(2,1)} %get-tuple-element.273), channel_id=1, source_target_pairs={{0,2},{2,0},{4,6},{6,4},{1,3},{3,1},{5,7},{7,5},{8,10},{10,8},{12,... | collective-permute-start | bytes 884744 | tf_op jit(solution)/shard_map/ppermute | solution.py:528
  64.4 46.6 %collective-permute-start.18 = (bf16[1,1,384,384]{3,2,1,0:T(8,128)(2,1)}, bf16[1,1,384,384]{3,2,1,0:T(8,128)(2,1)}, u32[]{:S(2)}, u32[]{:S(2)}) collective-permute-start(bf16[1,1,384,384]{3,2,1,0:T(8,128)(2,1)} %get-tuple-element.272), channel_id=1, source_target_pairs={{0,4},{2,6},{4,0},{6,2},{1,5},{3,7},{5,1},{7,3},{8,12},{10,14},{12... | collective-permute-start | bytes 884744 | tf_op jit(solution)/shard_map/ppermute | solution.py:528
  67.9 274.8 %all-gather.6.cloned.1.call-start = ((), (), s32[]{:S(2)}) async-start(), calls=%async_computation.1 | async-start | bytes 8773632 | tf_op jit(solution)/shard_map/all_gather | solution.py:412
  92.7 41.4 %collective-permute-start.1 = (bf16[1,1,384,384]{3,2,1,0:T(8,128)(2,1)}, bf16[1,1,384,384]{3,2,1,0:T(8,128)(2,1)S(1)}, u32[]{:S(2)}, u32[]{:S(2)}) collective-permute-start(bf16[1,1,384,384]{3,2,1,0:T(8,128)(2,1)} %get-tuple-element.258), channel_id=1, source_target_pairs={{0,4},{2,6},{4,0},{6,2},{1,5},{3,7},{5,1},{7,3},{8,12},{10,14},{12... | collective-permute-start | bytes 884744 | tf_op jit(solution)/shard_map/ppermute | solution.py:528
  111.0 39.3 %collective-permute-start.25 = (bf16[336,768]{1,0:T(8,128)(2,1)S(1)}, bf16[336,768]{1,0:T(8,128)(2,1)}, u32[]{:S(2)}, u32[]{:S(2)}) collective-permute-start(bf16[336,768]{1,0:T(8,128)(2,1)S(1)} %copy-done.112), channel_id=1, source_target_pairs={{0,1},{1,0},{2,3},{3,2},{4,5},{5,4},{6,7},{7,6},{8,9},{9,8},{10,11... | collective-permute-start | bytes 1548296 | tf_op jit(solution)/shard_map/ppermute | solution.py:411
  112.5 49.5 %collective-permute-start.12 = (bf16[1,1,192,384]{3,2,0,1:T(8,128)(2,1)}, bf16[1,1,192,384]{3,2,0,1:T(8,128)(2,1)}, u32[]{:S(2)}, u32[]{:S(2)}) collective-permute-start(bf16[1,1,192,384]{3,2,0,1:T(8,128)(2,1)} %get-tuple-element.307), channel_id=1, source_target_pairs={{0,2},{2,0},{4,6},{6,4},{1,3},{3,1},{5,7},{7,5},{8,10},{10,8},{12,... | collective-permute-start | bytes 442376 | tf_op jit(solution)/shard_map/ppermute | solution.py:528
  123.4 42.1 %collective-permute-start.13 = (bf16[1,1,192,384]{3,2,0,1:T(8,128)(2,1)}, bf16[1,1,192,384]{3,2,0,1:T(8,128)(2,1)}, u32[]{:S(2)}, u32[]{:S(2)}) collective-permute-start(bf16[1,1,192,384]{3,2,0,1:T(8,128)(2,1)} %get-tuple-element.306), channel_id=1, source_target_pairs={{0,4},{2,6},{4,0},{6,2},{1,5},{3,7},{5,1},{7,3},{8,12},{10,14},{12... | collective-permute-start | bytes 442376 | tf_op jit(solution)/shard_map/ppermute | solution.py:528
  134.1 33.5 %collective-permute-start.14 = (bf16[1,1,192,384]{3,2,0,1:T(8,128)(2,1)}, bf16[1,1,192,384]{3,2,0,1:T(8,128)(2,1)}, u32[]{:S(2)}, u32[]{:S(2)}) collective-permute-start(bf16[1,1,192,384]{3,2,0,1:T(8,128)(2,1)} %get-tuple-element.305), channel_id=1, source_target_pairs={{0,6},{2,4},{4,2},{6,0},{1,7},{3,5},{5,3},{7,1},{8,14},{10,12},{12... | collective-permute-start | bytes 442376 | tf_op jit(solution)/shard_map/ppermute | solution.py:528
  134.2 62.1 %collective-permute-start.20 = (bf16[1,1,192,384]{3,2,0,1:T(8,128)(2,1)}, bf16[1,1,192,384]{3,2,0,1:T(8,128)(2,1)}, u32[]{:S(2)}, u32[]{:S(2)}) collective-permute-start(bf16[1,1,192,384]{3,2,0,1:T(8,128)(2,1)} %get-tuple-element.310), channel_id=1, source_target_pairs={{0,2},{2,0},{4,6},{6,4},{1,3},{3,1},{5,7},{7,5},{8,10},{10,8},{12,... | collective-permute-start | bytes 442376 | tf_op jit(solution)/shard_map/ppermute | solution.py:528
  150.3 46.9 %collective-permute-start.21 = (bf16[1,1,192,384]{3,2,0,1:T(8,128)(2,1)}, bf16[1,1,192,384]{3,2,0,1:T(8,128)(2,1)}, u32[]{:S(2)}, u32[]{:S(2)}) collective-permute-start(bf16[1,1,192,384]{3,2,0,1:T(8,128)(2,1)} %get-tuple-element.309), channel_id=1, source_target_pairs={{0,4},{2,6},{4,0},{6,2},{1,5},{3,7},{5,1},{7,3},{8,12},{10,14},{12... | collective-permute-start | bytes 442376 | tf_op jit(solution)/shard_map/ppermute | solution.py:528
  150.4 782.1 %all-reduce.6.cloned.1.call-start = ((), (), s32[]{:S(2)}) async-start(), calls=%async_computation.3 | async-start | bytes 22020096 | tf_op jit(solution)/shard_map/psum | solution.py:677
  162.1 36.1 %collective-permute-start.22 = (bf16[1,1,192,384]{3,2,0,1:T(8,128)(2,1)S(1)}, bf16[1,1,192,384]{3,2,0,1:T(8,128)(2,1)S(1)}, u32[]{:S(2)}, u32[]{:S(2)}) collective-permute-start(bf16[1,1,192,384]{3,2,0,1:T(8,128)(2,1)S(1)} %copy-done.115), channel_id=1, source_target_pairs={{0,6},{2,4},{4,2},{6,0},{1,7},{3,5},{5,3},{7,1},{8,14},{10,12},{12... | collective-permute-start | bytes 442376 | tf_op jit(solution)/shard_map/ppermute | solution.py:528
  261.3 46.1 %collective-permute-start.24 = (bf16[384,1536]{1,0:T(8,128)(2,1)S(1)}, bf16[384,1536]{1,0:T(8,128)(2,1)S(1)}, u32[]{:S(2)}, u32[]{:S(2)}) collective-permute-start(bf16[384,1536]{1,0:T(8,128)(2,1)S(1)} %convolution_convert_fusion.7), channel_id=1, source_target_pairs={{0,1},{1,0},{2,3},{3,2},{4,5},{5,4},{6,7},{7,6},{8,9},{9,8},{10,11... | collective-permute-start | bytes 3538952 | tf_op jit(solution)/shard_map/ppermute | solution.py:383
  267.3 58.2 %collective-permute-start.8 = (bf16[384,1536]{1,0:T(8,128)(2,1)S(1)}, bf16[384,1536]{1,0:T(8,128)(2,1)}, u32[]{:S(2)}, u32[]{:S(2)}) collective-permute-start(bf16[384,1536]{1,0:T(8,128)(2,1)S(1)} %convolution_convert_fusion.9), channel_id=1, source_target_pairs={{0,1},{1,0},{2,3},{3,2},{4,5},{5,4},{6,7},{7,6},{8,9},{9,8},{10,11... | collective-permute-start | bytes 3538952 | tf_op jit(solution)/shard_map/ppermute | solution.py:383
  479.8 49.7 %collective-permute-start.29 = (bf16[384,1536]{1,0:T(8,128)(2,1)}, bf16[384,1536]{1,0:T(8,128)(2,1)}, u32[]{:S(2)}, u32[]{:S(2)}) collective-permute-start(bf16[384,1536]{1,0:T(8,128)(2,1)} %convolution_convert_fusion.4), channel_id=1, source_target_pairs={{0,1},{1,0},{2,3},{3,2},{4,5},{5,4},{6,7},{7,6},{8,9},{9,8},{10,11... | collective-permute-start | bytes 3538952 | tf_op jit(solution)/shard_map/ppermute | solution.py:383
  483.2 63.1 %collective-permute-start.28 = (bf16[384,1536]{1,0:T(8,128)(2,1)}, bf16[384,1536]{1,0:T(8,128)(2,1)}, u32[]{:S(2)}, u32[]{:S(2)}) collective-permute-start(bf16[384,1536]{1,0:T(8,128)(2,1)} %convolution_convert_fusion.5), channel_id=1, source_target_pairs={{0,1},{1,0},{2,3},{3,2},{4,5},{5,4},{6,7},{7,6},{8,9},{9,8},{10,11... | collective-permute-start | bytes 3538952 | tf_op jit(solution)/shard_map/ppermute | solution.py:383
  489.8 261.0 %collective-permute-start.74 = (bf16[768,1536]{1,0:T(8,128)(2,1)}, bf16[768,1536]{1,0:T(8,128)(2,1)}, u32[]{:S(2)}, u32[]{:S(2)}) collective-permute-start(bf16[768,1536]{1,0:T(8,128)(2,1)} %convolution_convert_fusion.2), channel_id=1, source_target_pairs={{0,8},{8,0},{16,24},{24,16},{1,9},{9,1},{17,25},{25,17},{2,10},{10... | collective-permute-start | bytes 7077896 | tf_op jit(solution)/shard_map/ppermute | solution.py:442
  494.9 264.0 %collective-permute-start.69 = (bf16[768,1536]{1,0:T(8,128)(2,1)}, bf16[768,1536]{1,0:T(8,128)(2,1)}, u32[]{:S(2)}, u32[]{:S(2)}) collective-permute-start(bf16[768,1536]{1,0:T(8,128)(2,1)} %convolution_convert_fusion.3), channel_id=1, source_target_pairs={{0,8},{8,0},{16,24},{24,16},{1,9},{9,1},{17,25},{25,17},{2,10},{10... | collective-permute-start | bytes 7077896 | tf_op jit(solution)/shard_map/ppermute | solution.py:442
  661.5 32.7 %collective-permute-start.53 = (bf16[1,1,320,384]{3,2,0,1:T(8,128)(2,1)S(1)}, bf16[1,1,320,384]{3,2,0,1:T(8,128)(2,1)}, u32[]{:S(2)}, u32[]{:S(2)}) collective-permute-start(bf16[1,1,320,384]{3,2,0,1:T(8,128)(2,1)S(1)} %get-tuple-element.285), channel_id=1, source_target_pairs={{0,6},{2,4},{4,2},{6,0},{1,7},{3,5},{5,3},{7,1},{8,14},{10,12},{12... | collective-permute-start | bytes 737288 | tf_op jit(solution)/shard_map/ppermute | solution.py:528
  712.4 34.4 %collective-permute-start.38 = (bf16[1,1,320,384]{3,2,0,1:T(8,128)(2,1)S(1)}, bf16[1,1,320,384]{3,2,0,1:T(8,128)(2,1)S(1)}, u32[]{:S(2)}, u32[]{:S(2)}) collective-permute-start(bf16[1,1,320,384]{3,2,0,1:T(8,128)(2,1)S(1)} %get-tuple-element.280), channel_id=1, source_target_pairs={{0,4},{2,6},{4,0},{6,2},{1,5},{3,7},{5,1},{7,3},{8,12},{10,14},{12... | collective-permute-start | bytes 737288 | tf_op jit(solution)/shard_map/ppermute | solution.py:528
  731.7 35.4 %collective-permute-start.64 = (bf16[768,768]{1,0:T(8,128)(2,1)S(1)}, bf16[768,768]{1,0:T(8,128)(2,1)S(1)}, u32[]{:S(2)}, u32[]{:S(2)}) collective-permute-start(bf16[768,768]{1,0:T(8,128)(2,1)S(1)} %copy-done.177), channel_id=1, source_target_pairs={{0,8},{8,0},{16,24},{24,16},{1,9},{9,1},{17,25},{25,17},{2,10},{10... | collective-permute-start | bytes 3538952 | tf_op jit(solution)/shard_map/ppermute | solution.py:442
  747.9 50.3 %collective-permute-start.47 = (bf16[384,1536]{1,0:T(8,128)(2,1)S(1)}, bf16[384,1536]{1,0:T(8,128)(2,1)S(1)}, u32[]{:S(2)}, u32[]{:S(2)}) collective-permute-start(bf16[384,1536]{1,0:T(8,128)(2,1)S(1)} %convolution_convert_fusion.11), channel_id=1, source_target_pairs={{0,1},{1,0},{2,3},{3,2},{4,5},{5,4},{6,7},{7,6},{8,9},{9,8},{10,11... | collective-permute-start | bytes 3538952 | tf_op jit(solution)/shard_map/ppermute | solution.py:383
  750.8 60.0 %collective-permute-start.40 = (bf16[384,1536]{1,0:T(8,128)(2,1)S(1)}, bf16[384,1536]{1,0:T(8,128)(2,1)S(1)}, u32[]{:S(2)}, u32[]{:S(2)}) collective-permute-start(bf16[384,1536]{1,0:T(8,128)(2,1)S(1)} %convolution_convert_fusion.12), channel_id=1, source_target_pairs={{0,1},{1,0},{2,3},{3,2},{4,5},{5,4},{6,7},{7,6},{8,9},{9,8},{10,11... | collective-permute-start | bytes 3538952 | tf_op jit(solution)/shard_map/ppermute | solution.py:383
  758.8 108.9 %collective-permute-start.75 = (bf16[384,1536]{1,0:T(8,128)(2,1)}, bf16[384,1536]{1,0:T(8,128)(2,1)}, u32[]{:S(2)}, u32[]{:S(2)}) collective-permute-start(bf16[384,1536]{1,0:T(8,128)(2,1)} %select_convert_fusion), channel_id=1, source_target_pairs={{0,16},{8,24},{16,0},{24,8},{1,17},{9,25},{17,1},{25,9},{2,18},{10... | collective-permute-start | bytes 3538952 | tf_op jit(solution)/shard_map/ppermute | solution.py:450
  767.1 105.9 %collective-permute-start.70 = (bf16[384,1536]{1,0:T(8,128)(2,1)}, bf16[384,1536]{1,0:T(8,128)(2,1)}, u32[]{:S(2)}, u32[]{:S(2)}) collective-permute-start(bf16[384,1536]{1,0:T(8,128)(2,1)} %select_convert_fusion.1), channel_id=1, source_target_pairs={{0,16},{8,24},{16,0},{24,8},{1,17},{9,25},{17,1},{25,9},{2,18},{10... | collective-permute-start | bytes 3538952 | tf_op jit(solution)/shard_map/ppermute | solution.py:450
  775.7 69.3 %collective-permute-start.65 = (bf16[384,768]{1,0:T(8,128)(2,1)}, bf16[384,768]{1,0:T(8,128)(2,1)}, u32[]{:S(2)}, u32[]{:S(2)}) collective-permute-start(bf16[384,768]{1,0:T(8,128)(2,1)} %select_convert_fusion.3), channel_id=1, source_target_pairs={{0,16},{8,24},{16,0},{24,8},{1,17},{9,25},{17,1},{25,9},{2,18},{10... | collective-permute-start | bytes 1769480 | tf_op jit(solution)/shard_map/ppermute | solution.py:450
  857.5 67.6 %collective-permute-start.59 = (bf16[768,1280]{1,0:T(8,128)(2,1)}, bf16[768,1280]{1,0:T(8,128)(2,1)}, u32[]{:S(2)}, u32[]{:S(2)}) collective-permute-start(bf16[768,1280]{1,0:T(8,128)(2,1)} %convolution_convert_fusion.1), channel_id=1, source_target_pairs={{0,8},{8,0},{16,24},{24,16},{1,9},{9,1},{17,25},{25,17},{2,10},{10... | collective-permute-start | bytes 5898248 | tf_op jit(solution)/shard_map/ppermute | solution.py:442
  (260 other events, 4085.2 us)
Sparse Core Ops, SparseCore 0:
  43.4 49.3 all-gather.3
  95.1 62.5 all-gather.7
  160.0 84.8 all-gather.5
  457.1 300.6 all-reduce.5

commit v3 on v2

v3 whole, which is shorter than its diff:
```python
import math

import jax
import jax.numpy as jnp
from jax import lax
from jax.experimental import pallas as pl
from jax.experimental.pallas import tpu as pltpu
from jax.sharding import PartitionSpec as P

KD = 64
VD = 192
FEAT = 192
BINS = 1536
CROP = 896


norm_eps = 1e-05
log_eps = 1e-07
exact_mode = lax.Precision.HIGHEST


def rel_basis():
    per_class = FEAT // 6
    distance = jnp.arange(-(BINS - 1), BINS).astype(jnp.float32)
    magnitude = jnp.abs(distance)[:, None]
    half_life = (2.0 ** jnp.linspace(3.0, math.log2(BINS), per_class)).astype(jnp.float32)
    decays = jnp.exp(-math.log(2.0) / half_life[None, :] * magnitude)
    widths = (2.0 ** jnp.arange(1, per_class + 1)).astype(jnp.float32) - 1.0
    central = (widths[None, :] > magnitude).astype(jnp.float32)
    spread = BINS / (2.0 * per_class)
    centre = jnp.linspace(BINS / per_class, BINS, per_class).astype(jnp.float32)
    concentration = (centre / spread) ** 2
    rate_param = centre / spread**2
    peak_at = (concentration - 1.0) / rate_param
    log_ratio = (concentration - 1.0) * (
        jnp.log(jnp.maximum(magnitude, 1e-20)) - jnp.log(peak_at)
    ) - rate_param * (magnitude - peak_at)
    density = jnp.exp(log_ratio)
    gammas = density / jnp.max(density, axis=0, keepdims=True)
    symmetric = jnp.concatenate([decays, central, gammas], axis=1)
    return jnp.concatenate([symmetric, jnp.sign(distance)[:, None] * symmetric], axis=1)


PACK = VD + 3 * KD
GRAD_PACK = VD + 2 * KD
TILE = 896
NN = (((1,), (0,)), ((), ()))
NT = (((1,), (1,)), ((), ()))
TN = (((0,), (0,)), ((), ()))


def mxu(left_arr, right_arr, dims, precision=None):
    return lax.dot_general(
        left_arr, right_arr, dims, precision=precision, preferred_element_type=jnp.float32
    )


def query_block(bins):
    for block in (384, 256, 128):
        if bins % block == 0:
            return block
    return bins


def attend_forward_kernel(block, bins, pack_ref, rel_ref, out_ref, probs_ref):
    step = pl.program_id(0)
    span = bins + block
    query = pack_ref[pl.ds(pl.multiple_of(step * block, block), block), VD + KD :]
    base = pl.multiple_of(bins - block - step * block, block)
    content = mxu(query[:, :KD], pack_ref[:, VD : VD + KD], NT)
    position = mxu(query[:, KD:], rel_ref[pl.ds(base, span), :], NT)
    position = pltpu.roll(position, span - (block - 1), 1, stride=1, stride_axis=0)
    scores = content + position[:, :bins]
    exps = jnp.exp(scores - jnp.max(scores, axis=1, keepdims=True))
    probs = (exps * (1.0 / jnp.sum(exps, axis=1, keepdims=True))).astype(jnp.bfloat16)
    probs_ref[...] = probs
    out_ref[0] = mxu(probs, pack_ref[:, :VD], NN).T.astype(jnp.bfloat16)


def attend_forward(pack, rel):
    bins = pack.shape[0]
    block = query_block(bins)
    steps = bins // block
    return pl.pallas_call(
        lambda *refs: attend_forward_kernel(block, bins, *refs),
        grid=(steps,),
        in_specs=[
            pl.BlockSpec((bins, PACK), lambda i: (0, 0)),
            pl.BlockSpec((2 * bins, KD), lambda i: (0, 0)),
        ],
        out_specs=[
            pl.BlockSpec((1, VD, block), lambda i: (i, 0, 0)),
            pl.BlockSpec((block, bins), lambda i: (i, 0)),
        ],
        out_shape=[
            jax.ShapeDtypeStruct((steps, VD, block), jnp.bfloat16),
            jax.ShapeDtypeStruct((bins, bins), jnp.bfloat16),
        ],
        compiler_params=pltpu.CompilerParams(vmem_limit_bytes=48 << 20),
        cost_estimate=pl.CostEstimate(
            flops=2 * bins * bins * 1024, bytes_accessed=2 * bins * bins, transcendentals=bins * bins
        ),
        name="attend_forward",
    )(pack, rel)


def attend_backward_kernel(
    block, bins, pack_ref, rel_ref, probs_ref, grad_ref, out_ref, drel_ref, stat_ref, acc_ref
):
    step = pl.program_id(0)
    steps = bins // block
    span = bins + block

    @pl.when(step == 0)
    def _():
        acc_ref[...] = jnp.zeros_like(acc_ref)
        drel_ref[...] = jnp.zeros_like(drel_ref)
        stat_ref[...] = jnp.zeros_like(stat_ref)

    query = pack_ref[pl.ds(pl.multiple_of(step * block, block), block), VD + KD :]
    base = pl.multiple_of(bins - block - step * block, block)
    grad_t = grad_ref[0]
    probs = probs_ref[...]
    acc_ref[:VD, :] += mxu(grad_t, probs, NN)
    grad_probs = mxu(grad_t.T, pack_ref[:, :VD], NT)
    wide = probs.astype(jnp.float32)
    scaled = wide * grad_probs
    delta = jnp.sum(scaled, axis=1, keepdims=True)
    grad_scores = (scaled - wide * delta).astype(jnp.bfloat16)
    grad_qc = mxu(grad_scores, pack_ref[:, VD : VD + KD], NN)
    query_t = query.T
    acc_ref[VD:, :] += mxu(query_t[:KD], grad_scores, NN)
    row = lax.broadcasted_iota(jnp.int32, (block, block), 0)
    col = lax.broadcasted_iota(jnp.int32, (block, block), 1)
    flip = (row + col == block - 1).astype(jnp.bfloat16)
    turned = mxu(flip, grad_scores, NN)
    turned = jnp.concatenate([turned, jnp.zeros((block, block), jnp.float32)], axis=1)
    turned = pltpu.roll(turned, 0, 1, stride=1, stride_axis=0).astype(jnp.bfloat16)
    grad_qp = mxu(
        flip.astype(jnp.float32),
        mxu(turned, rel_ref[pl.ds(base, span), :], NN),
        NN,
        exact_mode,
    )
    pos_turned = mxu(query_t[KD:], flip, NN).astype(jnp.bfloat16)
    drel_ref[:, pl.ds(base, span)] += mxu(pos_turned, turned, NN)
    stat_ref[0:1, :KD] += jnp.sum(grad_qc, axis=0, keepdims=True)
    stat_ref[1:2, :KD] += jnp.sum(grad_qp, axis=0, keepdims=True)
    out_ref[pl.ds(step, 1), VD + KD :, :] = (
        ((grad_qc + grad_qp) * (KD**-0.5)).T.astype(jnp.bfloat16)[None]
    )

    @pl.when(step == steps - 1)
    def _():
        for part in range(steps):
            out_ref[part, : VD + KD, :] = acc_ref[:, part * block : (part + 1) * block].astype(
                jnp.bfloat16
            )


def attend_backward(pack, rel, probs, grad):
    bins = pack.shape[0]
    block = query_block(bins)
    steps = bins // block
    return pl.pallas_call(
        lambda *refs: attend_backward_kernel(block, bins, *refs),
        grid=(steps,),
        in_specs=[
            pl.BlockSpec((bins, PACK), lambda i: (0, 0)),
            pl.BlockSpec((2 * bins, KD), lambda i: (0, 0)),
            pl.BlockSpec((block, bins), lambda i: (i, 0)),
            pl.BlockSpec((1, VD, block), lambda i: (i, 0, 0)),
        ],
        out_specs=[
            pl.BlockSpec((steps, GRAD_PACK, block), lambda i: (0, 0, 0)),
            pl.BlockSpec((KD, 2 * bins), lambda i: (0, 0)),
            pl.BlockSpec((8, 128), lambda i: (0, 0)),
        ],
        out_shape=[
            jax.ShapeDtypeStruct((steps, GRAD_PACK, block), jnp.bfloat16),
            jax.ShapeDtypeStruct((KD, 2 * bins), jnp.float32),
            jax.ShapeDtypeStruct((8, 128), jnp.float32),
        ],
        scratch_shapes=[pltpu.VMEM((VD + KD, bins), jnp.float32)],
        compiler_params=pltpu.CompilerParams(vmem_limit_bytes=48 << 20),
        cost_estimate=pl.CostEstimate(
            flops=2 * bins * bins * 2048, bytes_accessed=2 * bins * bins, transcendentals=0
        ),
        name="attend_backward",
    )(pack, rel, probs, grad)


def heads_kernel(
    track_human,
    track_mouse,
    pick_ref,
    rows_ref,
    weight_ref,
    human_ref,
    mouse_ref,
    human_other_ref,
    mouse_other_ref,
    bias_ref,
    count_human_ref,
    count_mouse_ref,
    grad_ref,
    dtrunk_ref,
    dbias_ref,
    loss_ref,
):
    step = pl.program_id(0)
    kind, swapped = pick_ref[0], pick_ref[1] == 1

    @pl.when(step == 0)
    def _():
        dtrunk_ref[...] = jnp.zeros_like(dtrunk_ref)
        loss_ref[...] = jnp.zeros_like(loss_ref)

    def score(own_ref, other_ref, count_ref, tracks):
        valid = lax.broadcasted_iota(jnp.int32, (TILE, 1), 0) + step * TILE < tracks
        own = jnp.where(valid, own_ref[...], 0.0).astype(jnp.bfloat16)
        oth = jnp.where(valid, other_ref[...], 0.0).astype(jnp.bfloat16)
        head = jnp.concatenate(
            [jnp.where(swapped, oth, own), jnp.where(swapped, own, oth)], axis=1
        )
        logits = mxu(head, rows_ref[...], NT) + bias_ref[:, 0:1]
        counts = count_ref[0].astype(jnp.float32)
        small = jnp.exp(-jnp.abs(logits))
        inverse = 1.0 / (1.0 + small)
        predicted = jnp.maximum(logits, 0.0) + jnp.log1p(small)
        shifted = predicted + log_eps
        sigma = jnp.where(logits >= 0.0, 1.0, small) * inverse
        weight = jnp.where(valid, weight_ref[0:1, :], 0.0)
        rows_loss = weight * (predicted - counts * jnp.log(shifted))
        grad = weight * (sigma - counts * sigma / shifted)
        loss_ref[...] += jnp.sum(rows_loss.reshape(TILE // 8, 8, -1), axis=0)
        bins = grad.shape[1]
        if bins % 128 == 0:
            folded = sum(grad[:, i : i + 128] for i in range(0, bins, 128))
        else:
            folded = jnp.broadcast_to(jnp.sum(grad, axis=1, keepdims=True) / 128, (TILE, 128))
        dbias_ref[...] = jnp.sum(folded.T.reshape(16, 8, TILE), axis=0)
        grad_low = grad.astype(jnp.bfloat16)
        grad_ref[...] = grad_low
        dtrunk_ref[...] += mxu(grad_low.T, head, NN)

    @pl.when(jnp.logical_and(kind == 0, step < pl.cdiv(track_human, TILE)))
    def _():
        score(human_ref, human_other_ref, count_human_ref, track_human)

    @pl.when(jnp.logical_and(kind == 1, step < pl.cdiv(track_mouse, TILE)))
    def _():
        score(mouse_ref, mouse_other_ref, count_mouse_ref, track_mouse)


def score_heads(window, pick, rows, weight, own, others, bias, count_human, count_mouse):
    bins, width = rows.shape
    share = own[0].shape[1]
    rest = width - share
    track_human, track_mouse = count_human.shape[1], count_mouse.shape[1]
    tiles_human, tiles_mouse = pl.cdiv(track_human, TILE), pl.cdiv(track_mouse, TILE)

    def tile(kind, tiles):
        return lambda t, p: jnp.where(p[0] == kind, jnp.minimum(t, tiles - 1), 0)

    human_tile, mouse_tile = tile(0, tiles_human), tile(1, tiles_mouse)

    def out_tile(t, p):
        mine = jnp.where(p[0] == 0, jnp.minimum(t, tiles_human - 1), 0)
        return jnp.where(p[0] == 1, tiles_human + jnp.minimum(t, tiles_mouse - 1), mine)

    whole = lambda t, p: (0, 0)
    tracks = (tiles_human + tiles_mouse) * TILE
    return pl.pallas_call(
        lambda *refs: heads_kernel(track_human, track_mouse, *refs),
        grid_spec=pltpu.PrefetchScalarGridSpec(
            num_scalar_prefetch=1,
            grid=(max(tiles_human, tiles_mouse),),
            in_specs=[
                pl.BlockSpec((bins, width), whole),
                pl.BlockSpec((8, bins), whole),
                pl.BlockSpec((TILE, share), lambda t, p: (human_tile(t, p), 0)),
                pl.BlockSpec((TILE, share), lambda t, p: (mouse_tile(t, p), 0)),
                pl.BlockSpec((TILE, rest), lambda t, p: (human_tile(t, p), 0)),
                pl.BlockSpec((TILE, rest), lambda t, p: (mouse_tile(t, p), 0)),
                pl.BlockSpec((TILE, 128), lambda t, p: (out_tile(t, p), 0)),
                pl.BlockSpec((1, TILE, bins), lambda t, p: (window, human_tile(t, p), 0)),
                pl.BlockSpec((1, TILE, bins), lambda t, p: (window, mouse_tile(t, p), 0)),
            ],
            out_specs=[
                pl.BlockSpec((TILE, bins), lambda t, p: (out_tile(t, p), 0)),
                pl.BlockSpec((bins, width), whole),
                pl.BlockSpec((8, TILE), lambda t, p: (0, out_tile(t, p))),
                pl.BlockSpec((8, bins), whole),
            ],
        ),
        out_shape=[
            jax.ShapeDtypeStruct((tracks, bins), jnp.bfloat16),
            jax.ShapeDtypeStruct((bins, width), jnp.float32),
            jax.ShapeDtypeStruct((8, tracks), jnp.float32),
            jax.ShapeDtypeStruct((8, bins), jnp.float32),
        ],
        compiler_params=pltpu.CompilerParams(vmem_limit_bytes=56 << 20),
        cost_estimate=pl.CostEstimate(
            flops=4 * bins * width * track_human,
            bytes_accessed=4 * width * track_human,
            transcendentals=4 * bins * track_human,
        ),
        name="score_heads",
    )(pick, rows, weight, *own, *others, bias, count_human, count_mouse)


def head_tile(step, parity, quarter):
    upper = jnp.where(step >= quarter, 1, 0)
    return upper * quarter + parity * quarter + step


def head_grads_kernel(windows, tiles_human, quarter, has_more, pick_ref, *refs):
    grads, rows, out_ref, acc_ref = refs[:windows], refs[windows], refs[-2], refs[-1]
    tile = head_tile(pl.program_id(0), pick_ref[windows], quarter)
    mine = jnp.where(tile < tiles_human, 0, 1)
    acc_ref[...] = refs[windows + 1][...].astype(jnp.float32) if has_more else jnp.zeros_like(acc_ref)
    for window in range(windows):

        @pl.when(pick_ref[window] == mine)
        def _():
            acc_ref[...] += mxu(grads[window][...], rows[window], NN)

    out_ref[...] = acc_ref[...].astype(jnp.bfloat16)


def head_grads(pick, grads, rows, tiles_human, tiles, more=None):
    windows, bins, share = rows.shape
    last = grads[0].shape[0] // TILE - 1

    def tile_of(window):
        def index(t, p):
            tile = head_tile(t, p[windows], tiles // 2)
            kept = jnp.where(p[window] == 0, jnp.minimum(tile, tiles_human - 1), 0)
            kept = jnp.where(p[window] == 1, jnp.maximum(tile, tiles_human), kept)
            return (jnp.minimum(kept, last), 0)

        return index

    extra = [] if more is None else [more]
    return pl.pallas_call(
        lambda *refs: head_grads_kernel(
            windows, tiles_human, tiles // 2, more is not None, *refs
        ),
        grid_spec=pltpu.PrefetchScalarGridSpec(
            num_scalar_prefetch=1,
            grid=(tiles,),
            in_specs=[pl.BlockSpec((TILE, bins), tile_of(w)) for w in range(windows)]
            + [pl.BlockSpec((windows, bins, share), lambda t, p: (0, 0, 0))]
            + [pl.BlockSpec((TILE, share), lambda t, p: (t, 0))] * len(extra),
            out_specs=pl.BlockSpec((TILE, share), lambda t, p: (t, 0)),
            scratch_shapes=[pltpu.VMEM((TILE, share), jnp.float32)],
        ),
        out_shape=jax.ShapeDtypeStruct((tiles * TILE, share), jnp.bfloat16),
        compiler_params=pltpu.CompilerParams(vmem_limit_bytes=40 << 20),
        cost_estimate=pl.CostEstimate(
            flops=2 * windows * bins * share * tiles * TILE,
            bytes_accessed=4 * tiles * TILE * share,
            transcendentals=0,
        ),
        name="head_grads",
    )(pick, *grads, rows, *extra)


def half_product_kernel(windows, turned, has_more, pick_ref, *refs):
    lefts, rights, out_ref = refs[:windows], refs[windows : 2 * windows], refs[-1]
    total = None
    for left, right in zip(lefts, rights):
        if turned:
            term = mxu(right[...], left[...], NN)
        else:
            term = mxu(left[...], right[...], TN)
        total = term if total is None else total + term
    if turned:
        total = total.T
    if has_more:
        total = total + refs[2 * windows][...].astype(jnp.float32)
    out_ref[...] = total.astype(jnp.bfloat16)


def half_product(half, lefts, rights, slabs, turned, more=None):
    windows = len(lefts)
    rows, width = lefts[0].shape
    slab = width // slabs
    cols = rights[0].shape[0 if turned else 1]
    step = cols
    while step > 768 and step % 256 == 0:
        step //= 2
    left_spec = pl.BlockSpec((rows, slab), lambda u, j, p: (0, 2 * u + p[0]))
    if turned:
        right_spec = pl.BlockSpec((step, rows), lambda u, j, p: (j, 0))
    else:
        right_spec = pl.BlockSpec((rows, step), lambda u, j, p: (0, j))
    out_spec = pl.BlockSpec((slab, step), lambda u, j, p: (u, j))
    extra = [] if more is None else [more]
    return pl.pallas_call(
        lambda *refs: half_product_kernel(windows, turned, more is not None, *refs),
        grid_spec=pltpu.PrefetchScalarGridSpec(
            num_scalar_prefetch=1,
            grid=(slabs // 2, cols // step),
            in_specs=[left_spec] * windows + [right_spec] * windows + [out_spec] * len(extra),
            out_specs=out_spec,
        ),
        out_shape=jax.ShapeDtypeStruct((width // 2, cols), jnp.bfloat16),
        compiler_params=pltpu.CompilerParams(vmem_limit_bytes=48 << 20),
        cost_estimate=pl.CostEstimate(
            flops=windows * rows * width * cols,
            bytes_accessed=windows * rows * (width + 2 * cols),
            transcendentals=0,
        ),
        name="half_product",
    )(half, *lefts, *rights, *extra)


def norm_stats(values):
    mean = jnp.mean(values, axis=-1, keepdims=True)
    centred = values - mean
    inverse = lax.rsqrt(jnp.mean(centred * centred, axis=-1, keepdims=True) + norm_eps)
    return mean, inverse


def norm_backward(grad_output, scaled, inverse, norm_gain):
    grad_scaled = grad_output * norm_gain
    mean_grad = jnp.mean(grad_scaled, axis=-1, keepdims=True)
    mean_proj = jnp.mean(grad_scaled * scaled, axis=-1, keepdims=True)
    grad_input = inverse * (grad_scaled - mean_grad - scaled * mean_proj)
    return (grad_input, jnp.sum(grad_output * scaled, axis=0), jnp.sum(grad_output, axis=0))


def sum_over_model(partial, done, after_line):
    low = done(partial.astype(jnp.bfloat16))
    if lax.axis_size("mp") == 2:
        other = lax.ppermute(low, "mp", [(0, 1), (1, 0)])
        return lambda: low.astype(jnp.float32) + after_line(other).astype(jnp.float32)
    total = lax.psum(low, "mp")
    return lambda: after_line(total).astype(jnp.float32)


def in_model_order(own, dim, after_line):
    if lax.axis_size("mp") == 2:
        first = lax.axis_index("mp") == 0
        other = lax.ppermute(own, "mp", [(0, 1), (1, 0)])

        def ordered():
            got = after_line(other)
            return jnp.concatenate(
                [jnp.where(first, own, got), jnp.where(first, got, own)], axis=dim
            )

        return ordered
    full = lax.all_gather(own, "mp", axis=dim, tiled=True)
    return lambda: after_line(full)


class OtherRows:
    def __init__(self, own, tile, after_line, done):
        self.after_line, self.done = after_line, done
        count = lax.axis_size("dp")
        size = -(-own.shape[0] // tile) * tile // count
        part = None
        for place in range(count - 1, -1, -1):
            piece = own[place * size : (place + 1) * size]
            piece = jnp.pad(piece, [(0, size - piece.shape[0]), (0, 0)])
            here = lax.axis_index("dp") == place
            part = piece if part is None else jnp.where(here, piece, part)
        self.mine = lax.ppermute(done(part), "mp", [(0, 1), (1, 0)])

    def share(self):
        self.full = lax.all_gather(
            self.done(self.after_line(self.mine)), "dp", axis=0, tiled=True
        )

    def finish(self):
        return self.after_line(self.full)


def swap_pairs(axis, step):
    return [(i, i ^ step) for i in range(lax.axis_size(axis))]


class SmallSums:
    def __init__(self, parts, axes, after_line, done):
        self.parts, self.after_line, self.done = parts, after_line, done
        padded = [jnp.pad(x.reshape(-1), (0, -x.size % 128)) for x in parts]
        self.total = jnp.concatenate(padded).reshape(-1, 128)
        self.moves = [
            (axis, 1 << bit)
            for axis in axes
            for bit in range(lax.axis_size(axis).bit_length() - 1)
        ]
        self.got = None
        self.step()

    def step(self):
        if self.got is not None:
            self.total, self.got = self.total + self.after_line(self.got), None
        if self.moves:
            axis, step = self.moves.pop(0)
            self.total = self.done(self.total)
            self.got = lax.ppermute(self.total, axis, swap_pairs(axis, step))

    def finish(self):
        while self.got is not None:
            self.step()
        results, start, total = [], 0, self.total.reshape(-1)
        for x in self.parts:
            results.append(total[start : start + x.size].reshape(x.shape))
            start += -(-x.size // 128) * 128
        return results


class SeqSum:
    def __init__(self, parts, done):
        self.got = lax.all_to_all(done(parts), "seq", split_axis=0, concat_axis=0, tiled=True)

    def arrive(self, after_line):
        self.got = after_line(self.got)

    def finish(self, after_line, done):
        return done(jnp.sum(after_line(self.got).astype(jnp.float32), axis=0))


class ScatterProduct:
    def __init__(self, lefts, rights, after_line, done, turned=False):
        self.after_line, self.done, self.turned = after_line, done, turned
        self.lefts, self.rights = lefts, rights
        lefts = [after_line(lefts[0])] + lefts[1:]
        self.got = lax.ppermute(done(self.half(1, lefts)), "dp", swap_pairs("dp", 1))

    def half(self, other, lefts, more=None):
        pick = jnp.reshape((lax.axis_index("dp") + other) % 2, (1,)).astype(jnp.int32)
        return half_product(pick, lefts, self.rights, lax.axis_size("dp"), self.turned, more)

    def keep(self):
        self.kept = self.done(self.half(0, self.lefts, self.after_line(self.got)))
        return self


class ScatterRest:
    def __init__(self, kept, after_line, done):
        self.after_line, self.done = after_line, done
        size = kept.shape[0] // 2
        upper = lax.axis_index("dp") // 2 == 1
        low, high = kept[:size], kept[size:]
        self.mine = jnp.where(upper, high, low)
        self.got = lax.ppermute(done(jnp.where(upper, low, high)), "dp", swap_pairs("dp", 2))

    def along_seq(self):
        got = self.after_line(self.got).astype(jnp.float32)
        total = (self.mine.astype(jnp.float32) + got).astype(jnp.bfloat16)
        parts = total.reshape(lax.axis_size("seq"), -1, total.shape[1])
        self.sum = SeqSum(parts, self.done)

    def arrive(self):
        self.sum.arrive(self.after_line)

    def finish(self):
        return self.sum.finish(self.after_line, self.done)


def on_device(
    trunk_in,
    norm1_gain,
    norm1_bias,
    w_query,
    w_key,
    w_value,
    w_rel,
    content_bias,
    pos_bias,
    w_out,
    b_out,
    norm2_gain,
    norm2_bias,
    w_in,
    b_in,
    w_hid,
    b_hid,
    head_human,
    bias_human,
    head_mouse,
    bias_mouse,
    species,
    targets_human,
    targets_mouse,
):
    windows, bins, width = trunk_in.shape
    heads = content_bias.shape[0]
    dp_size, seq_size, mp_size = (lax.axis_size(axis) for axis in ("dp", "seq", "mp"))
    seq_index, mp_index = lax.axis_index("seq"), lax.axis_index("mp")
    place = lax.axis_index("dp") * seq_size + seq_index
    places = dp_size * seq_size
    all_bins = bins * seq_size
    query_start = seq_index * bins
    key_scale = KD ** (-0.5)
    loss_scale = 1.0 / math.sqrt(windows * dp_size * CROP)
    crop_start = (all_bins - CROP) // 2
    bf16 = jnp.bfloat16
    me = jnp.reshape(seq_index, (1,)).astype(jnp.int32)

    groups = [[w] for w in range(windows)] if heads % seq_size == 0 else [list(range(windows))]
    group_size = len(groups[0])
    pairs = heads * group_size
    pairs_here = -(-pairs // seq_size)
    block = query_block(all_bins)
    pair_heads = [
        jnp.minimum((seq_index * pairs_here + j) // group_size, heads - 1)
        for j in range(pairs_here)
    ]

    tokens = [jnp.zeros((8, 128), jnp.float32)]

    def after_line(array):
        array, token = lax.optimization_barrier((array, tokens[-1]))
        tokens.append(token)
        return array

    done = after_line

    def exchange(array):
        return lax.all_to_all(array, "seq", split_axis=0, concat_axis=0, tiled=True)

    def spread(array):
        short = seq_size * pairs_here - pairs
        if short:
            array = jnp.pad(array, [(0, short)] + [(0, 0)] * (array.ndim - 1))
        return exchange(array.reshape((seq_size, pairs_here) + array.shape[1:]))

    def regroup(array, size):
        if array.shape[2] == size:
            return array
        depth = array.shape[1]
        array = array.transpose(1, 0, 2).reshape(depth, all_bins // size, size)
        return array.transpose(1, 0, 2)

    def to_owners(arrays):
        return exchange(jnp.stack([regroup(a, bins) for a in arrays], axis=1))

    def by_head(array):
        depth = array.shape[2]
        array = array.reshape(seq_size * pairs_here, depth, bins)[:pairs]
        array = array.reshape(heads, group_size, depth, bins).transpose(0, 2, 1, 3)
        return array.reshape(heads * depth, group_size * bins)

    track_human, track_mouse = head_human.shape[1], head_mouse.shape[1]
    own_heads = (head_human.T, head_mouse.T)
    parts = {}

    def fetch_out(_):
        if mp_size == 2:
            parts["out"] = OtherRows(w_out, w_out.shape[0], after_line, done)

    def fetch_out_share(_):
        if mp_size == 2:
            parts["out"].share()

    def fetch_out_end(_):
        if mp_size != 2:
            parts["w_out"] = lax.all_gather(w_out, "mp", axis=0, tiled=True)
            return
        other, first = parts["out"].finish(), mp_index == 0
        parts["w_out"] = done(
            jnp.concatenate(
                [jnp.where(first, w_out, other), jnp.where(first, other, w_out)], axis=0
            )
        )

    def fetch_heads(_):
        if mp_size == 2:
            parts["heads"] = [OtherRows(own, TILE, after_line, done) for own in own_heads]

    def fetch_heads_share(_):
        if mp_size == 2:
            for part in parts["heads"]:
                part.share()

    def fetch_heads_end(_):
        if mp_size == 2:
            parts["others"] = [part.finish() for part in parts["heads"]]
            parts["own"] = own_heads
            return
        full = [lax.all_gather(own, "mp", axis=1, tiled=True) for own in own_heads]
        parts["own"] = [x[:, : width // 2] for x in full]
        parts["others"] = [x[:, width // 2 :] for x in full]

    def of_head(weight, size, h):
        return weight[:, h * size : (h + 1) * size]

    w_packs = [
        jnp.concatenate(
            [of_head(w_value, VD, h), of_head(w_key, KD, h)] + [of_head(w_query, KD, h)] * 2, axis=1
        )
        for h in range(heads)
    ]
    w_grad = jnp.concatenate([w[:, :GRAD_PACK] for w in w_packs], axis=1)
    pack_scale = jnp.concatenate(
        [jnp.ones((VD + KD,), jnp.float32), jnp.full((2 * KD,), key_scale, jnp.float32)]
    )
    pack_biases = [
        jnp.concatenate([jnp.zeros((VD + KD,), jnp.float32), content_bias[h], pos_bias[h]])
        for h in range(heads)
    ]

    basis = jnp.pad(rel_basis(), [(0, 1), (0, 0)])
    w_rel_heads = w_rel.reshape(FEAT, heads, KD)
    rels = [
        mxu(
            basis,
            lax.dynamic_index_in_dim(w_rel_heads, head, 1, keepdims=False).astype(jnp.float32),
            NN,
            exact_mode,
        ).astype(bf16)
        for head in pair_heads
    ]

    count = len(groups)
    many = lambda: [None] * count
    trunk, stats1, normed1, packs, probs, attended = many(), many(), many(), many(), many(), many()
    mids, stats2, normed2, preacts, actives = many(), many(), many(), many(), many()
    trunk_out, grad_trunks, grad_outs, grad_pres = many(), many(), many(), many()
    grad_mids, grad_mid_lows, packed_grads, grad_inputs = many(), many(), many(), many()
    moving, grad_att, own_rows = many(), many(), [None] * windows
    logit_grads, track_sums, losses = [None] * windows, [], []
    sums = [0.0] * 5
    sums1 = [0.0, 0.0]
    drels = [0.0] * pairs_here
    dstats = [0.0] * pairs_here

    def project(g):
        rows = group_size * bins
        values = trunk_in[groups[g][0] : groups[g][-1] + 1].reshape(rows, width).astype(jnp.float32)
        mean, inverse = norm_stats(values)
        normed = ((values - mean) * inverse * norm1_gain + norm1_bias).astype(bf16)
        normed = after_line(normed)
        trunk[g], stats1[g], normed1[g] = values, (mean, inverse), normed
        parts = []
        for h in range(heads):
            pack = (mxu(normed, w_packs[h], NN) * pack_scale + pack_biases[h]).astype(bf16)
            parts.append(pack.reshape(group_size, bins, PACK))
        pack = spread(done(jnp.concatenate(parts, axis=0)))
        packs[g] = pack

    def arrive(g):
        packs[g] = after_line(packs[g])

    def arrive_out(g):
        moving[g] = after_line(moving[g])

    def arrive_grad(g):
        grad_att[g] = after_line(grad_att[g])

    def arrive_packed(g):
        packed_grads[g] = by_head(after_line(packed_grads[g]))

    def attend(g):
        outs, kept = [], []
        pack = after_line(packs[g])
        packs[g] = [pack[:, j].reshape(all_bins, PACK) for j in range(pairs_here)]
        for j in range(pairs_here):
            out, prob = attend_forward(packs[g][j], rels[j])
            outs.append(done(out))
            kept.append(prob)
        probs[g] = kept
        moving[g] = to_owners(outs)

    def attend_swap(g):
        attended[g] = done(by_head(after_line(moving[g])))
        moving[g] = in_model_order(attended[g], 0, after_line)

    def feed_forward(g):
        mid = trunk[g] + mxu(moving[g](), parts["w_out"], TN) + b_out
        mean, inverse = norm_stats(mid)
        normed = ((mid - mean) * inverse * norm2_gain + norm2_bias).astype(bf16)
        preact = mxu(normed, w_in, NN) + b_in
        active = jnp.maximum(preact, 0.0).astype(bf16)
        mids[g], stats2[g], normed2[g], actives[g] = mid, (mean, inverse), normed, active
        moving[g] = sum_over_model(mxu(active, w_hid, NN), done, after_line)

    def score(g):
        out = mids[g] + (moving[g]() + b_hid)
        trunk_out[g] = out
        low = out.astype(bf16)
        grads = []
        for i, window in enumerate(groups[g]):
            rows = low[i * bins : (i + 1) * bins]
            own_rows[window] = lax.dynamic_slice_in_dim(rows, mp_index * share, share, 1)
            pick = jnp.stack([picks[window], jnp.int32(0) + order])
            logit_grads[window], grad_out, track_sum, loss = score_heads(
                window, pick, rows, weight, parts["own"], parts["others"], bias_rows[0], count_human, count_mouse
            )
            track = jnp.sum(track_sum, axis=0)
            scored = jnp.arange(track.size) < tiles_human * TILE
            scored = scored == (picks[window] == 0)
            track_sums.append(jnp.where(scored & (picks[window] < 2), track, 0.0))
            losses.append(jnp.sum(loss))
            grads.append(grad_out)
        grad_trunks[g] = done(jnp.concatenate(grads, axis=0))

    def back_hidden(g):
        grad_out = after_line(grad_trunks[g].astype(bf16))
        grad_preact = jnp.where(actives[g] > 0, mxu(grad_out, w_hid, NT), 0.0)
        grad_pre = grad_preact.astype(bf16)
        grad_outs[g], grad_pres[g] = grad_out, grad_pre
        sums[3] = sums[3] + jnp.sum(grad_trunks[g], axis=0)
        sums[4] = sums[4] + jnp.sum(grad_preact, axis=0)
        moving[g] = sum_over_model(mxu(grad_pre, w_in, NT), done, after_line)

    def back_mid(g):
        mean, inverse = stats2[g]
        grad_normed = moving[g]()
        grad_norm, dgain, dbias = norm_backward(
            grad_normed, (mids[g] - mean) * inverse, inverse, norm2_gain
        )
        grad_mids[g] = grad_trunks[g] + grad_norm
        grad_mid_lows[g] = grad_mids[g].astype(bf16)
        sums[0] = sums[0] + dgain
        sums[1] = sums[1] + dbias
        sums[2] = sums[2] + jnp.sum(grad_mids[g], axis=0)
        grad = done(mxu(w_out, grad_mid_lows[g], NT).astype(bf16))
        grad = grad.reshape(heads, VD, group_size, bins).transpose(0, 2, 1, 3)
        grad_att[g] = spread(grad.reshape(pairs, VD, bins))

    def back_attend(g):
        outs = []
        grad = after_line(grad_att[g])
        for j in range(pairs_here):
            out, drel, stat = attend_backward(
                packs[g][j], rels[j], probs[g][j], regroup(grad[:, j], block)
            )
            outs.append(done(out))
            drels[j] = drels[j] + drel
            dstats[j] = dstats[j] + stat
        packed_grads[g] = to_owners(outs)

    def back_project(g):
        packed_grads[g] = after_line(packed_grads[g])
        product = lax.dot_general(
            packed_grads[g],
            w_grad,
            (((0,), (1,)), ((), ())),
            preferred_element_type=jnp.float32,
        )
        moving[g] = sum_over_model(product, done, after_line)

    def back_input(g):
        mean, inverse = stats1[g]
        grad_norm, dgain, dbias = norm_backward(
            moving[g](), (trunk[g] - mean) * inverse, inverse, norm1_gain
        )
        sums1[0] = sums1[0] + dgain
        sums1[1] = sums1[1] + dbias
        grad_inputs[g] = (grad_mids[g] + grad_norm).reshape(group_size, bins, width)

    bin_place = query_start + jnp.arange(bins)
    in_crop = ((bin_place >= crop_start) & (bin_place < crop_start + CROP)).astype(jnp.float32)
    weight = jnp.broadcast_to((in_crop * loss_scale)[None, :], (8, bins))
    has_crop = (query_start + bins > crop_start) & (query_start < crop_start + CROP)
    picks = jnp.where(has_crop, species, 2)
    count_human = targets_human.transpose(0, 2, 1)
    count_mouse = targets_mouse.transpose(0, 2, 1)
    tiles_human, tiles_mouse = pl.cdiv(track_human, TILE), pl.cdiv(track_mouse, TILE)
    half_tiles = (tiles_human + tiles_mouse) // 2
    bias_all = jnp.concatenate(
        [
            jnp.pad(bias_human, (0, tiles_human * TILE - track_human)),
            jnp.pad(bias_mouse, (0, tiles_mouse * TILE - track_mouse)),
        ]
    )
    bias_rows = []

    def spread_bias(_):
        wide = jnp.broadcast_to(after_line(bias_all)[:, None], (bias_all.size, 128))
        bias_rows.append(done(wide))

    order = mp_index if mp_size == 2 else 0
    share = head_human.shape[0]
    join = lambda arrays: jnp.concatenate(arrays, axis=0)
    results = {}
    width_out = heads * VD

    def pick_half(half):
        return jnp.concatenate([picks, jnp.reshape(half, (1,)).astype(jnp.int32)])

    def grads_heads(_):
        parity = lax.axis_index("dp") % 2
        rows = jnp.stack(own_rows)
        grads = [after_line(logit_grads[0])] + logit_grads[1:]
        sent = head_grads(pick_half(1 - parity), grads, rows, tiles_human, half_tiles)
        got = lax.ppermute(done(sent), "dp", swap_pairs("dp", 1))
        results["heads"] = (grads, rows, got, parity)

    def grads_heads_keep(_):
        grads, rows, got, parity = results["heads"]
        kept = done(
            head_grads(pick_half(parity), grads, rows, tiles_human, half_tiles, after_line(got))
        )
        results["heads"] = ScatterRest(kept, after_line, done)

    def grads_heads_seq(_):
        results["heads"].along_seq()

    def heads_arrive(_):
        results["heads"].arrive()

    def wide_arrive(_):
        results["wide"].arrive()

    def grads_heads_end(_):
        total = results["heads"].finish().astype(bf16)
        results["heads"] = lax.all_gather(total, ("dp", "seq"), axis=0, tiled=True)

    def grads_in(_):
        results["in"] = ScatterProduct(normed2, grad_pres, after_line, done)

    def grads_hid(_):
        results["hid"] = ScatterProduct(grad_outs, actives, after_line, done)

    def grads_in_keep(_):
        results["in"].keep()

    def grads_hid_keep(_):
        results["hid"].keep()
        kept = jnp.concatenate([results["in"].kept, results["hid"].kept], axis=1)
        results["wide"] = ScatterRest(kept, after_line, done)

    def grads_wide_seq(_):
        results["wide"].along_seq()

    def grads_wide_end(_):
        results["wide"] = results["wide"].finish()

    def grads_out(_):
        results["out"] = ScatterProduct(grad_mid_lows, attended, after_line, done, True)

    def grads_out_keep(_):
        results["out"].keep()

    def grads_pack(_):
        results["pack"] = ScatterProduct(normed1, packed_grads, after_line, done, True)

    def grads_pack_keep(_):
        kept = jnp.concatenate([results["out"].kept, results["pack"].keep().kept], axis=1)
        results["late_rows"] = ScatterRest(kept, after_line, done)

    def grads_pack_seq(_):
        results["late_rows"].along_seq()

    def grads_pack_end(_):
        late = results["late_rows"].finish()
        results["out"], results["pack"] = late[:, :width_out], late[:, width_out:]

    def sums_early(_):
        values = list(sums) + [sum(track_sums), sum(losses)[None]]
        results["early"] = SmallSums(values, ("seq", "dp"), after_line, done)

    def sums_heads(_):
        dw_rel = jnp.zeros((heads, FEAT, KD), jnp.float32)
        dstat = jnp.zeros((heads, 2, KD), jnp.float32)
        for j, head in enumerate(pair_heads):
            part = lax.dot_general(
                basis,
                drels[j],
                (((0,), (1,)), ((), ())),
                precision=exact_mode,
                preferred_element_type=jnp.float32,
            )
            mine = (jnp.arange(heads) == head).astype(jnp.float32)[:, None, None]
            dw_rel = dw_rel + mine * part
            dstat = dstat + mine * dstats[j][None, :2, :KD]
        values = [part, dstats[0]] if heads == seq_size else [dstat, dw_rel]
        axes = ("dp",) if heads == seq_size else ("dp", "seq")
        results["own_head"] = SmallSums(values, axes, after_line, done)

    def sums_late(_):
        results["late"] = SmallSums(list(sums1), ("dp", "seq"), after_line, done)

    def step_early(_):
        results["early"].step()

    def step_heads(_):
        results["own_head"].step()

    def step_late(_):
        results["late"].step()

    def heads_out(_):
        full = after_line(results["heads"])
        first = tiles_human * TILE
        results["human"] = done(full[:track_human].astype(jnp.float32))
        results["mouse"] = done(full[first : first + track_mouse].astype(jnp.float32))

    def each(stage):
        return [(stage, g) for g in range(count)]

    def one(*stages):
        return [(stage, -1) for stage in stages]

    if count == 3:
        plan = one(fetch_out) + [(project, 0)] + one(fetch_out_share, fetch_heads)
        plan += [(project, 1), (project, 2)] + one(spread_bias) + [(attend, 0), (attend, 1)]
        plan += one(fetch_heads_share) + [(attend_swap, 0)] + one(fetch_out_end)
        plan += [(feed_forward, 0), (attend, 2), (attend_swap, 1), (feed_forward, 1)]
        plan += [(attend_swap, 2)] + one(fetch_heads_end)
        plan += [(score, 0), (feed_forward, 2), (back_hidden, 0)]
        plan += [(score, 1), (back_hidden, 1), (back_mid, 0), (score, 2)]
        plan += one(grads_heads) + [(arrive_grad, 0), (back_attend, 0), (back_hidden, 2)]
        plan += one(grads_heads_keep) + [(back_mid, 1), (arrive_packed, 0)] + one(grads_in)
        plan += [(arrive_grad, 1), (back_attend, 1)] + one(grads_in_keep) + [(back_mid, 2)]
        plan += one(sums_early) + [(back_project, 0), (arrive_packed, 1)] + one(step_early, grads_hid)
        plan += [(arrive_grad, 2)] + one(step_early, grads_heads_seq) + [(back_attend, 2)]
        plan += one(grads_hid_keep, step_early) + [(back_project, 1), (back_input, 0)]
        plan += one(grads_out, step_early, sums_heads, grads_out_keep, step_heads)
        plan += one(heads_arrive, grads_heads_end) + [(back_input, 1), (arrive_packed, 2)]
        plan += one(grads_pack) + [(back_project, 2)]
        plan += one(grads_wide_seq, step_heads, grads_pack_keep) + [(back_input, 2)]
        plan += one(sums_late, wide_arrive, step_late, grads_pack_seq, step_late, heads_out)
        plan += one(grads_wide_end, step_late, grads_pack_end, step_late)
    else:
        plan = one(fetch_out, fetch_out_share, fetch_out_end, spread_bias)
        plan += one(fetch_heads, fetch_heads_share, fetch_heads_end)
        plan += each(project) + each(attend) + each(attend_swap) + each(feed_forward) + each(score)
        plan += each(back_hidden) + each(back_mid)
        plan += one(grads_heads, grads_heads_keep, grads_heads_seq, grads_heads_end)
        plan += each(back_attend) + one(grads_in, grads_in_keep, grads_hid, grads_hid_keep)
        plan += one(grads_wide_seq, grads_wide_end, grads_out, grads_out_keep)
        plan += each(arrive_packed) + each(back_project) + one(grads_pack, grads_pack_keep)
        plan += one(grads_pack_seq, grads_pack_end) + each(back_input)
        plan += one(sums_early, sums_heads, sums_late, heads_out)
    for stage, g in plan:
        stage(g)
    dgain2, dbias2, db_out, db_hid, db_in, dtracks, loss = results["early"].finish()
    dgain1, dbias1 = results["late"].finish()
    mids_sum = results["own_head"].finish()
    if heads == seq_size:
        share_rel, share_stat = FEAT // places, KD // places
        own_rel = mids_sum[0].reshape(dp_size, seq_size, share_rel * KD)
        own_stat = mids_sum[1][:2, :KD].reshape(2, dp_size, seq_size, share_stat)
        dp_here = lax.axis_index("dp")
        own_rel = lax.dynamic_index_in_dim(own_rel, dp_here, 0, keepdims=False)
        own_stat = lax.dynamic_index_in_dim(own_stat, dp_here, 1, keepdims=False)
        own_stat = own_stat.transpose(1, 0, 2).reshape(seq_size, 2 * share_stat)
        small = jnp.concatenate([own_rel, own_stat], axis=1)
        small = jnp.pad(small, [(0, 0), (0, -small.shape[1] % 128)])
        small = lax.all_to_all(small[:, None], "seq", split_axis=0, concat_axis=0, tiled=True)[:, 0]
        rel_rows = small[:, : share_rel * KD].reshape(heads, share_rel, KD)
        rel_rows = rel_rows.transpose(1, 0, 2).reshape(share_rel, heads * KD)
        stats = small[:, share_rel * KD : share_rel * KD + 2 * share_stat]
        dstat = stats.reshape(heads, 2, share_stat)
        dcontent, dposition = dstat[:, 0], dstat[:, 1]
    else:
        dstat, dw_rel = mids_sum
    dw_out = results["out"]
    dw_in, dw_hid = jnp.split(results["wide"], 2, axis=1)
    pack_summed = results["pack"].reshape(-1, heads, GRAD_PACK)
    def own(array, dim=0):
        size = array.shape[dim] // places
        return lax.dynamic_slice_in_dim(array, place * size, size, dim)

    if heads != seq_size:
        rel_rows = own(dw_rel, 1).transpose(1, 0, 2).reshape(-1, heads * KD)
        dcontent, dposition = own(dstat[:, 0], 1), own(dstat[:, 1], 1)
    pack_rows = pack_summed.shape[0]
    mouse_start = tiles_human * TILE
    shape3 = (windows, bins, width)
    return (
        join(trunk_out).reshape(shape3),
        loss[0] + tokens[-1][0, 0],
        join(grad_inputs).reshape(shape3),
        own(dgain1),
        own(dbias1),
        pack_summed[:, :, VD + KD :].reshape(pack_rows, heads * KD),
        pack_summed[:, :, VD : VD + KD].reshape(pack_rows, heads * KD),
        pack_summed[:, :, :VD].reshape(pack_rows, heads * VD),
        rel_rows,
        dcontent,
        dposition,
        dw_out.T,
        own(db_out),
        own(dgain2),
        own(dbias2),
        dw_in,
        db_in,
        dw_hid.T,
        own(db_hid),
        results["human"].T,
        dtracks[:track_human],
        results["mouse"].T,
        dtracks[mouse_start : mouse_start + track_mouse],
    )


def solution(mesh):
    in_specs = (
        P("dp", "seq", None),
        P(),
        P(),
        P(None, "mp"),
        P(None, "mp"),
        P(None, "mp"),
        P(None, "mp"),
        P("mp", None),
        P("mp", None),
        P("mp", None),
        P(),
        P(),
        P(),
        P(None, "mp"),
        P("mp"),
        P("mp", None),
        P(),
        P("mp", None),
        P(),
        P("mp", None),
        P(),
        P("dp"),
        P("dp", "seq", None),
        P("dp", "seq", None),
    )
    out_specs = (
        P("dp", "seq", None),
        P(),
        P("dp", "seq", None),
        P(("dp", "seq")),
        P(("dp", "seq")),
        P(("dp", "seq"), "mp"),
        P(("dp", "seq"), "mp"),
        P(("dp", "seq"), "mp"),
        P(("dp", "seq"), "mp"),
        P("mp", ("dp", "seq")),
        P("mp", ("dp", "seq")),
        P("mp", ("dp", "seq")),
        P(("dp", "seq")),
        P(("dp", "seq")),
        P(("dp", "seq")),
        P(("dp", "seq"), "mp"),
        P("mp"),
        P("mp", ("dp", "seq")),
        P(("dp", "seq")),
        P("mp", None),
        P(),
        P("mp", None),
        P(),
    )
    return jax.shard_map(
        on_device, mesh=mesh, in_specs=in_specs, out_specs=out_specs, check_vma=False
    )
```

time: 995 us -> 904 us (0.909); the launches traced: 993 us -> 891 us
  waiting for transfers between devices: 302 us -> 186 us
  Pallas kernels: 193 us -> 223 us
  starting transfers between devices: 127 us -> 100 us
  other arithmetic: 128 us -> 154 us
  local copies, waits for them, and re-layouts: 115 us -> 99.8 us
    ppermute x67 -> x21, waiting for transfers between devices: 145 us -> 29 us  [the longest x3 17.3 us: __init__(): self.mine = lax.ppermute(done(part), 'mp', [(0, 1), (1, 0)])]
    ppermute x67 -> x21, starting transfers between devices: 113 us -> 19 us  [the longest x10 10.3 us: step(): self.got = lax.ppermute(self.total, axis, swap_pairs(axis, step))]
    all_to_all x0 -> x16, waiting for transfers between devices: none -> 93.8 us  [the longest x3 48.7 us: __init__(): lax.all_to_all(done(parts), 'seq', split_axis=0, concat_axis=0, tiled=True)]
    ppermute x9, waiting for transfers between devices: 131 us -> 37.6 us  [sum_over_model(): other = lax.ppermute(low, 'mp', [(0, 1), (1, 0)])]
    all_to_all x0 -> x16, starting transfers between devices: none -> 70.9 us  [the longest x12 54.4 us: exchange(): return lax.all_to_all(array, 'seq', split_axis=0, concat_axis=0, tiled=True)]
    pallas_call x4 -> x13, Pallas kernels: 108 us -> 137 us  [the longest x3 67 us: score_heads(): pl.pallas_call(lambda *refs: heads_kernel(track_human, track_mouse, *refs...]
    transpose x4 -> x0, other arithmetic: 18.3 us -> none  [the longest x1 11 us: on_device(): dheads[:track_human].astype(jnp.float32)]
    dynamic_update_slice x36 -> x0, local copies, waits for them, and re-layouts: 18.2 us -> none  [exchange(): result = lax.dynamic_update_slice_in_dim(result, block_in, other, 0)]
  transfers between devices with their start and end apart: 83 -> 53, of which waited for: 32 -> 22; matrix products, arithmetic and copies ran while one was open for 30% -> 33% of each run, Pallas kernels for 9% -> 19%
where the time goes in v3:
time: 904 us; the launch traced here: 891 us
  Pallas kernels  223 us (25%)
  waiting for transfers between devices  186 us (21%)
  other arithmetic  154 us (17%)
  matrix products  103 us (11%)
  starting transfers between devices  100 us (11%)
  local copies, waits for them, and re-layouts  99.8 us (11%)
  between operations  25 us (3%)
    dot_general x31, matrix products, mxu(): lax.dot_general(left_arr, right_arr, dims, precision=precision, preferred...  90.8 us
    pallas_call x3, Pallas kernels, score_heads(): pl.pallas_call(lambda *refs: heads_kernel(track_human, track_mouse, *refs...  67 us
    all_to_all x12, starting transfers between devices, exchange(): return lax.all_to_all(array, 'seq', split_axis=0, concat_axis=0, tiled=True)  54.4 us
    pallas_call x3, Pallas kernels, attend_backward(): pl.pallas_call(lambda *refs: attend_backward_kernel(block, bins, *refs),...  54.3 us
    unnamed x462, local copies, waits for them, and re-layouts  54.2 us
    pallas_call x8, Pallas kernels, half_product(): pl.pallas_call(lambda *refs: half_product_kernel(windows, turned, more is...  52.9 us
    all_to_all x3, waiting for transfers between devices, __init__(): lax.all_to_all(done(parts), 'seq', split_axis=0, concat_axis=0, tiled=True)  48.7 us
    all_to_all x12, waiting for transfers between devices, exchange(): return lax.all_to_all(array, 'seq', split_axis=0, concat_axis=0, tiled=True)  41.7 us
  transfers between devices with their start and end apart: 53, of which 22 were waited for; matrix products, arithmetic and copies ran while one was open for 33% of the time, Pallas kernels for 19%

profile of v3, /device:TPU:0, one launch (start us, length us, event | category | flops | bytes accessed | tf_op | source)
XLA Modules:
  0.0 891.2 jit_solution(1368878179202805418)
XLA Ops:
  75.9 10.4 %attend_forward.3 = (bf16[4,192,384]{2,1,0:T(8,128)(2,1)}, bf16[1536,1536]{1,0:T(8,128)(2,1)}) custom-call(bf16[1536,384]{1,0:T(8,128)(2,1)S(1)} %bitcast.362, bf16[3072,64]{1,0:T(8,128)(2,1)S(1)} %convolution_convert_fusion.refs_1_), custom_call_target="tpu_custom_call" | custom-call | flops 4831838208 | bytes 4718592 | tf_op jit(solution)/shard_map/attend_forward/pallas_call | solution.py:84
  91.1 10.4 %attend_forward.4 = (bf16[4,192,384]{2,1,0:T(8,128)(2,1)}, bf16[1536,1536]{1,0:T(8,128)(2,1)}) custom-call(bf16[1536,384]{1,0:T(8,128)(2,1)S(1)} %bitcast.360, bf16[3072,64]{1,0:T(8,128)(2,1)S(1)} %convolution_convert_fusion.refs_1_), custom_call_target="tpu_custom_call" | custom-call | flops 4831838208 | bytes 4718592 | tf_op jit(solution)/shard_map/attend_forward/pallas_call | solution.py:84
  109.9 14.4 %collective-permute-done.1 = bf16[448,768]{1,0:T(8,128)(2,1)S(1)} collective-permute-done((bf16[448,768]{1,0:T(8,128)(2,1)S(1)}, bf16[448,768]{1,0:T(8,128)(2,1)S(1)}, u32[]{:S(2)}, u32[]{:S(2)}) %collective-permute-start.1) | collective-permute-done | bytes 688160 | tf_op jit(solution)/shard_map/ppermute | solution.py:471
  134.3 8.0 collective-permute-done.3
  164.4 10.2 %attend_forward.5 = (bf16[4,192,384]{2,1,0:T(8,128)(2,1)S(1)}, bf16[1536,1536]{1,0:T(8,128)(2,1)}) custom-call(bf16[1536,384]{1,0:T(8,128)(2,1)S(1)} %bitcast.358, bf16[3072,64]{1,0:T(8,128)(2,1)S(1)} %copy-done.63), custom_call_target="tpu_custom_call" | custom-call | flops 4831838208 | bytes 4718592 | tf_op jit(solution)/shard_map/attend_forward/pallas_call | solution.py:84
  208.4 8.6 collective-permute-done.4
  222.9 16.5 %score_heads.3 = (bf16[7168,384]{1,0:T(8,128)(2,1)}, f32[384,1536]{1,0:T(8,128)}, f32[8,7168]{1,0:T(8,128)}, f32[8,384]{1,0:T(8,128)}) custom-call(s32[2]{0:T(128)} %get-tuple-element.845.refs_0_, bf16[384,1536]{1,0:T(8,128)(2,1)} %get-tuple-element.764.refs_1_, f32[8,384]{1,0:T(8,128)} %broadcast_in_dim.29.refs_2_, bf16[5313,768]{1,0:T(8,128)(2,1)} %bitcast.373, ...), custom_call_target="tpu_custom_call" | custom-call | flops 12534939648 | bytes 32643072 | tf_op jit(solution)/shard_map/score_heads/pallas_call | solution.py:274
  239.4 13.1 %collective-permute-done.7 = bf16[768,384]{1,0:T(8,128)(2,1)S(1)} collective-permute-done((bf16[768,384]{1,0:T(8,128)(2,1)S(1)}, bf16[768,384]{1,0:T(8,128)(2,1)S(1)}, u32[]{:S(2)}, u32[]{:S(2)}) %collective-permute-start.7) | collective-permute-done | bytes 589856 | tf_op jit(solution)/shard_map/ppermute | solution.py:447
  278.9 16.7 %score_heads.4 = (bf16[7168,384]{1,0:T(8,128)(2,1)}, f32[384,1536]{1,0:T(8,128)}, f32[8,7168]{1,0:T(8,128)}, f32[8,384]{1,0:T(8,128)}) custom-call(s32[2]{0:T(128)} %get-tuple-element.846.refs_0_, bf16[384,1536]{1,0:T(8,128)(2,1)} %get-tuple-element.762.refs_1_, f32[8,384]{1,0:T(8,128)} %broadcast_in_dim.29.refs_2_, bf16[5313,768]{1,0:T(8,128)(2,1)} %bitcast.374, ...), custom_call_target="tpu_custom_call" | custom-call | flops 12534939648 | bytes 32643072 | tf_op jit(solution)/shard_map/score_heads/pallas_call | solution.py:274
  321.7 8.9 collective-permute-done.8
  335.2 33.9 %score_heads.5 = (bf16[7168,384]{1,0:T(8,128)(2,1)}, f32[384,1536]{1,0:T(8,128)}, f32[8,7168]{1,0:T(8,128)}, f32[8,384]{1,0:T(8,128)}) custom-call(s32[2]{0:T(128)} %pad_add_fusion.3.refs_0_, bf16[384,1536]{1,0:T(8,128)(2,1)} %copy-done.95, f32[8,384]{1,0:T(8,128)} %broadcast_in_dim.29.refs_2_, bf16[5313,768]{1,0:T(8,128)(2,1)} %bitcast.375, ...), custom_call_target="tpu_custom_call" | custom-call | flops 12534939648 | bytes 32643072 | tf_op jit(solution)/shard_map/score_heads/pallas_call | solution.py:274
  370.6 9.9 %head_grads.2 = bf16[3584,768]{1,0:T(8,128)(2,1)} custom-call(s32[4]{0:T(128)S(1)} %get-tuple-element.831.refs_0_, bf16[7168,384]{1,0:T(8,128)(2,1)S(1)} %bitcast.337, bf16[7168,384]{1,0:T(8,128)(2,1)} %get-tuple-element.416.refs_2_, bf16[7168,384]{1,0:T(8,128)(2,1)} %get-tuple-element.417.refs_3_, bf16[3,384,768]{2,1,0:T(8,128)(2,1)S(1)} %pad_maximum_fusion.3.refs_4_), custom_call_target="tpu_custom_call" | custom-call | flops 6341787648 | bytes 11010048 | tf_op jit(solution)/shard_map/head_grads/pallas_call | solution.py:346
  390.1 13.0 %all-to-all-done.6 = bf16[4,1,192,384]{3,2,1,0:T(8,128)(2,1)S(1)} async-done(((bf16[4,1,192,384]{3,2,1,0:T(8,128)(2,1)}), bf16[4,1,192,384]{3,2,1,0:T(8,128)(2,1)S(1)}, u32[]{:S(2)}, u32[]{:S(2)}) %all-to-all-start.6) | async-done | bytes 589856 | tf_op jit(solution)/shard_map/all_to_all | solution.py:626
  405.5 17.7 %attend_backward.3 = (bf16[4,320,384]{2,1,0:T(8,128)(2,1)S(1)}, f32[64,3072]{1,0:T(8,128)S(1)}, f32[8,128]{1,0:T(8,128)S(1)}) custom-call(bf16[1536,384]{1,0:T(8,128)(2,1)S(1)} %bitcast.363, bf16[3072,64]{1,0:T(8,128)(2,1)S(1)} %copy-done.64, bf16[1536,1536]{1,0:T(8,128)(2,1)} %get-tuple-element.421.refs_2_, bf16[4,192,384]{2,1,0:T(8,128)(2,1)S(1)} %bitcast.367), custom_call_target="tpu_custom_call" | custom-call | flops 9663676416 | bytes 4718592 | tf_op jit(solution)/shard_map/attend_backward/pallas_call | solution.py:165
  434.4 6.0 convolution_convert_fusion.1
  440.4 7.7 head_grads.3
  467.6 7.0 half_product.8
  486.7 9.2 %concatenate.148 = bf16[1536,1280]{1,0:T(8,128)(2,1)} concatenate(bf16[1536,192]{1,0:T(8,128)(2,1)} %copy-done.103, bf16[1536,64]{1,0:T(8,128)(2,1)} %copy-done.115, bf16[1536,64]{1,0:T(8,128)(2,1)} %copy-done.130, bf16[1536,192]{1,0:T(8,128)(2,1)} %copy-done.106, bf16[1536,64]{1,0:T(8,128)(2,1)} %copy-done.116, bf16[1536,64]{1,0:T(8,128)(2,1)} %copy-done.127, ...), dimensions={1} | concatenate | bytes 7864320 | tf_op jit(solution)/shard_map/concatenate | solution.py:700
  503.9 17.7 %attend_backward.4 = (bf16[4,320,384]{2,1,0:T(8,128)(2,1)S(1)}, f32[64,3072]{1,0:T(8,128)S(1)}, f32[8,128]{1,0:T(8,128)S(1)}) custom-call(bf16[1536,384]{1,0:T(8,128)(2,1)S(1)} %bitcast.361, bf16[3072,64]{1,0:T(8,128)(2,1)S(1)} %copy-done.65, bf16[1536,1536]{1,0:T(8,128)(2,1)} %get-tuple-element.445.refs_2_, bf16[4,192,384]{2,1,0:T(8,128)(2,1)} %bitcast.64.refs_3_), custom_call_target="tpu_custom_call" | custom-call | flops 9663676416 | bytes 4718592 | tf_op jit(solution)/shard_map/attend_backward/pallas_call | solution.py:165
  535.0 7.5 half_product.9
  582.9 7.1 half_product.10
  599.0 6.0 add_convert_fusion
  611.0 18.8 %attend_backward.5 = (bf16[4,320,384]{2,1,0:T(8,128)(2,1)}, f32[64,3072]{1,0:T(8,128)S(1)}, f32[8,128]{1,0:T(8,128)S(1)}) custom-call(bf16[1536,384]{1,0:T(8,128)(2,1)S(1)} %bitcast.359, bf16[3072,64]{1,0:T(8,128)(2,1)S(1)} %copy-done.66, bf16[1536,1536]{1,0:T(8,128)(2,1)} %get-tuple-element.486.refs_2_, bf16[4,192,384]{2,1,0:T(8,128)(2,1)} %bitcast.80.refs_3_), custom_call_target="tpu_custom_call" | custom-call | flops 9663676416 | bytes 4718592 | tf_op jit(solution)/shard_map/attend_backward/pallas_call | solution.py:165
  629.9 7.3 half_product.11
  682.8 5.9 pad_maximum_fusion
  693.8 16.0 %collective-permute-done.21 = bf16[384,1536]{1,0:T(8,128)(2,1)} collective-permute-done((bf16[384,1536]{1,0:T(8,128)(2,1)}, bf16[384,1536]{1,0:T(8,128)(2,1)}, u32[]{:S(2)}, u32[]{:S(2)}) %collective-permute-start.21) | collective-permute-done | bytes 1179680 | tf_op jit(solution)/shard_map/ppermute | solution.py:438
  709.8 18.1 %all-to-all-done.12 = bf16[4,1,320,384]{3,2,1,0:T(8,128)(2,1)} async-done(((bf16[4,1,320,384]{3,2,1,0:T(8,128)(2,1)}), bf16[4,1,320,384]{3,2,1,0:T(8,128)(2,1)}, u32[]{:S(2)}, u32[]{:S(2)}) %all-to-all-start.12) | async-done | bytes 983072 | tf_op jit(solution)/shard_map/all_to_all | solution.py:626
  729.2 7.3 half_product.14
  764.2 7.5 half_product.15
  796.6 34.2 %all-to-all-done.13 = bf16[4,96,3072]{2,1,0:T(8,128)(2,1)} async-done(((bf16[4,96,3072]{2,1,0:T(8,128)(2,1)}), bf16[4,96,3072]{2,1,0:T(8,128)(2,1)}, u32[]{:S(2)}, u32[]{:S(2)}) %all-to-all-start.13) | async-done | bytes 2359328 | tf_op jit(solution)/shard_map/all_to_all | solution.py:519
  840.7 10.7 %slice_convert_fusion = f32[5313,768]{1,0:T(8,128)} fusion(bf16[7168,768]{1,0:T(8,128)(2,1)} %all-gather.11.cloned.1.call-done), kind=kLoop, calls=%fused_computation | loop fusion | flops 4080384 | bytes 24482304 | tf_op jit(solution)/shard_map/convert_element_type | solution.py:994
  863.7 11.2 %all-to-all-done.14 = bf16[4,96,2048]{2,1,0:T(8,128)(2,1)S(1)} async-done(((bf16[4,96,2048]{2,1,0:T(8,128)(2,1)}), bf16[4,96,2048]{2,1,0:T(8,128)(2,1)S(1)}, u32[]{:S(2)}, u32[]{:S(2)}) %all-to-all-start.14) | async-done | bytes 1572896 | tf_op jit(solution)/shard_map/all_to_all | solution.py:519
  (779 shorter events, 469.5 us)
Async XLA Ops:
  9.7 40.8 %collective-permute-start = (bf16[192,1536]{1,0:T(8,128)(2,1)}, bf16[192,1536]{1,0:T(8,128)(2,1)}, u32[]{:S(2)}, u32[]{:S(2)}) collective-permute-start(bf16[192,1536]{1,0:T(8,128)(2,1)} %select_select_fusion), channel_id=1, source_target_pairs={{0,1},{1,0},{2,3},{3,2},{4,5},{5,4},{6,7},{7,6},{8,9},{9,8},{10,11... | collective-permute-start | bytes 1769480 | tf_op jit(solution)/shard_map/ppermute | solution.py:471
  26.3 33.1 %all-to-all-start = ((bf16[4,1,384,384]{3,2,1,0:T(8,128)(2,1)}), bf16[4,1,384,384]{3,2,1,0:T(8,128)(2,1)S(1)}, u32[]{:S(2)}, u32[]{:S(2)}) async-start(bf16[4,1,384,384]{3,2,1,0:T(8,128)(2,1)} %bitcast.14), calls=%async_computation | async-start | bytes 2359296 | tf_op jit(solution)/shard_map/all_to_all | solution.py:626
  31.2 100.0 %all-gather.5.cloned.1.call-start = ((), (), s32[]{:S(2)}) async-start(), calls=%async_computation.16 | async-start | bytes 2949120 | tf_op jit(solution)/shard_map/all_gather | solution.py:474
  57.9 46.4 %collective-permute-start.2 = (bf16[1344,768]{1,0:T(8,128)(2,1)}, bf16[1344,768]{1,0:T(8,128)(2,1)}, u32[]{:S(2)}, u32[]{:S(2)}) collective-permute-start(bf16[1344,768]{1,0:T(8,128)(2,1)} %fusion.70), channel_id=1, source_target_pairs={{0,1},{1,0},{2,3},{3,2},{4,5},{5,4},{6,7},{7,6},{8,9},{9,8},{10,11... | collective-permute-start | bytes 6193160 | tf_op jit(solution)/shard_map/ppermute | solution.py:471
  59.5 31.7 %all-to-all-start.2 = ((bf16[4,1,384,384]{3,2,1,0:T(8,128)(2,1)}), bf16[4,1,384,384]{3,2,1,0:T(8,128)(2,1)S(1)}, u32[]{:S(2)}, u32[]{:S(2)}) async-start(bf16[4,1,384,384]{3,2,1,0:T(8,128)(2,1)} %bitcast.392), calls=%async_computation.2 | async-start | bytes 2359296 | tf_op jit(solution)/shard_map/all_to_all | solution.py:626
  63.8 144.6 %all-gather.9.cloned.1.call-start = ((), (), s32[]{:S(2)}) async-start(), calls=%async_computation.18 | async-start | bytes 10321920 | tf_op jit(solution)/shard_map/all_gather | solution.py:474
  125.2 30.2 %all-to-all-start.3 = ((bf16[4,1,384,384]{3,2,1,0:T(8,128)(2,1)}), bf16[4,1,384,384]{3,2,1,0:T(8,128)(2,1)S(1)}, u32[]{:S(2)}, u32[]{:S(2)}) async-start(bf16[4,1,384,384]{3,2,1,0:T(8,128)(2,1)} %bitcast.37), calls=%async_computation.3 | async-start | bytes 2359296 | tf_op jit(solution)/shard_map/all_to_all | solution.py:626
  130.0 78.4 %all-gather.7.cloned.1.call-start = ((), (), s32[]{:S(2)}) async-start(), calls=%async_computation.17 | async-start | bytes 3440640 | tf_op jit(solution)/shard_map/all_gather | solution.py:474
  180.3 36.7 %collective-permute-start.4 = (bf16[384,1536]{1,0:T(8,128)(2,1)}, bf16[384,1536]{1,0:T(8,128)(2,1)}, u32[]{:S(2)}, u32[]{:S(2)}) collective-permute-start(bf16[384,1536]{1,0:T(8,128)(2,1)} %convolution_convert_fusion.6), channel_id=1, source_target_pairs={{0,1},{1,0},{2,3},{3,2},{4,5},{5,4},{6,7},{7,6},{8,9},{9,8},{10,11... | collective-permute-start | bytes 3538952 | tf_op jit(solution)/shard_map/ppermute | solution.py:438
  206.3 66.1 %collective-permute-start.6 = (bf16[384,1536]{1,0:T(8,128)(2,1)}, bf16[384,1536]{1,0:T(8,128)(2,1)}, u32[]{:S(2)}, u32[]{:S(2)}) collective-permute-start(bf16[384,1536]{1,0:T(8,128)(2,1)} %convolution_convert_fusion.5), channel_id=1, source_target_pairs={{0,1},{1,0},{2,3},{3,2},{4,5},{5,4},{6,7},{7,6},{8,9},{9,8},{10,11... | collective-permute-start | bytes 3538952 | tf_op jit(solution)/shard_map/ppermute | solution.py:438
  206.9 45.6 %collective-permute-start.7 = (bf16[768,384]{1,0:T(8,128)(2,1)S(1)}, bf16[768,384]{1,0:T(8,128)(2,1)S(1)}, u32[]{:S(2)}, u32[]{:S(2)}) collective-permute-start(bf16[768,384]{1,0:T(8,128)(2,1)S(1)} %bitcast.348), channel_id=1, source_target_pairs={{0,1},{1,0},{2,3},{3,2},{4,5},{5,4},{6,7},{7,6},{8,9},{9,8},{10,11... | collective-permute-start | bytes 1769480 | tf_op jit(solution)/shard_map/ppermute | solution.py:447
  276.9 32.8 %collective-permute-start.9 = (bf16[384,1536]{1,0:T(8,128)(2,1)S(1)}, bf16[384,1536]{1,0:T(8,128)(2,1)}, u32[]{:S(2)}, u32[]{:S(2)}) collective-permute-start(bf16[384,1536]{1,0:T(8,128)(2,1)S(1)} %convolution_convert_fusion.3), channel_id=1, source_target_pairs={{0,1},{1,0},{2,3},{3,2},{4,5},{5,4},{6,7},{7,6},{8,9},{9,8},{10,11... | collective-permute-start | bytes 3538952 | tf_op jit(solution)/shard_map/ppermute | solution.py:438
  277.3 53.2 %collective-permute-start.8 = (bf16[384,1536]{1,0:T(8,128)(2,1)}, bf16[384,1536]{1,0:T(8,128)(2,1)}, u32[]{:S(2)}, u32[]{:S(2)}) collective-permute-start(bf16[384,1536]{1,0:T(8,128)(2,1)} %convolution_convert_fusion.4), channel_id=1, source_target_pairs={{0,1},{1,0},{2,3},{3,2},{4,5},{5,4},{6,7},{7,6},{8,9},{9,8},{10,11... | collective-permute-start | bytes 3538952 | tf_op jit(solution)/shard_map/ppermute | solution.py:438
  380.5 59.9 %collective-permute-start.11 = (bf16[3584,768]{1,0:T(8,128)(2,1)}, bf16[3584,768]{1,0:T(8,128)(2,1)}, u32[]{:S(2)}, u32[]{:S(2)}) collective-permute-start(bf16[3584,768]{1,0:T(8,128)(2,1)} %head_grads.2), channel_id=1, source_target_pairs={{0,8},{8,0},{16,24},{24,16},{1,9},{9,1},{17,25},{25,17},{2,10},{10... | collective-permute-start | bytes 16515080 | tf_op jit(solution)/shard_map/ppermute | solution.py:894
  387.1 65.0 %collective-permute-start.10 = (bf16[384,1536]{1,0:T(8,128)(2,1)}, bf16[384,1536]{1,0:T(8,128)(2,1)}, u32[]{:S(2)}, u32[]{:S(2)}) collective-permute-start(bf16[384,1536]{1,0:T(8,128)(2,1)} %convolution_convert_fusion.2), channel_id=1, source_target_pairs={{0,1},{1,0},{2,3},{3,2},{4,5},{5,4},{6,7},{7,6},{8,9},{9,8},{10,11... | collective-permute-start | bytes 3538952 | tf_op jit(solution)/shard_map/ppermute | solution.py:438
  425.2 36.9 %all-to-all-start.7 = ((bf16[4,1,320,384]{3,2,1,0:T(8,128)(2,1)}), bf16[4,1,320,384]{3,2,1,0:T(8,128)(2,1)S(1)}, u32[]{:S(2)}, u32[]{:S(2)}) async-start(bf16[4,1,320,384]{3,2,1,0:T(8,128)(2,1)} %bitcast.365), calls=%async_computation.7 | async-start | bytes 1966080 | tf_op jit(solution)/shard_map/all_to_all | solution.py:626
  474.6 54.0 %collective-permute-start.13 = (bf16[768,1536]{1,0:T(8,128)(2,1)}, bf16[768,1536]{1,0:T(8,128)(2,1)}, u32[]{:S(2)}, u32[]{:S(2)}) collective-permute-start(bf16[768,1536]{1,0:T(8,128)(2,1)} %half_product.8), channel_id=1, source_target_pairs={{0,8},{8,0},{16,24},{24,16},{1,9},{9,1},{17,25},{25,17},{2,10},{10... | collective-permute-start | bytes 7077896 | tf_op jit(solution)/shard_map/ppermute | solution.py:533
  482.4 60.1 %collective-permute-start.12 = (bf16[384,1536]{1,0:T(8,128)(2,1)}, bf16[384,1536]{1,0:T(8,128)(2,1)}, u32[]{:S(2)}, u32[]{:S(2)}) collective-permute-start(bf16[384,1536]{1,0:T(8,128)(2,1)} %convolution_convert_fusion.1), channel_id=1, source_target_pairs={{0,1},{1,0},{2,3},{3,2},{4,5},{5,4},{6,7},{7,6},{8,9},{9,8},{10,11... | collective-permute-start | bytes 3538952 | tf_op jit(solution)/shard_map/ppermute | solution.py:438
  502.7 96.3 %collective-permute-start.18 = (bf16[1792,768]{1,0:T(8,128)(2,1)}, bf16[1792,768]{1,0:T(8,128)(2,1)}, u32[]{:S(2)}, u32[]{:S(2)}) collective-permute-start(bf16[1792,768]{1,0:T(8,128)(2,1)} %broadcast_select_fusion), channel_id=1, source_target_pairs={{0,16},{8,24},{16,0},{24,8},{1,17},{9,25},{17,1},{25,9},{2,18},{10... | collective-permute-start | bytes 8257544 | tf_op jit(solution)/shard_map/ppermute | solution.py:551
  523.5 49.0 %all-to-all-start.9 = ((bf16[4,1,320,384]{3,2,1,0:T(8,128)(2,1)}), bf16[4,1,320,384]{3,2,1,0:T(8,128)(2,1)S(1)}, u32[]{:S(2)}, u32[]{:S(2)}) async-start(bf16[4,1,320,384]{3,2,1,0:T(8,128)(2,1)} %bitcast.364), calls=%async_computation.9 | async-start | bytes 1966080 | tf_op jit(solution)/shard_map/all_to_all | solution.py:626
  590.0 39.9 %collective-permute-start.17 = (bf16[768,1536]{1,0:T(8,128)(2,1)}, bf16[768,1536]{1,0:T(8,128)(2,1)}, u32[]{:S(2)}, u32[]{:S(2)}) collective-permute-start(bf16[768,1536]{1,0:T(8,128)(2,1)} %half_product.10), channel_id=1, source_target_pairs={{0,8},{8,0},{16,24},{24,16},{1,9},{9,1},{17,25},{25,17},{2,10},{10... | collective-permute-start | bytes 7077896 | tf_op jit(solution)/shard_map/ppermute | solution.py:533
  590.0 59.0 %collective-permute-start.20 = (bf16[384,1536]{1,0:T(8,128)(2,1)}, bf16[384,1536]{1,0:T(8,128)(2,1)}, u32[]{:S(2)}, u32[]{:S(2)}) collective-permute-start(bf16[384,1536]{1,0:T(8,128)(2,1)} %convolution_convert_fusion.9), channel_id=1, source_target_pairs={{0,1},{1,0},{2,3},{3,2},{4,5},{5,4},{6,7},{7,6},{8,9},{9,8},{10,11... | collective-permute-start | bytes 3538952 | tf_op jit(solution)/shard_map/ppermute | solution.py:438
  598.9 45.7 %collective-permute-start.16 = (f32[117,128]{1,0:T(8,128)}, f32[117,128]{1,0:T(8,128)}, u32[]{:S(2)}, u32[]{:S(2)}) collective-permute-start(f32[117,128]{1,0:T(8,128)} %add.639), channel_id=1, source_target_pairs={{0,8},{8,0},{16,24},{24,16},{1,9},{9,1},{17,25},{25,17},{2,10},{10... | collective-permute-start | bytes 179720 | tf_op jit(solution)/shard_map/ppermute | solution.py:505
  604.9 68.0 %all-to-all-start.11 = ((bf16[4,448,768]{2,1,0:T(8,128)(2,1)}), bf16[4,448,768]{2,1,0:T(8,128)(2,1)}, u32[]{:S(2)}, u32[]{:S(2)}) async-start(bf16[4,448,768]{2,1,0:T(8,128)(2,1)} %bitcast.387), calls=%async_computation.11 | async-start | bytes 5505024 | tf_op jit(solution)/shard_map/all_to_all | solution.py:519
  609.9 230.8 %all-gather.11.cloned.1.call-start = ((), (), s32[]{:S(2)}) async-start(), calls=%async_computation.19 | async-start | bytes 11698176 | tf_op jit(solution)/shard_map/all_gather | solution.py:915
  676.1 66.5 %collective-permute-start.27 = (bf16[384,3072]{1,0:T(8,128)(2,1)}, bf16[384,3072]{1,0:T(8,128)(2,1)}, u32[]{:S(2)}, u32[]{:S(2)}) collective-permute-start(bf16[384,3072]{1,0:T(8,128)(2,1)} %broadcast_select_fusion.1), channel_id=1, source_target_pairs={{0,16},{8,24},{16,0},{24,8},{1,17},{9,25},{17,1},{25,9},{2,18},{10... | collective-permute-start | bytes 7077896 | tf_op jit(solution)/shard_map/ppermute | solution.py:551
  678.2 49.8 %all-to-all-start.12 = ((bf16[4,1,320,384]{3,2,1,0:T(8,128)(2,1)}), bf16[4,1,320,384]{3,2,1,0:T(8,128)(2,1)}, u32[]{:S(2)}, u32[]{:S(2)}) async-start(bf16[4,1,320,384]{3,2,1,0:T(8,128)(2,1)} %bitcast.87), calls=%async_computation.12 | async-start | bytes 1966080 | tf_op jit(solution)/shard_map/all_to_all | solution.py:626
  693.4 53.4 %collective-permute-start.26 = (f32[104,128]{1,0:T(8,128)S(1)}, f32[104,128]{1,0:T(8,128)S(1)}, u32[]{:S(2)}, u32[]{:S(2)}) collective-permute-start(f32[104,128]{1,0:T(8,128)S(1)} %add.648), channel_id=1, source_target_pairs={{0,16},{8,24},{16,0},{24,8},{1,17},{9,25},{17,1},{25,9},{2,18},{10... | collective-permute-start | bytes 159752 | tf_op jit(solution)/shard_map/ppermute | solution.py:505
  756.8 74.0 %all-to-all-start.13 = ((bf16[4,96,3072]{2,1,0:T(8,128)(2,1)}), bf16[4,96,3072]{2,1,0:T(8,128)(2,1)}, u32[]{:S(2)}, u32[]{:S(2)}) async-start(bf16[4,96,3072]{2,1,0:T(8,128)(2,1)} %bitcast.388), calls=%async_computation.13 | async-start | bytes 4718592 | tf_op jit(solution)/shard_map/all_to_all | solution.py:519
  785.8 45.1 %collective-permute-start.28 = (f32[24,128]{1,0:T(8,128)S(1)}, f32[24,128]{1,0:T(8,128)S(1)}, u32[]{:S(2)}, u32[]{:S(2)}) collective-permute-start(f32[24,128]{1,0:T(8,128)S(1)} %pad_maximum_fusion.11), channel_id=1, source_target_pairs={{0,8},{8,0},{16,24},{24,16},{1,9},{9,1},{17,25},{25,17},{2,10},{10... | collective-permute-start | bytes 36872 | tf_op jit(solution)/shard_map/ppermute | solution.py:505
  785.9 45.8 %collective-permute-start.30 = (bf16[384,2048]{1,0:T(8,128)(2,1)}, bf16[384,2048]{1,0:T(8,128)(2,1)}, u32[]{:S(2)}, u32[]{:S(2)}) collective-permute-start(bf16[384,2048]{1,0:T(8,128)(2,1)} %broadcast_select_fusion.4), channel_id=1, source_target_pairs={{0,16},{8,24},{16,0},{24,8},{1,17},{9,25},{17,1},{25,9},{2,18},{10... | collective-permute-start | bytes 4718600 | tf_op jit(solution)/shard_map/ppermute | solution.py:551
  835.0 39.9 %all-to-all-start.14 = ((bf16[4,96,2048]{2,1,0:T(8,128)(2,1)}), bf16[4,96,2048]{2,1,0:T(8,128)(2,1)S(1)}, u32[]{:S(2)}, u32[]{:S(2)}) async-start(bf16[4,96,2048]{2,1,0:T(8,128)(2,1)} %bitcast.390), calls=%async_computation.14 | async-start | bytes 3145728 | tf_op jit(solution)/shard_map/all_to_all | solution.py:519
  (248 other events, 2162.7 us)
Sparse Core Ops, SparseCore 0:
  50.7 24.8 all-gather.4
  104.5 57.9 all-gather.8
  164.0 26.2 all-gather.6
  676.3 127.4 all-gather.10

commit v4 on v3

--- a/solution.py
+++ b/solution.py
@@ -97,9 +97,7 @@
             jax.ShapeDtypeStruct((bins, bins), jnp.bfloat16),
         ],
         compiler_params=pltpu.CompilerParams(vmem_limit_bytes=48 << 20),
-        cost_estimate=pl.CostEstimate(
-            flops=2 * bins * bins * 1024, bytes_accessed=2 * bins * bins, transcendentals=bins * bins
-        ),
+        cost_estimate=pl.CostEstimate(flops=1, bytes_accessed=1, transcendentals=0),
         name="attend_forward",
     )(pack, rel)
 
@@ -183,9 +181,7 @@
         ],
         scratch_shapes=[pltpu.VMEM((VD + KD, bins), jnp.float32)],
         compiler_params=pltpu.CompilerParams(vmem_limit_bytes=48 << 20),
-        cost_estimate=pl.CostEstimate(
-            flops=2 * bins * bins * 2048, bytes_accessed=2 * bins * bins, transcendentals=0
-        ),
+        cost_estimate=pl.CostEstimate(flops=1, bytes_accessed=1, transcendentals=0),
         name="attend_backward",
     )(pack, rel, probs, grad)
 
@@ -301,11 +297,7 @@
             jax.ShapeDtypeStruct((8, bins), jnp.float32),
         ],
         compiler_params=pltpu.CompilerParams(vmem_limit_bytes=56 << 20),
-        cost_estimate=pl.CostEstimate(
-            flops=4 * bins * width * track_human,
-            bytes_accessed=4 * width * track_human,
-            transcendentals=4 * bins * track_human,
-        ),
+        cost_estimate=pl.CostEstimate(flops=1, bytes_accessed=1, transcendentals=0),
         name="score_heads",
     )(pick, rows, weight, *own, *others, bias, count_human, count_mouse)
 
@@ -358,11 +350,7 @@
         ),
         out_shape=jax.ShapeDtypeStruct((tiles * TILE, share), jnp.bfloat16),
         compiler_params=pltpu.CompilerParams(vmem_limit_bytes=40 << 20),
-        cost_estimate=pl.CostEstimate(
-            flops=2 * windows * bins * share * tiles * TILE,
-            bytes_accessed=4 * tiles * TILE * share,
-            transcendentals=0,
-        ),
+        cost_estimate=pl.CostEstimate(flops=1, bytes_accessed=1, transcendentals=0),
         name="head_grads",
     )(pick, *grads, rows, *extra)
 
@@ -408,11 +396,7 @@
         ),
         out_shape=jax.ShapeDtypeStruct((width // 2, cols), jnp.bfloat16),
         compiler_params=pltpu.CompilerParams(vmem_limit_bytes=48 << 20),
-        cost_estimate=pl.CostEstimate(
-            flops=windows * rows * width * cols,
-            bytes_accessed=windows * rows * (width + 2 * cols),
-            transcendentals=0,
-        ),
+        cost_estimate=pl.CostEstimate(flops=1, bytes_accessed=1, transcendentals=0),
         name="half_product",
     )(half, *lefts, *rights, *extra)
 
@@ -674,10 +658,13 @@
         if mp_size == 2:
             parts["heads"] = [OtherRows(own, TILE, after_line, done) for own in own_heads]
 
-    def fetch_heads_share(_):
+    def fetch_human_share(_):
         if mp_size == 2:
-            for part in parts["heads"]:
-                part.share()
+            parts["heads"][0].share()
+
+    def fetch_mouse_share(_):
+        if mp_size == 2:
+            parts["heads"][1].share()
 
     def fetch_heads_end(_):
         if mp_size == 2:
@@ -954,10 +941,6 @@
         late = results["late_rows"].finish()
         results["out"], results["pack"] = late[:, :width_out], late[:, width_out:]
 
-    def sums_early(_):
-        values = list(sums) + [sum(track_sums), sum(losses)[None]]
-        results["early"] = SmallSums(values, ("seq", "dp"), after_line, done)
-
     def sums_heads(_):
         dw_rel = jnp.zeros((heads, FEAT, KD), jnp.float32)
         dstat = jnp.zeros((heads, 2, KD), jnp.float32)
@@ -977,10 +960,8 @@
         results["own_head"] = SmallSums(values, axes, after_line, done)
 
     def sums_late(_):
-        results["late"] = SmallSums(list(sums1), ("dp", "seq"), after_line, done)
-
-    def step_early(_):
-        results["early"].step()
+        values = list(sums1) + list(sums) + [sum(track_sums), sum(losses)[None]]
+        results["late"] = SmallSums(values, ("dp", "seq"), after_line, done)
 
     def step_heads(_):
         results["own_head"].step()
@@ -1003,26 +984,25 @@
     if count == 3:
         plan = one(fetch_out) + [(project, 0)] + one(fetch_out_share, fetch_heads)
         plan += [(project, 1), (project, 2)] + one(spread_bias) + [(attend, 0), (attend, 1)]
-        plan += one(fetch_heads_share) + [(attend_swap, 0)] + one(fetch_out_end)
-        plan += [(feed_forward, 0), (attend, 2), (attend_swap, 1), (feed_forward, 1)]
-        plan += [(attend_swap, 2)] + one(fetch_heads_end)
+        plan += one(fetch_human_share) + [(attend_swap, 0)] + one(fetch_out_end)
+        plan += [(feed_forward, 0)] + one(fetch_mouse_share) + [(attend, 2), (attend_swap, 1)]
+        plan += [(feed_forward, 1), (attend_swap, 2)] + one(fetch_heads_end)
         plan += [(score, 0), (feed_forward, 2), (back_hidden, 0)]
-        plan += [(score, 1), (back_hidden, 1), (back_mid, 0), (score, 2)]
-        plan += one(grads_heads) + [(arrive_grad, 0), (back_attend, 0), (back_hidden, 2)]
-        plan += one(grads_heads_keep) + [(back_mid, 1), (arrive_packed, 0)] + one(grads_in)
-        plan += [(arrive_grad, 1), (back_attend, 1)] + one(grads_in_keep) + [(back_mid, 2)]
-        plan += one(sums_early) + [(back_project, 0), (arrive_packed, 1)] + one(step_early, grads_hid)
-        plan += [(arrive_grad, 2)] + one(step_early, grads_heads_seq) + [(back_attend, 2)]
-        plan += one(grads_hid_keep, step_early) + [(back_project, 1), (back_input, 0)]
-        plan += one(grads_out, step_early, sums_heads, grads_out_keep, step_heads)
-        plan += one(heads_arrive, grads_heads_end) + [(back_input, 1), (arrive_packed, 2)]
-        plan += one(grads_pack) + [(back_project, 2)]
-        plan += one(grads_wide_seq, step_heads, grads_pack_keep) + [(back_input, 2)]
-        plan += one(sums_late, wide_arrive, step_late, grads_pack_seq, step_late, heads_out)
-        plan += one(grads_wide_end, step_late, grads_pack_end, step_late)
+        plan += [(score, 1), (back_hidden, 1), (back_mid, 0), (score, 2), (arrive_grad, 0)]
+        plan += one(grads_heads) + [(back_attend, 0), (back_hidden, 2)] + one(grads_heads_keep)
+        plan += [(back_mid, 1), (arrive_packed, 0), (back_project, 0)] + one(grads_in)
+        plan += [(back_mid, 2), (arrive_grad, 1), (back_attend, 1)] + one(grads_hid, grads_in_keep)
+        plan += [(arrive_grad, 2)] + one(grads_heads_seq) + [(back_attend, 2)]
+        plan += one(grads_hid_keep) + [(back_input, 0)] + one(heads_arrive, grads_out)
+        plan += one(sums_heads, grads_out_keep) + [(arrive_packed, 1), (back_project, 1)]
+        plan += one(grads_wide_seq, step_heads) + [(arrive_packed, 2)] + one(grads_heads_end)
+        plan += one(grads_pack) + [(back_project, 2)] + one(grads_pack_keep)
+        plan += [(back_input, 1)] + one(wide_arrive, step_heads) + [(back_input, 2)]
+        plan += one(sums_late, grads_pack_seq, step_late, grads_wide_end, step_late)
+        plan += one(heads_out, step_late, grads_pack_end, step_late)
     else:
         plan = one(fetch_out, fetch_out_share, fetch_out_end, spread_bias)
-        plan += one(fetch_heads, fetch_heads_share, fetch_heads_end)
+        plan += one(fetch_heads, fetch_human_share, fetch_mouse_share, fetch_heads_end)
         plan += each(project) + each(attend) + each(attend_swap) + each(feed_forward) + each(score)
         plan += each(back_hidden) + each(back_mid)
         plan += one(grads_heads, grads_heads_keep, grads_heads_seq, grads_heads_end)
@@ -1030,11 +1010,11 @@
         plan += one(grads_wide_seq, grads_wide_end, grads_out, grads_out_keep)
         plan += each(arrive_packed) + each(back_project) + one(grads_pack, grads_pack_keep)
         plan += one(grads_pack_seq, grads_pack_end) + each(back_input)
-        plan += one(sums_early, sums_heads, sums_late, heads_out)
+        plan += one(sums_heads, sums_late, heads_out)
     for stage, g in plan:
         stage(g)
-    dgain2, dbias2, db_out, db_hid, db_in, dtracks, loss = results["early"].finish()
-    dgain1, dbias1 = results["late"].finish()
+    summed = results["late"].finish()
+    dgain1, dbias1, dgain2, dbias2, db_out, db_hid, db_in, dtracks, loss = summed
     mids_sum = results["own_head"].finish()
     if heads == seq_size:
         share_rel, share_stat = FEAT // places, KD // places

time: 904 us -> 899 us (level); the launches traced: 891 us -> 903 us
  starting transfers between devices: 100 us -> 120 us
  local copies, waits for them, and re-layouts: 99.8 us -> 87.9 us
    all_to_all x3, waiting for transfers between devices: 48.7 us -> 82.1 us  [__init__(): lax.all_to_all(done(parts), 'seq', split_axis=0, concat_axis=0, tiled=True)]
    ppermute x9, waiting for transfers between devices: 37.6 us -> 15.7 us  [sum_over_model(): other = lax.ppermute(low, 'mp', [(0, 1), (1, 0)])]
    ppermute x3, starting transfers between devices: 2.41 us -> 24 us  [__init__(): lax.ppermute(done(jnp.where(upper, low, high)), 'dp', swap_pairs('dp', 2))]
    ppermute x3, waiting for transfers between devices: 17.3 us -> 0.01 us  [__init__(): self.mine = lax.ppermute(done(part), 'mp', [(0, 1), (1, 0)])]
    unnamed x462 -> x454, local copies, waits for them, and re-layouts: 54.2 us -> 38.2 us
    all_to_all x12, waiting for transfers between devices: 41.7 us -> 54.2 us  [exchange(): return lax.all_to_all(array, 'seq', split_axis=0, concat_axis=0, tiled=True)]
  transfers between devices with their start and end apart: 53 -> 49, of which waited for: 22 -> 17; matrix products, arithmetic and copies ran while one was open for 33% -> 32% of each run, Pallas kernels for 19% -> 24%
where the time goes in v4:
time: 899 us; the launch traced here: 903 us
  Pallas kernels  224 us (25%)
  waiting for transfers between devices  187 us (21%)
  other arithmetic  152 us (17%)
  starting transfers between devices  120 us (13%)
  matrix products  106 us (12%)
  local copies, waits for them, and re-layouts  87.9 us (10%)
  between operations  25.3 us (3%)
    dot_general x31, matrix products, mxu(): lax.dot_general(left_arr, right_arr, dims, precision=precision, preferred...  88.4 us
    all_to_all x3, waiting for transfers between devices, __init__(): lax.all_to_all(done(parts), 'seq', split_axis=0, concat_axis=0, tiled=True)  82.1 us
    pallas_call x3, Pallas kernels, score_heads(): pl.pallas_call(lambda *refs: heads_kernel(track_human, track_mouse, *refs...  68.2 us
    all_to_all x12, starting transfers between devices, exchange(): return lax.all_to_all(array, 'seq', split_axis=0, concat_axis=0, tiled=True)  55.5 us
    all_to_all x12, waiting for transfers between devices, exchange(): return lax.all_to_all(array, 'seq', split_axis=0, concat_axis=0, tiled=True)  54.2 us
    pallas_call x8, Pallas kernels, half_product(): pl.pallas_call(lambda *refs: half_product_kernel(windows, turned, more is...  53.8 us
    pallas_call x3, Pallas kernels, attend_backward(): pl.pallas_call(lambda *refs: attend_backward_kernel(block, bins, *refs),...  53.7 us
    unnamed x454, local copies, waits for them, and re-layouts  38.2 us
  transfers between devices with their start and end apart: 49, of which 17 were waited for; matrix products, arithmetic and copies ran while one was open for 32% of the time, Pallas kernels for 24%

profile of v4, /device:TPU:0, one launch (start us, length us, event | category | flops | bytes accessed | tf_op | source)
XLA Modules:
  0.0 902.9 jit_solution(15764749684463782384)
XLA Ops:
  50.7 8.9 all-to-all-done
  82.0 10.4 %attend_forward.3 = (bf16[4,192,384]{2,1,0:T(8,128)(2,1)}, bf16[1536,1536]{1,0:T(8,128)(2,1)}) custom-call(bf16[1536,384]{1,0:T(8,128)(2,1)S(1)} %bitcast.338, bf16[3072,64]{1,0:T(8,128)(2,1)S(1)} %convolution_convert_fusion.refs_1_), custom_call_target="tpu_custom_call" | custom-call | flops 1 | bytes 1 | tf_op jit(solution)/shard_map/attend_forward/pallas_call | solution.py:84
  92.4 10.2 %attend_forward.4 = (bf16[4,192,384]{2,1,0:T(8,128)(2,1)S(1)}, bf16[1536,1536]{1,0:T(8,128)(2,1)}) custom-call(bf16[1536,384]{1,0:T(8,128)(2,1)S(1)} %bitcast.334, bf16[3072,64]{1,0:T(8,128)(2,1)S(1)} %convolution_convert_fusion.refs_1_), custom_call_target="tpu_custom_call" | custom-call | flops 1 | bytes 1 | tf_op jit(solution)/shard_map/attend_forward/pallas_call | solution.py:84
  109.3 14.1 %all-to-all-done.1 = bf16[4,1,192,384]{3,2,1,0:T(8,128)(2,1)S(1)} async-done(((bf16[4,1,192,384]{3,2,1,0:T(8,128)(2,1)}), bf16[4,1,192,384]{3,2,1,0:T(8,128)(2,1)S(1)}, u32[]{:S(2)}, u32[]{:S(2)}) %all-to-all-start.1) | async-done | bytes 589856 | tf_op jit(solution)/shard_map/all_to_all | solution.py:610
  131.6 10.8 %collective-permute-done.2 = bf16[768,384]{1,0:T(8,128)(2,1)S(1)} collective-permute-done((bf16[768,384]{1,0:T(8,128)(2,1)}, bf16[768,384]{1,0:T(8,128)(2,1)S(1)}, u32[]{:S(2)}, u32[]{:S(2)}) %collective-permute-start.2) | collective-permute-done | bytes 589856 | tf_op jit(solution)/shard_map/ppermute | solution.py:431
  148.0 7.8 all-to-all-done.3
  170.2 10.4 %attend_forward.5 = (bf16[4,192,384]{2,1,0:T(8,128)(2,1)}, bf16[1536,1536]{1,0:T(8,128)(2,1)}) custom-call(bf16[1536,384]{1,0:T(8,128)(2,1)S(1)} %bitcast.336, bf16[3072,64]{1,0:T(8,128)(2,1)S(1)} %convolution_convert_fusion.refs_1_), custom_call_target="tpu_custom_call" | custom-call | flops 1 | bytes 1 | tf_op jit(solution)/shard_map/attend_forward/pallas_call | solution.py:84
  215.1 7.3 collective-permute-done.3
  227.6 17.1 %score_heads.3 = (bf16[7168,384]{1,0:T(8,128)(2,1)}, f32[384,1536]{1,0:T(8,128)}, f32[8,7168]{1,0:T(8,128)}, f32[8,384]{1,0:T(8,128)}) custom-call(s32[2]{0:T(128)} %get-tuple-element.821.refs_0_, bf16[384,1536]{1,0:T(8,128)(2,1)} %get-tuple-element.740.refs_1_, f32[8,384]{1,0:T(8,128)} %broadcast_in_dim.29.refs_2_, bf16[5313,768]{1,0:T(8,128)(2,1)} %bitcast.362, ...), custom_call_target="tpu_custom_call" | custom-call | flops 1 | bytes 1 | tf_op jit(solution)/shard_map/score_heads/pallas_call | solution.py:270
  244.7 13.7 %collective-permute-done.7 = bf16[768,384]{1,0:T(8,128)(2,1)S(1)} collective-permute-done((bf16[768,384]{1,0:T(8,128)(2,1)S(1)}, bf16[768,384]{1,0:T(8,128)(2,1)S(1)}, u32[]{:S(2)}, u32[]{:S(2)}) %collective-permute-start.7) | collective-permute-done | bytes 589856 | tf_op jit(solution)/shard_map/ppermute | solution.py:431
  285.1 16.4 %score_heads.4 = (bf16[7168,384]{1,0:T(8,128)(2,1)}, f32[384,1536]{1,0:T(8,128)}, f32[8,7168]{1,0:T(8,128)}, f32[8,384]{1,0:T(8,128)}) custom-call(s32[2]{0:T(128)} %get-tuple-element.822.refs_0_, bf16[384,1536]{1,0:T(8,128)(2,1)} %get-tuple-element.738.refs_1_, f32[8,384]{1,0:T(8,128)} %broadcast_in_dim.29.refs_2_, bf16[5313,768]{1,0:T(8,128)(2,1)} %bitcast.363, ...), custom_call_target="tpu_custom_call" | custom-call | flops 1 | bytes 1 | tf_op jit(solution)/shard_map/score_heads/pallas_call | solution.py:270
  327.8 6.9 collective-permute-done.8
  346.3 34.7 %score_heads.5 = (bf16[7168,384]{1,0:T(8,128)(2,1)}, f32[384,1536]{1,0:T(8,128)}, f32[8,7168]{1,0:T(8,128)}, f32[8,384]{1,0:T(8,128)}) custom-call(s32[2]{0:T(128)} %pad_add_fusion.2.refs_0_, bf16[384,1536]{1,0:T(8,128)(2,1)} %get-tuple-element.736.refs_1_, f32[8,384]{1,0:T(8,128)} %broadcast_in_dim.29.refs_2_, bf16[5313,768]{1,0:T(8,128)(2,1)} %bitcast.364, ...), custom_call_target="tpu_custom_call" | custom-call | flops 1 | bytes 1 | tf_op jit(solution)/shard_map/score_heads/pallas_call | solution.py:270
  383.9 9.8 %head_grads.2 = bf16[3584,768]{1,0:T(8,128)(2,1)} custom-call(s32[4]{0:T(128)S(1)} %get-tuple-element.807.refs_0_, bf16[7168,384]{1,0:T(8,128)(2,1)S(1)} %copy-done.1, bf16[7168,384]{1,0:T(8,128)(2,1)} %get-tuple-element.407.refs_2_, bf16[7168,384]{1,0:T(8,128)(2,1)} %get-tuple-element.408.refs_3_, bf16[3,384,768]{2,1,0:T(8,128)(2,1)S(1)} %pad_maximum_fusion.3.refs_4_), custom_call_target="tpu_custom_call" | custom-call | flops 1 | bytes 1 | tf_op jit(solution)/shard_map/head_grads/pallas_call | solution.py:338
  393.8 9.1 %concatenate.143 = bf16[1536,1280]{1,0:T(8,128)(2,1)} concatenate(bf16[1536,192]{1,0:T(8,128)(2,1)} %copy-done.105, bf16[1536,64]{1,0:T(8,128)(2,1)S(1)} %copy-done.121, bf16[1536,64]{1,0:T(8,128)(2,1)} %copy-done.138, bf16[1536,192]{1,0:T(8,128)(2,1)} %copy-done.107, bf16[1536,64]{1,0:T(8,128)(2,1)} %copy-done.122, bf16[1536,64]{1,0:T(8,128)(2,1)} %copy-done.135, ...), dimensions={1} | concatenate | bytes 7864320 | tf_op jit(solution)/shard_map/concatenate | solution.py:687
  406.4 17.9 %attend_backward.3 = (bf16[4,320,384]{2,1,0:T(8,128)(2,1)S(1)}, f32[64,3072]{1,0:T(8,128)S(1)}, f32[8,128]{1,0:T(8,128)S(1)}) custom-call(bf16[1536,384]{1,0:T(8,128)(2,1)S(1)} %bitcast.339, bf16[3072,64]{1,0:T(8,128)(2,1)S(1)} %convolution_convert_fusion.refs_1_, bf16[1536,1536]{1,0:T(8,128)(2,1)} %get-tuple-element.398.refs_2_, ...), custom_call_target="tpu_custom_call" | custom-call | flops 1 | bytes 1 | tf_op jit(solution)/shard_map/attend_backward/pallas_call | solution.py:163
  444.3 7.7 head_grads.3
  473.9 23.5 %collective-permute-start.16 = (bf16[1792,768]{1,0:T(8,128)(2,1)}, bf16[1792,768]{1,0:T(8,128)(2,1)}, u32[]{:S(2)}, u32[]{:S(2)}) collective-permute-start(bf16[1792,768]{1,0:T(8,128)(2,1)} %broadcast_select_fusion), channel_id=1, source_target_pairs={{0,16},{8,24},{16,0},{24,8},{1,17},{9,25},{17,1},{25,9},{2,18},{10... | collective-permute-start | bytes 8257544 | tf_op jit(solution)/shard_map/ppermute | solution.py:535
  502.3 7.1 half_product.8
  529.2 17.9 %attend_backward.4 = (bf16[4,320,384]{2,1,0:T(8,128)(2,1)S(1)}, f32[64,3072]{1,0:T(8,128)S(1)}, f32[8,128]{1,0:T(8,128)S(1)}) custom-call(bf16[1536,384]{1,0:T(8,128)(2,1)S(1)} %bitcast.335, bf16[3072,64]{1,0:T(8,128)(2,1)S(1)} %convolution_convert_fusion.refs_1_, bf16[1536,1536]{1,0:T(8,128)(2,1)} %get-tuple-element.439.refs_2_, ...), custom_call_target="tpu_custom_call" | custom-call | flops 1 | bytes 1 | tf_op jit(solution)/shard_map/attend_backward/pallas_call | solution.py:163
  549.0 7.1 half_product.9
  556.1 7.4 half_product.10
  577.6 17.9 %attend_backward.5 = (bf16[4,320,384]{2,1,0:T(8,128)(2,1)S(1)}, f32[64,3072]{1,0:T(8,128)S(1)}, f32[8,128]{1,0:T(8,128)S(1)}) custom-call(bf16[1536,384]{1,0:T(8,128)(2,1)S(1)} %bitcast.337, bf16[3072,64]{1,0:T(8,128)(2,1)S(1)} %convolution_convert_fusion.refs_1_, bf16[1536,1536]{1,0:T(8,128)(2,1)} %get-tuple-element.457.refs_2_, ...), custom_call_target="tpu_custom_call" | custom-call | flops 1 | bytes 1 | tf_op jit(solution)/shard_map/attend_backward/pallas_call | solution.py:163
  595.6 7.7 half_product.11
  608.4 28.7 %all-to-all-done.11 = bf16[4,448,768]{2,1,0:T(8,128)(2,1)} async-done(((bf16[4,448,768]{2,1,0:T(8,128)(2,1)}), bf16[4,448,768]{2,1,0:T(8,128)(2,1)}, u32[]{:S(2)}, u32[]{:S(2)}) %all-to-all-start.11) | async-done | bytes 2752544 | tf_op jit(solution)/shard_map/all_to_all | solution.py:503
  649.1 16.1 %all-to-all-done.10 = bf16[4,1,320,384]{3,2,1,0:T(8,128)(2,1)} async-done(((bf16[4,1,320,384]{3,2,1,0:T(8,128)(2,1)}), bf16[4,1,320,384]{3,2,1,0:T(8,128)(2,1)}, u32[]{:S(2)}, u32[]{:S(2)}) %all-to-all-start.10) | async-done | bytes 983072 | tf_op jit(solution)/shard_map/all_to_all | solution.py:610
  686.2 7.2 all-to-all-done.12
  701.5 7.3 half_product.14
  734.1 7.7 half_product.15
  747.9 43.6 %all-to-all-done.13 = bf16[4,96,3072]{2,1,0:T(8,128)(2,1)} async-done(((bf16[4,96,3072]{2,1,0:T(8,128)(2,1)}), bf16[4,96,3072]{2,1,0:T(8,128)(2,1)}, u32[]{:S(2)}, u32[]{:S(2)}) %all-to-all-start.13) | async-done | bytes 2359328 | tf_op jit(solution)/shard_map/all_to_all | solution.py:503
  855.9 10.7 %slice_convert_fusion = f32[5313,768]{1,0:T(8,128)} fusion(bf16[7168,768]{1,0:T(8,128)(2,1)} %all-gather.11.cloned.1.call-done), kind=kLoop, calls=%fused_computation | loop fusion | flops 4080384 | bytes 24482304 | tf_op jit(solution)/shard_map/convert_element_type | solution.py:975
  871.8 9.9 %all-to-all-done.14 = bf16[4,96,2048]{2,1,0:T(8,128)(2,1)S(1)} async-done(((bf16[4,96,2048]{2,1,0:T(8,128)(2,1)}), bf16[4,96,2048]{2,1,0:T(8,128)(2,1)S(1)}, u32[]{:S(2)}, u32[]{:S(2)}) %all-to-all-start.14) | async-done | bytes 1572896 | tf_op jit(solution)/shard_map/all_to_all | solution.py:503
  (756 shorter events, 444.9 us)
Async XLA Ops:
  9.7 33.1 %collective-permute-start = (bf16[192,1536]{1,0:T(8,128)(2,1)}, bf16[192,1536]{1,0:T(8,128)(2,1)}, u32[]{:S(2)}, u32[]{:S(2)}) collective-permute-start(bf16[192,1536]{1,0:T(8,128)(2,1)} %select_select_fusion), channel_id=1, source_target_pairs={{0,1},{1,0},{2,3},{3,2},{4,5},{5,4},{6,7},{7,6},{8,9},{9,8},{10,11... | collective-permute-start | bytes 1769480 | tf_op jit(solution)/shard_map/ppermute | solution.py:455
  26.5 33.1 %all-to-all-start = ((bf16[4,1,384,384]{3,2,1,0:T(8,128)(2,1)}), bf16[4,1,384,384]{3,2,1,0:T(8,128)(2,1)S(1)}, u32[]{:S(2)}, u32[]{:S(2)}) async-start(bf16[4,1,384,384]{3,2,1,0:T(8,128)(2,1)} %bitcast.14), calls=%async_computation | async-start | bytes 2359296 | tf_op jit(solution)/shard_map/all_to_all | solution.py:610
  31.3 97.2 %all-gather.5.cloned.1.call-start = ((), (), s32[]{:S(2)}) async-start(), calls=%async_computation.16 | async-start | bytes 2949120 | tf_op jit(solution)/shard_map/all_gather | solution.py:458
  49.9 52.7 %collective-permute-start.1 = (bf16[1344,768]{1,0:T(8,128)(2,1)}, bf16[1344,768]{1,0:T(8,128)(2,1)}, u32[]{:S(2)}, u32[]{:S(2)}) collective-permute-start(bf16[1344,768]{1,0:T(8,128)(2,1)} %fusion.70), channel_id=1, source_target_pairs={{0,1},{1,0},{2,3},{3,2},{4,5},{5,4},{6,7},{7,6},{8,9},{9,8},{10,11... | collective-permute-start | bytes 6193160 | tf_op jit(solution)/shard_map/ppermute | solution.py:455
  59.6 32.8 %all-to-all-start.2 = ((bf16[4,1,384,384]{3,2,1,0:T(8,128)(2,1)}), bf16[4,1,384,384]{3,2,1,0:T(8,128)(2,1)S(1)}, u32[]{:S(2)}, u32[]{:S(2)}) async-start(bf16[4,1,384,384]{3,2,1,0:T(8,128)(2,1)} %bitcast.33), calls=%async_computation.2 | async-start | bytes 2359296 | tf_op jit(solution)/shard_map/all_to_all | solution.py:610
  63.1 152.0 %all-gather.9.cloned.1.call-start = ((), (), s32[]{:S(2)}) async-start(), calls=%async_computation.18 | async-start | bytes 10321920 | tf_op jit(solution)/shard_map/all_gather | solution.py:458
  108.5 61.6 %collective-permute-start.4 = (bf16[448,768]{1,0:T(8,128)(2,1)}, bf16[448,768]{1,0:T(8,128)(2,1)}, u32[]{:S(2)}, u32[]{:S(2)}) collective-permute-start(bf16[448,768]{1,0:T(8,128)(2,1)} %fusion.129), channel_id=1, source_target_pairs={{0,1},{1,0},{2,3},{3,2},{4,5},{5,4},{6,7},{7,6},{8,9},{9,8},{10,11... | collective-permute-start | bytes 2064392 | tf_op jit(solution)/shard_map/ppermute | solution.py:455
  159.9 55.2 %all-gather.7.cloned.1.call-start = ((), (), s32[]{:S(2)}) async-start(), calls=%async_computation.17 | async-start | bytes 3440640 | tf_op jit(solution)/shard_map/all_gather | solution.py:458
  185.1 37.3 %collective-permute-start.3 = (bf16[384,1536]{1,0:T(8,128)(2,1)}, bf16[384,1536]{1,0:T(8,128)(2,1)}, u32[]{:S(2)}, u32[]{:S(2)}) collective-permute-start(bf16[384,1536]{1,0:T(8,128)(2,1)} %convolution_convert_fusion.6), channel_id=1, source_target_pairs={{0,1},{1,0},{2,3},{3,2},{4,5},{5,4},{6,7},{7,6},{8,9},{9,8},{10,11... | collective-permute-start | bytes 3538952 | tf_op jit(solution)/shard_map/ppermute | solution.py:422
  213.1 66.0 %collective-permute-start.6 = (bf16[384,1536]{1,0:T(8,128)(2,1)}, bf16[384,1536]{1,0:T(8,128)(2,1)}, u32[]{:S(2)}, u32[]{:S(2)}) collective-permute-start(bf16[384,1536]{1,0:T(8,128)(2,1)} %convolution_convert_fusion.5), channel_id=1, source_target_pairs={{0,1},{1,0},{2,3},{3,2},{4,5},{5,4},{6,7},{7,6},{8,9},{9,8},{10,11... | collective-permute-start | bytes 3538952 | tf_op jit(solution)/shard_map/ppermute | solution.py:422
  213.9 44.5 %collective-permute-start.7 = (bf16[768,384]{1,0:T(8,128)(2,1)S(1)}, bf16[768,384]{1,0:T(8,128)(2,1)S(1)}, u32[]{:S(2)}, u32[]{:S(2)}) collective-permute-start(bf16[768,384]{1,0:T(8,128)(2,1)S(1)} %bitcast.344), channel_id=1, source_target_pairs={{0,1},{1,0},{2,3},{3,2},{4,5},{5,4},{6,7},{7,6},{8,9},{9,8},{10,11... | collective-permute-start | bytes 1769480 | tf_op jit(solution)/shard_map/ppermute | solution.py:431
  283.1 33.4 %collective-permute-start.9 = (bf16[384,1536]{1,0:T(8,128)(2,1)}, bf16[384,1536]{1,0:T(8,128)(2,1)}, u32[]{:S(2)}, u32[]{:S(2)}) collective-permute-start(bf16[384,1536]{1,0:T(8,128)(2,1)} %convolution_convert_fusion.3), channel_id=1, source_target_pairs={{0,1},{1,0},{2,3},{3,2},{4,5},{5,4},{6,7},{7,6},{8,9},{9,8},{10,11... | collective-permute-start | bytes 3538952 | tf_op jit(solution)/shard_map/ppermute | solution.py:422
  283.8 51.0 %collective-permute-start.8 = (bf16[384,1536]{1,0:T(8,128)(2,1)}, bf16[384,1536]{1,0:T(8,128)(2,1)}, u32[]{:S(2)}, u32[]{:S(2)}) collective-permute-start(bf16[384,1536]{1,0:T(8,128)(2,1)} %convolution_convert_fusion.4), channel_id=1, source_target_pairs={{0,1},{1,0},{2,3},{3,2},{4,5},{5,4},{6,7},{7,6},{8,9},{9,8},{10,11... | collective-permute-start | bytes 3538952 | tf_op jit(solution)/shard_map/ppermute | solution.py:422
  336.9 44.5 %all-to-all-start.6 = ((bf16[4,1,192,384]{3,2,1,0:T(8,128)(2,1)}), bf16[4,1,192,384]{3,2,1,0:T(8,128)(2,1)S(1)}, u32[]{:S(2)}, u32[]{:S(2)}) async-start(bf16[4,1,192,384]{3,2,1,0:T(8,128)(2,1)} %bitcast.51), calls=%async_computation.6 | async-start | bytes 1179648 | tf_op jit(solution)/shard_map/all_to_all | solution.py:610
  393.8 50.5 %collective-permute-start.11 = (bf16[3584,768]{1,0:T(8,128)(2,1)}, bf16[3584,768]{1,0:T(8,128)(2,1)}, u32[]{:S(2)}, u32[]{:S(2)}) collective-permute-start(bf16[3584,768]{1,0:T(8,128)(2,1)} %head_grads.2), channel_id=1, source_target_pairs={{0,8},{8,0},{16,24},{24,16},{1,9},{9,1},{17,25},{25,17},{2,10},{10... | collective-permute-start | bytes 16515080 | tf_op jit(solution)/shard_map/ppermute | solution.py:881
  402.9 53.1 %collective-permute-start.10 = (bf16[384,1536]{1,0:T(8,128)(2,1)}, bf16[384,1536]{1,0:T(8,128)(2,1)}, u32[]{:S(2)}, u32[]{:S(2)}) collective-permute-start(bf16[384,1536]{1,0:T(8,128)(2,1)} %convolution_convert_fusion.2), channel_id=1, source_target_pairs={{0,1},{1,0},{2,3},{3,2},{4,5},{5,4},{6,7},{7,6},{8,9},{9,8},{10,11... | collective-permute-start | bytes 3538952 | tf_op jit(solution)/shard_map/ppermute | solution.py:422
  426.2 41.3 %all-to-all-start.7 = ((bf16[4,1,320,384]{3,2,1,0:T(8,128)(2,1)}), bf16[4,1,320,384]{3,2,1,0:T(8,128)(2,1)S(1)}, u32[]{:S(2)}, u32[]{:S(2)}) async-start(bf16[4,1,320,384]{3,2,1,0:T(8,128)(2,1)} %bitcast.355), calls=%async_computation.7 | async-start | bytes 1966080 | tf_op jit(solution)/shard_map/all_to_all | solution.py:610
  442.9 66.6 %collective-permute-start.14 = (bf16[384,1536]{1,0:T(8,128)(2,1)}, bf16[384,1536]{1,0:T(8,128)(2,1)}, u32[]{:S(2)}, u32[]{:S(2)}) collective-permute-start(bf16[384,1536]{1,0:T(8,128)(2,1)} %convolution_convert_fusion.1), channel_id=1, source_target_pairs={{0,1},{1,0},{2,3},{3,2},{4,5},{5,4},{6,7},{7,6},{8,9},{9,8},{10,11... | collective-permute-start | bytes 3538952 | tf_op jit(solution)/shard_map/ppermute | solution.py:422
  468.5 52.7 %all-to-all-start.8 = ((bf16[4,1,192,384]{3,2,1,0:T(8,128)(2,1)}), bf16[4,1,192,384]{3,2,1,0:T(8,128)(2,1)S(1)}, u32[]{:S(2)}, u32[]{:S(2)}) async-start(bf16[4,1,192,384]{3,2,1,0:T(8,128)(2,1)} %bitcast.64), calls=%async_computation.8 | async-start | bytes 1179648 | tf_op jit(solution)/shard_map/all_to_all | solution.py:610
  473.9 89.6 %collective-permute-start.16 = (bf16[1792,768]{1,0:T(8,128)(2,1)}, bf16[1792,768]{1,0:T(8,128)(2,1)}, u32[]{:S(2)}, u32[]{:S(2)}) collective-permute-start(bf16[1792,768]{1,0:T(8,128)(2,1)} %broadcast_select_fusion), channel_id=1, source_target_pairs={{0,16},{8,24},{16,0},{24,8},{1,17},{9,25},{17,1},{25,9},{2,18},{10... | collective-permute-start | bytes 8257544 | tf_op jit(solution)/shard_map/ppermute | solution.py:535
  509.4 46.7 %collective-permute-start.13 = (bf16[768,1536]{1,0:T(8,128)(2,1)}, bf16[768,1536]{1,0:T(8,128)(2,1)}, u32[]{:S(2)}, u32[]{:S(2)}) collective-permute-start(bf16[768,1536]{1,0:T(8,128)(2,1)} %half_product.8), channel_id=1, source_target_pairs={{0,8},{8,0},{16,24},{24,16},{1,9},{9,1},{17,25},{25,17},{2,10},{10... | collective-permute-start | bytes 7077896 | tf_op jit(solution)/shard_map/ppermute | solution.py:517
  521.3 42.2 %all-to-all-start.9 = ((bf16[4,1,192,384]{3,2,1,0:T(8,128)(2,1)}), bf16[4,1,192,384]{3,2,1,0:T(8,128)(2,1)}, u32[]{:S(2)}, u32[]{:S(2)}) async-start(bf16[4,1,192,384]{3,2,1,0:T(8,128)(2,1)} %bitcast.68), calls=%async_computation.9 | async-start | bytes 1179648 | tf_op jit(solution)/shard_map/all_to_all | solution.py:610
  569.5 67.6 %all-to-all-start.11 = ((bf16[4,448,768]{2,1,0:T(8,128)(2,1)}), bf16[4,448,768]{2,1,0:T(8,128)(2,1)}, u32[]{:S(2)}, u32[]{:S(2)}) async-start(bf16[4,448,768]{2,1,0:T(8,128)(2,1)} %bitcast.376), calls=%async_computation.11 | async-start | bytes 5505024 | tf_op jit(solution)/shard_map/all_to_all | solution.py:503
  574.8 66.5 %collective-permute-start.12 = (bf16[384,1536]{1,0:T(8,128)(2,1)}, bf16[384,1536]{1,0:T(8,128)(2,1)}, u32[]{:S(2)}, u32[]{:S(2)}) collective-permute-start(bf16[384,1536]{1,0:T(8,128)(2,1)} %convolution_convert_fusion.9), channel_id=1, source_target_pairs={{0,1},{1,0},{2,3},{3,2},{4,5},{5,4},{6,7},{7,6},{8,9},{9,8},{10,11... | collective-permute-start | bytes 3538952 | tf_op jit(solution)/shard_map/ppermute | solution.py:422
  608.2 73.0 %collective-permute-start.20 = (bf16[384,3072]{1,0:T(8,128)(2,1)}, bf16[384,3072]{1,0:T(8,128)(2,1)}, u32[]{:S(2)}, u32[]{:S(2)}) collective-permute-start(bf16[384,3072]{1,0:T(8,128)(2,1)} %broadcast_select_fusion.1), channel_id=1, source_target_pairs={{0,16},{8,24},{16,0},{24,8},{1,17},{9,25},{17,1},{25,9},{2,18},{10... | collective-permute-start | bytes 7077896 | tf_op jit(solution)/shard_map/ppermute | solution.py:535
  669.5 186.4 %all-gather.11.cloned.1.call-start = ((), (), s32[]{:S(2)}) async-start(), calls=%async_computation.19 | async-start | bytes 11698176 | tf_op jit(solution)/shard_map/all_gather | solution.py:902
  696.6 94.8 %all-to-all-start.13 = ((bf16[4,96,3072]{2,1,0:T(8,128)(2,1)}), bf16[4,96,3072]{2,1,0:T(8,128)(2,1)}, u32[]{:S(2)}, u32[]{:S(2)}) async-start(bf16[4,96,3072]{2,1,0:T(8,128)(2,1)} %bitcast.377), calls=%async_computation.13 | async-start | bytes 4718592 | tf_op jit(solution)/shard_map/all_to_all | solution.py:503
  724.7 68.8 %collective-permute-start.22 = (bf16[384,1536]{1,0:T(8,128)(2,1)}, bf16[384,1536]{1,0:T(8,128)(2,1)}, u32[]{:S(2)}, u32[]{:S(2)}) collective-permute-start(bf16[384,1536]{1,0:T(8,128)(2,1)} %convolution_convert_fusion.7), channel_id=1, source_target_pairs={{0,1},{1,0},{2,3},{3,2},{4,5},{5,4},{6,7},{7,6},{8,9},{9,8},{10,11... | collective-permute-start | bytes 3538952 | tf_op jit(solution)/shard_map/ppermute | solution.py:422
  732.4 59.0 %collective-permute-start.23 = (f32[104,128]{1,0:T(8,128)}, f32[104,128]{1,0:T(8,128)}, u32[]{:S(2)}, u32[]{:S(2)}) collective-permute-start(f32[104,128]{1,0:T(8,128)} %add.607), channel_id=1, source_target_pairs={{0,16},{8,24},{16,0},{24,8},{1,17},{9,25},{17,1},{25,9},{2,18},{10... | collective-permute-start | bytes 159752 | tf_op jit(solution)/shard_map/ppermute | solution.py:489
  747.5 77.4 %collective-permute-start.25 = (bf16[384,2048]{1,0:T(8,128)(2,1)}, bf16[384,2048]{1,0:T(8,128)(2,1)}, u32[]{:S(2)}, u32[]{:S(2)}) collective-permute-start(bf16[384,2048]{1,0:T(8,128)(2,1)} %broadcast_select_fusion.4), channel_id=1, source_target_pairs={{0,16},{8,24},{16,0},{24,8},{1,17},{9,25},{17,1},{25,9},{2,18},{10... | collective-permute-start | bytes 4718600 | tf_op jit(solution)/shard_map/ppermute | solution.py:535
  800.9 38.3 %all-to-all-start.15 = ((f32[4,1,896]{2,1,0:T(1,128)}), f32[4,1,896]{2,1,0:T(1,128)}, u32[]{:S(2)}, u32[]{:S(2)}) async-start(f32[4,1,896]{2,1,0:T(1,128)} %broadcast_in_dim.32), calls=%async_computation.15 | async-start | bytes 28672 | tf_op jit(solution)/shard_map/all_to_all | solution.py:1029
  839.2 42.5 %all-to-all-start.14 = ((bf16[4,96,2048]{2,1,0:T(8,128)(2,1)}), bf16[4,96,2048]{2,1,0:T(8,128)(2,1)S(1)}, u32[]{:S(2)}, u32[]{:S(2)}) async-start(bf16[4,96,2048]{2,1,0:T(8,128)(2,1)} %bitcast.88), calls=%async_computation.14 | async-start | bytes 3145728 | tf_op jit(solution)/shard_map/all_to_all | solution.py:503
  (240 other events, 2463.3 us)
Sparse Core Ops, SparseCore 0:
  43.0 24.9 all-gather.4
  102.7 58.1 all-gather.8
  170.3 26.8 all-gather.6
  696.7 137.3 all-gather.10

commit v5 on v4

--- a/solution.py
+++ b/solution.py
@@ -684,7 +684,10 @@
         )
         for h in range(heads)
     ]
-    w_grad = jnp.concatenate([w[:, :GRAD_PACK] for w in w_packs], axis=1)
+
+    def grad_weights(_):
+        parts["w_grad"] = done(jnp.concatenate([w[:, :GRAD_PACK] for w in w_packs], axis=1))
+
     pack_scale = jnp.concatenate(
         [jnp.ones((VD + KD,), jnp.float32), jnp.full((2 * KD,), key_scale, jnp.float32)]
     )
@@ -828,7 +831,7 @@
         packed_grads[g] = after_line(packed_grads[g])
         product = lax.dot_general(
             packed_grads[g],
-            w_grad,
+            parts["w_grad"],
             (((0,), (1,)), ((), ())),
             preferred_element_type=jnp.float32,
         )
@@ -984,7 +987,7 @@
     if count == 3:
         plan = one(fetch_out) + [(project, 0)] + one(fetch_out_share, fetch_heads)
         plan += [(project, 1), (project, 2)] + one(spread_bias) + [(attend, 0), (attend, 1)]
-        plan += one(fetch_human_share) + [(attend_swap, 0)] + one(fetch_out_end)
+        plan += one(fetch_human_share, grad_weights) + [(attend_swap, 0)] + one(fetch_out_end)
         plan += [(feed_forward, 0)] + one(fetch_mouse_share) + [(attend, 2), (attend_swap, 1)]
         plan += [(feed_forward, 1), (attend_swap, 2)] + one(fetch_heads_end)
         plan += [(score, 0), (feed_forward, 2), (back_hidden, 0)]
@@ -1001,7 +1004,7 @@
         plan += one(sums_late, grads_pack_seq, step_late, grads_wide_end, step_late)
         plan += one(heads_out, step_late, grads_pack_end, step_late)
     else:
-        plan = one(fetch_out, fetch_out_share, fetch_out_end, spread_bias)
+        plan = one(fetch_out, fetch_out_share, fetch_out_end, spread_bias, grad_weights)
         plan += one(fetch_heads, fetch_human_share, fetch_mouse_share, fetch_heads_end)
         plan += each(project) + each(attend) + each(attend_swap) + each(feed_forward) + each(score)
         plan += each(back_hidden) + each(back_mid)

time: 899 us -> 901 us (level); the launches traced: 903 us -> 886 us
  waiting for transfers between devices: 187 us -> 160 us
  Pallas kernels: 224 us -> 245 us
  starting transfers between devices: 120 us -> 109 us
    ppermute x3, starting transfers between devices: 24 us -> 3.47 us  [__init__(): lax.ppermute(done(jnp.where(upper, low, high)), 'dp', swap_pairs('dp', 2))]
    pallas_call x3, Pallas kernels: 68.2 us -> 85.6 us  [score_heads(): pl.pallas_call(lambda *refs: heads_kernel(track_human, track_mouse, *refs...]
    all_to_all x12, waiting for transfers between devices: 54.2 us -> 40.2 us  [exchange(): return lax.all_to_all(array, 'seq', split_axis=0, concat_axis=0, tiled=True)]
    ppermute x1, starting transfers between devices: 0.01 us -> 9.53 us  [grads_heads(): got = lax.ppermute(done(sent), 'dp', swap_pairs('dp', 1))]
    ppermute x3, waiting for transfers between devices: 30.1 us -> 20.9 us  [in_model_order(): other = lax.ppermute(own, 'mp', [(0, 1), (1, 0)])]
  transfers between devices with their start and end apart: 49 -> 49, of which waited for: 17 -> 16; matrix products, arithmetic and copies ran while one was open for 32% -> 33% of each run, Pallas kernels for 24% -> 27%
where the time goes in v5:
time: 901 us; the launch traced here: 886 us
  Pallas kernels  245 us (27%)
  waiting for transfers between devices  160 us (18%)
  other arithmetic  152 us (17%)
  starting transfers between devices  109 us (12%)
  matrix products  106 us (12%)
  local copies, waits for them, and re-layouts  88.4 us (10%)
  between operations  25.4 us (3%)
    dot_general x31, matrix products, mxu(): lax.dot_general(left_arr, right_arr, dims, precision=precision, preferred...  88.4 us
    pallas_call x3, Pallas kernels, score_heads(): pl.pallas_call(lambda *refs: heads_kernel(track_human, track_mouse, *refs...  85.6 us
    all_to_all x3, waiting for transfers between devices, __init__(): lax.all_to_all(done(parts), 'seq', split_axis=0, concat_axis=0, tiled=True)  82 us
    all_to_all x12, starting transfers between devices, exchange(): return lax.all_to_all(array, 'seq', split_axis=0, concat_axis=0, tiled=True)  55.2 us
    pallas_call x8, Pallas kernels, half_product(): pl.pallas_call(lambda *refs: half_product_kernel(windows, turned, more is...  53.9 us
    pallas_call x3, Pallas kernels, attend_backward(): pl.pallas_call(lambda *refs: attend_backward_kernel(block, bins, *refs),...  53.6 us
    all_to_all x12, waiting for transfers between devices, exchange(): return lax.all_to_all(array, 'seq', split_axis=0, concat_axis=0, tiled=True)  40.2 us
    unnamed x454, local copies, waits for them, and re-layouts  38.3 us
  transfers between devices with their start and end apart: 49, of which 16 were waited for; matrix products, arithmetic and copies ran while one was open for 33% of the time, Pallas kernels for 27%

profile of v5, /device:TPU:0, one launch (start us, length us, event | category | flops | bytes accessed | tf_op | source)
XLA Modules:
  0.0 885.6 jit_solution(11286359322236050192)
XLA Ops:
  50.7 8.9 %all-to-all-done = bf16[4,1,384,384]{3,2,1,0:T(8,128)(2,1)S(1)} async-done(((bf16[4,1,384,384]{3,2,1,0:T(8,128)(2,1)}), bf16[4,1,384,384]{3,2,1,0:T(8,128)(2,1)S(1)}, u32[]{:S(2)}, u32[]{:S(2)}) %all-to-all-start) | async-done | bytes 1179680 | tf_op jit(solution)/shard_map/all_to_all | solution.py:610
  82.0 10.4 %attend_forward.3 = (bf16[4,192,384]{2,1,0:T(8,128)(2,1)}, bf16[1536,1536]{1,0:T(8,128)(2,1)}) custom-call(bf16[1536,384]{1,0:T(8,128)(2,1)S(1)} %bitcast.336, bf16[3072,64]{1,0:T(8,128)(2,1)S(1)} %convolution_convert_fusion.refs_1_), custom_call_target="tpu_custom_call" | custom-call | flops 1 | bytes 1 | tf_op jit(solution)/shard_map/attend_forward/pallas_call | solution.py:84
  92.4 10.2 %attend_forward.4 = (bf16[4,192,384]{2,1,0:T(8,128)(2,1)S(1)}, bf16[1536,1536]{1,0:T(8,128)(2,1)}) custom-call(bf16[1536,384]{1,0:T(8,128)(2,1)S(1)} %bitcast.334, bf16[3072,64]{1,0:T(8,128)(2,1)S(1)} %convolution_convert_fusion.refs_1_), custom_call_target="tpu_custom_call" | custom-call | flops 1 | bytes 1 | tf_op jit(solution)/shard_map/attend_forward/pallas_call | solution.py:84
  108.6 9.5 %concatenate.136 = bf16[1536,1280]{1,0:T(8,128)(2,1)} concatenate(bf16[1536,192]{1,0:T(8,128)(2,1)S(1)} %copy-done.107, bf16[1536,64]{1,0:T(8,128)(2,1)} %copy-done.120, bf16[1536,64]{1,0:T(8,128)(2,1)} %copy-done.138, bf16[1536,192]{1,0:T(8,128)(2,1)} %copy-done.108, bf16[1536,64]{1,0:T(8,128)(2,1)} %copy-done.122, bf16[1536,64]{1,0:T(8,128)(2,1)} %copy-done.135, ...), dimensions={1} | concatenate | bytes 7864320 | tf_op jit(solution)/shard_map/concatenate | solution.py:689
  131.6 15.2 %collective-permute-done.2 = bf16[768,384]{1,0:T(8,128)(2,1)S(1)} collective-permute-done((bf16[768,384]{1,0:T(8,128)(2,1)}, bf16[768,384]{1,0:T(8,128)(2,1)S(1)}, u32[]{:S(2)}, u32[]{:S(2)}) %collective-permute-start.2) | collective-permute-done | bytes 589856 | tf_op jit(solution)/shard_map/ppermute | solution.py:431
  170.2 10.4 %attend_forward.5 = (bf16[4,192,384]{2,1,0:T(8,128)(2,1)}, bf16[1536,1536]{1,0:T(8,128)(2,1)}) custom-call(bf16[1536,384]{1,0:T(8,128)(2,1)S(1)} %bitcast.338, bf16[3072,64]{1,0:T(8,128)(2,1)S(1)} %convolution_convert_fusion.refs_1_), custom_call_target="tpu_custom_call" | custom-call | flops 1 | bytes 1 | tf_op jit(solution)/shard_map/attend_forward/pallas_call | solution.py:84
  215.2 7.3 collective-permute-done.3
  227.7 34.5 %score_heads.3 = (bf16[7168,384]{1,0:T(8,128)(2,1)}, f32[384,1536]{1,0:T(8,128)}, f32[8,7168]{1,0:T(8,128)}, f32[8,384]{1,0:T(8,128)}) custom-call(s32[2]{0:T(128)} %get-tuple-element.825.refs_0_, bf16[384,1536]{1,0:T(8,128)(2,1)} %get-tuple-element.744.refs_1_, f32[8,384]{1,0:T(8,128)} %broadcast_in_dim.29.refs_2_, bf16[5313,768]{1,0:T(8,128)(2,1)} %bitcast.362, ...), custom_call_target="tpu_custom_call" | custom-call | flops 1 | bytes 1 | tf_op jit(solution)/shard_map/score_heads/pallas_call | solution.py:270
  289.0 16.4 %score_heads.4 = (bf16[7168,384]{1,0:T(8,128)(2,1)}, f32[384,1536]{1,0:T(8,128)}, f32[8,7168]{1,0:T(8,128)}, f32[8,384]{1,0:T(8,128)}) custom-call(s32[2]{0:T(128)} %get-tuple-element.826.refs_0_, bf16[384,1536]{1,0:T(8,128)(2,1)} %get-tuple-element.742.refs_1_, f32[8,384]{1,0:T(8,128)} %broadcast_in_dim.29.refs_2_, bf16[5313,768]{1,0:T(8,128)(2,1)} %bitcast.363, ...), custom_call_target="tpu_custom_call" | custom-call | flops 1 | bytes 1 | tf_op jit(solution)/shard_map/score_heads/pallas_call | solution.py:270
  312.7 5.9 convolution_convert_fusion.2
  346.4 34.7 %score_heads.5 = (bf16[7168,384]{1,0:T(8,128)(2,1)}, f32[384,1536]{1,0:T(8,128)}, f32[8,7168]{1,0:T(8,128)}, f32[8,384]{1,0:T(8,128)}) custom-call(s32[2]{0:T(128)} %pad_add_fusion.2.refs_0_, bf16[384,1536]{1,0:T(8,128)(2,1)} %get-tuple-element.740.refs_1_, f32[8,384]{1,0:T(8,128)} %broadcast_in_dim.29.refs_2_, bf16[5313,768]{1,0:T(8,128)(2,1)} %bitcast.364, ...), custom_call_target="tpu_custom_call" | custom-call | flops 1 | bytes 1 | tf_op jit(solution)/shard_map/score_heads/pallas_call | solution.py:270
  383.9 9.8 %head_grads.2 = bf16[3584,768]{1,0:T(8,128)(2,1)} custom-call(s32[4]{0:T(128)S(1)} %get-tuple-element.811.refs_0_, bf16[7168,384]{1,0:T(8,128)(2,1)S(1)} %copy-done.1, bf16[7168,384]{1,0:T(8,128)(2,1)} %get-tuple-element.410.refs_2_, bf16[7168,384]{1,0:T(8,128)(2,1)} %get-tuple-element.411.refs_3_, bf16[3,384,768]{2,1,0:T(8,128)(2,1)S(1)} %pad_maximum_fusion.3.refs_4_), custom_call_target="tpu_custom_call" | custom-call | flops 1 | bytes 1 | tf_op jit(solution)/shard_map/head_grads/pallas_call | solution.py:338
  393.8 9.5 %collective-permute-start.11 = (bf16[3584,768]{1,0:T(8,128)(2,1)}, bf16[3584,768]{1,0:T(8,128)(2,1)}, u32[]{:S(2)}, u32[]{:S(2)}) collective-permute-start(bf16[3584,768]{1,0:T(8,128)(2,1)} %head_grads.2), channel_id=1, source_target_pairs={{0,8},{8,0},{16,24},{24,16},{1,9},{9,1},{17,25},{25,17},{2,10},{10... | collective-permute-start | bytes 16515080 | tf_op jit(solution)/shard_map/ppermute | solution.py:884
  406.8 17.9 %attend_backward.3 = (bf16[4,320,384]{2,1,0:T(8,128)(2,1)S(1)}, f32[64,3072]{1,0:T(8,128)S(1)}, f32[8,128]{1,0:T(8,128)S(1)}) custom-call(bf16[1536,384]{1,0:T(8,128)(2,1)S(1)} %bitcast.337, bf16[3072,64]{1,0:T(8,128)(2,1)S(1)} %convolution_convert_fusion.refs_1_, bf16[1536,1536]{1,0:T(8,128)(2,1)} %get-tuple-element.401.refs_2_, ...), custom_call_target="tpu_custom_call" | custom-call | flops 1 | bytes 1 | tf_op jit(solution)/shard_map/attend_backward/pallas_call | solution.py:163
  437.1 6.0 convolution_convert_fusion.1
  444.4 10.7 %head_grads.3 = bf16[3584,768]{1,0:T(8,128)(2,1)S(1)} custom-call(s32[4]{0:T(128)S(1)} %get-tuple-element.810.refs_0_, bf16[7168,384]{1,0:T(8,128)(2,1)S(1)} %bitcast.333, bf16[7168,384]{1,0:T(8,128)(2,1)} %get-tuple-element.410.refs_2_, bf16[7168,384]{1,0:T(8,128)(2,1)} %get-tuple-element.411.refs_3_, bf16[3,384,768]{2,1,0:T(8,128)(2,1)S(1)} %pad_maximum_fusion.3.refs_4_, ...), custom_call_target="tpu_custom_call" | custom-call | flops 1 | bytes 1 | tf_op jit(solution)/shard_map/head_grads/pallas_call | solution.py:338
  485.0 7.1 half_product.8
  511.9 17.9 %attend_backward.4 = (bf16[4,320,384]{2,1,0:T(8,128)(2,1)S(1)}, f32[64,3072]{1,0:T(8,128)S(1)}, f32[8,128]{1,0:T(8,128)S(1)}) custom-call(bf16[1536,384]{1,0:T(8,128)(2,1)S(1)} %bitcast.335, bf16[3072,64]{1,0:T(8,128)(2,1)S(1)} %convolution_convert_fusion.refs_1_, bf16[1536,1536]{1,0:T(8,128)(2,1)} %get-tuple-element.443.refs_2_, ...), custom_call_target="tpu_custom_call" | custom-call | flops 1 | bytes 1 | tf_op jit(solution)/shard_map/attend_backward/pallas_call | solution.py:163
  531.7 7.1 half_product.9
  538.9 7.4 half_product.10
  546.3 6.0 add_convert_fusion
  560.4 17.9 %attend_backward.5 = (bf16[4,320,384]{2,1,0:T(8,128)(2,1)S(1)}, f32[64,3072]{1,0:T(8,128)S(1)}, f32[8,128]{1,0:T(8,128)S(1)}) custom-call(bf16[1536,384]{1,0:T(8,128)(2,1)S(1)} %bitcast.339, bf16[3072,64]{1,0:T(8,128)(2,1)S(1)} %convolution_convert_fusion.refs_1_, bf16[1536,1536]{1,0:T(8,128)(2,1)} %get-tuple-element.461.refs_2_, ...), custom_call_target="tpu_custom_call" | custom-call | flops 1 | bytes 1 | tf_op jit(solution)/shard_map/attend_backward/pallas_call | solution.py:163
  578.4 7.7 half_product.11
  591.2 28.7 %all-to-all-done.11 = bf16[4,448,768]{2,1,0:T(8,128)(2,1)} async-done(((bf16[4,448,768]{2,1,0:T(8,128)(2,1)}), bf16[4,448,768]{2,1,0:T(8,128)(2,1)}, u32[]{:S(2)}, u32[]{:S(2)}) %all-to-all-start.11) | async-done | bytes 2752544 | tf_op jit(solution)/shard_map/all_to_all | solution.py:503
  631.9 16.1 %all-to-all-done.10 = bf16[4,1,320,384]{3,2,1,0:T(8,128)(2,1)} async-done(((bf16[4,1,320,384]{3,2,1,0:T(8,128)(2,1)}), bf16[4,1,320,384]{3,2,1,0:T(8,128)(2,1)}, u32[]{:S(2)}, u32[]{:S(2)}) %all-to-all-start.10) | async-done | bytes 983072 | tf_op jit(solution)/shard_map/all_to_all | solution.py:610
  668.8 7.3 all-to-all-done.12
  684.2 7.3 half_product.14
  716.8 7.7 half_product.15
  730.6 43.4 %all-to-all-done.13 = bf16[4,96,3072]{2,1,0:T(8,128)(2,1)} async-done(((bf16[4,96,3072]{2,1,0:T(8,128)(2,1)}), bf16[4,96,3072]{2,1,0:T(8,128)(2,1)}, u32[]{:S(2)}, u32[]{:S(2)}) %all-to-all-start.13) | async-done | bytes 2359328 | tf_op jit(solution)/shard_map/all_to_all | solution.py:503
  789.6 6.0 fusion.51
  838.6 10.7 %slice_convert_fusion = f32[5313,768]{1,0:T(8,128)} fusion(bf16[7168,768]{1,0:T(8,128)(2,1)} %all-gather.11.cloned.1.call-done), kind=kLoop, calls=%fused_computation | loop fusion | flops 4080384 | bytes 24482304 | tf_op jit(solution)/shard_map/convert_element_type | solution.py:978
  854.5 9.9 %all-to-all-done.14 = bf16[4,96,2048]{2,1,0:T(8,128)(2,1)S(1)} async-done(((bf16[4,96,2048]{2,1,0:T(8,128)(2,1)}), bf16[4,96,2048]{2,1,0:T(8,128)(2,1)S(1)}, u32[]{:S(2)}, u32[]{:S(2)}) %all-to-all-start.14) | async-done | bytes 1572896 | tf_op jit(solution)/shard_map/all_to_all | solution.py:503
  (756 shorter events, 434.8 us)
Async XLA Ops:
  9.7 33.1 %collective-permute-start = (bf16[192,1536]{1,0:T(8,128)(2,1)}, bf16[192,1536]{1,0:T(8,128)(2,1)}, u32[]{:S(2)}, u32[]{:S(2)}) collective-permute-start(bf16[192,1536]{1,0:T(8,128)(2,1)} %select_select_fusion), channel_id=1, source_target_pairs={{0,1},{1,0},{2,3},{3,2},{4,5},{5,4},{6,7},{7,6},{8,9},{9,8},{10,11... | collective-permute-start | bytes 1769480 | tf_op jit(solution)/shard_map/ppermute | solution.py:455
  26.5 33.1 %all-to-all-start = ((bf16[4,1,384,384]{3,2,1,0:T(8,128)(2,1)}), bf16[4,1,384,384]{3,2,1,0:T(8,128)(2,1)S(1)}, u32[]{:S(2)}, u32[]{:S(2)}) async-start(bf16[4,1,384,384]{3,2,1,0:T(8,128)(2,1)} %bitcast.14), calls=%async_computation | async-start | bytes 2359296 | tf_op jit(solution)/shard_map/all_to_all | solution.py:610
  31.3 97.3 %all-gather.5.cloned.1.call-start = ((), (), s32[]{:S(2)}) async-start(), calls=%async_computation.16 | async-start | bytes 2949120 | tf_op jit(solution)/shard_map/all_gather | solution.py:458
  49.9 52.8 %collective-permute-start.1 = (bf16[1344,768]{1,0:T(8,128)(2,1)}, bf16[1344,768]{1,0:T(8,128)(2,1)}, u32[]{:S(2)}, u32[]{:S(2)}) collective-permute-start(bf16[1344,768]{1,0:T(8,128)(2,1)} %fusion.70), channel_id=1, source_target_pairs={{0,1},{1,0},{2,3},{3,2},{4,5},{5,4},{6,7},{7,6},{8,9},{9,8},{10,11... | collective-permute-start | bytes 6193160 | tf_op jit(solution)/shard_map/ppermute | solution.py:455
  59.6 32.8 %all-to-all-start.2 = ((bf16[4,1,384,384]{3,2,1,0:T(8,128)(2,1)}), bf16[4,1,384,384]{3,2,1,0:T(8,128)(2,1)S(1)}, u32[]{:S(2)}, u32[]{:S(2)}) async-start(bf16[4,1,384,384]{3,2,1,0:T(8,128)(2,1)} %bitcast.33), calls=%async_computation.2 | async-start | bytes 2359296 | tf_op jit(solution)/shard_map/all_to_all | solution.py:610
  63.1 152.0 %all-gather.9.cloned.1.call-start = ((), (), s32[]{:S(2)}) async-start(), calls=%async_computation.18 | async-start | bytes 10321920 | tf_op jit(solution)/shard_map/all_gather | solution.py:458
  118.1 52.0 %collective-permute-start.4 = (bf16[448,768]{1,0:T(8,128)(2,1)}, bf16[448,768]{1,0:T(8,128)(2,1)}, u32[]{:S(2)}, u32[]{:S(2)}) collective-permute-start(bf16[448,768]{1,0:T(8,128)(2,1)} %fusion.129), channel_id=1, source_target_pairs={{0,1},{1,0},{2,3},{3,2},{4,5},{5,4},{6,7},{7,6},{8,9},{9,8},{10,11... | collective-permute-start | bytes 2064392 | tf_op jit(solution)/shard_map/ppermute | solution.py:455
  160.0 55.2 %all-gather.7.cloned.1.call-start = ((), (), s32[]{:S(2)}) async-start(), calls=%async_computation.17 | async-start | bytes 3440640 | tf_op jit(solution)/shard_map/all_gather | solution.py:458
  185.2 37.3 %collective-permute-start.3 = (bf16[384,1536]{1,0:T(8,128)(2,1)}, bf16[384,1536]{1,0:T(8,128)(2,1)}, u32[]{:S(2)}, u32[]{:S(2)}) collective-permute-start(bf16[384,1536]{1,0:T(8,128)(2,1)} %convolution_convert_fusion.6), channel_id=1, source_target_pairs={{0,1},{1,0},{2,3},{3,2},{4,5},{5,4},{6,7},{7,6},{8,9},{9,8},{10,11... | collective-permute-start | bytes 3538952 | tf_op jit(solution)/shard_map/ppermute | solution.py:422
  213.1 69.8 %collective-permute-start.6 = (bf16[384,1536]{1,0:T(8,128)(2,1)}, bf16[384,1536]{1,0:T(8,128)(2,1)}, u32[]{:S(2)}, u32[]{:S(2)}) collective-permute-start(bf16[384,1536]{1,0:T(8,128)(2,1)} %convolution_convert_fusion.5), channel_id=1, source_target_pairs={{0,1},{1,0},{2,3},{3,2},{4,5},{5,4},{6,7},{7,6},{8,9},{9,8},{10,11... | collective-permute-start | bytes 3538952 | tf_op jit(solution)/shard_map/ppermute | solution.py:422
  213.9 48.3 %collective-permute-start.7 = (bf16[768,384]{1,0:T(8,128)(2,1)S(1)}, bf16[768,384]{1,0:T(8,128)(2,1)S(1)}, u32[]{:S(2)}, u32[]{:S(2)}) collective-permute-start(bf16[768,384]{1,0:T(8,128)(2,1)S(1)} %bitcast.344), channel_id=1, source_target_pairs={{0,1},{1,0},{2,3},{3,2},{4,5},{5,4},{6,7},{7,6},{8,9},{9,8},{10,11... | collective-permute-start | bytes 1769480 | tf_op jit(solution)/shard_map/ppermute | solution.py:431
  287.0 33.5 %collective-permute-start.9 = (bf16[384,1536]{1,0:T(8,128)(2,1)}, bf16[384,1536]{1,0:T(8,128)(2,1)}, u32[]{:S(2)}, u32[]{:S(2)}) collective-permute-start(bf16[384,1536]{1,0:T(8,128)(2,1)} %convolution_convert_fusion.3), channel_id=1, source_target_pairs={{0,1},{1,0},{2,3},{3,2},{4,5},{5,4},{6,7},{7,6},{8,9},{9,8},{10,11... | collective-permute-start | bytes 3538952 | tf_op jit(solution)/shard_map/ppermute | solution.py:422
  287.8 47.0 %collective-permute-start.8 = (bf16[384,1536]{1,0:T(8,128)(2,1)}, bf16[384,1536]{1,0:T(8,128)(2,1)}, u32[]{:S(2)}, u32[]{:S(2)}) collective-permute-start(bf16[384,1536]{1,0:T(8,128)(2,1)} %convolution_convert_fusion.4), channel_id=1, source_target_pairs={{0,1},{1,0},{2,3},{3,2},{4,5},{5,4},{6,7},{7,6},{8,9},{9,8},{10,11... | collective-permute-start | bytes 3538952 | tf_op jit(solution)/shard_map/ppermute | solution.py:422
  336.9 44.5 %all-to-all-start.6 = ((bf16[4,1,192,384]{3,2,1,0:T(8,128)(2,1)}), bf16[4,1,192,384]{3,2,1,0:T(8,128)(2,1)S(1)}, u32[]{:S(2)}, u32[]{:S(2)}) async-start(bf16[4,1,192,384]{3,2,1,0:T(8,128)(2,1)} %bitcast.51), calls=%async_computation.6 | async-start | bytes 1179648 | tf_op jit(solution)/shard_map/all_to_all | solution.py:610
  393.8 50.6 %collective-permute-start.11 = (bf16[3584,768]{1,0:T(8,128)(2,1)}, bf16[3584,768]{1,0:T(8,128)(2,1)}, u32[]{:S(2)}, u32[]{:S(2)}) collective-permute-start(bf16[3584,768]{1,0:T(8,128)(2,1)} %head_grads.2), channel_id=1, source_target_pairs={{0,8},{8,0},{16,24},{24,16},{1,9},{9,1},{17,25},{25,17},{2,10},{10... | collective-permute-start | bytes 16515080 | tf_op jit(solution)/shard_map/ppermute | solution.py:884
  403.3 55.8 %collective-permute-start.10 = (bf16[384,1536]{1,0:T(8,128)(2,1)}, bf16[384,1536]{1,0:T(8,128)(2,1)}, u32[]{:S(2)}, u32[]{:S(2)}) collective-permute-start(bf16[384,1536]{1,0:T(8,128)(2,1)} %convolution_convert_fusion.2), channel_id=1, source_target_pairs={{0,1},{1,0},{2,3},{3,2},{4,5},{5,4},{6,7},{7,6},{8,9},{9,8},{10,11... | collective-permute-start | bytes 3538952 | tf_op jit(solution)/shard_map/ppermute | solution.py:422
  426.6 44.0 %all-to-all-start.7 = ((bf16[4,1,320,384]{3,2,1,0:T(8,128)(2,1)}), bf16[4,1,320,384]{3,2,1,0:T(8,128)(2,1)S(1)}, u32[]{:S(2)}, u32[]{:S(2)}) async-start(bf16[4,1,320,384]{3,2,1,0:T(8,128)(2,1)} %bitcast.355), calls=%async_computation.7 | async-start | bytes 1966080 | tf_op jit(solution)/shard_map/all_to_all | solution.py:610
  443.0 49.1 %collective-permute-start.14 = (bf16[384,1536]{1,0:T(8,128)(2,1)}, bf16[384,1536]{1,0:T(8,128)(2,1)}, u32[]{:S(2)}, u32[]{:S(2)}) collective-permute-start(bf16[384,1536]{1,0:T(8,128)(2,1)} %convolution_convert_fusion.1), channel_id=1, source_target_pairs={{0,1},{1,0},{2,3},{3,2},{4,5},{5,4},{6,7},{7,6},{8,9},{9,8},{10,11... | collective-permute-start | bytes 3538952 | tf_op jit(solution)/shard_map/ppermute | solution.py:422
  471.7 32.3 %all-to-all-start.8 = ((bf16[4,1,192,384]{3,2,1,0:T(8,128)(2,1)}), bf16[4,1,192,384]{3,2,1,0:T(8,128)(2,1)S(1)}, u32[]{:S(2)}, u32[]{:S(2)}) async-start(bf16[4,1,192,384]{3,2,1,0:T(8,128)(2,1)} %bitcast.64), calls=%async_computation.8 | async-start | bytes 1179648 | tf_op jit(solution)/shard_map/all_to_all | solution.py:610
  477.1 69.2 %collective-permute-start.16 = (bf16[1792,768]{1,0:T(8,128)(2,1)}, bf16[1792,768]{1,0:T(8,128)(2,1)}, u32[]{:S(2)}, u32[]{:S(2)}) collective-permute-start(bf16[1792,768]{1,0:T(8,128)(2,1)} %broadcast_select_fusion), channel_id=1, source_target_pairs={{0,16},{8,24},{16,0},{24,8},{1,17},{9,25},{17,1},{25,9},{2,18},{10... | collective-permute-start | bytes 8257544 | tf_op jit(solution)/shard_map/ppermute | solution.py:535
  492.1 46.7 %collective-permute-start.13 = (bf16[768,1536]{1,0:T(8,128)(2,1)}, bf16[768,1536]{1,0:T(8,128)(2,1)}, u32[]{:S(2)}, u32[]{:S(2)}) collective-permute-start(bf16[768,1536]{1,0:T(8,128)(2,1)} %half_product.8), channel_id=1, source_target_pairs={{0,8},{8,0},{16,24},{24,16},{1,9},{9,1},{17,25},{25,17},{2,10},{10... | collective-permute-start | bytes 7077896 | tf_op jit(solution)/shard_map/ppermute | solution.py:517
  504.0 42.3 %all-to-all-start.9 = ((bf16[4,1,192,384]{3,2,1,0:T(8,128)(2,1)}), bf16[4,1,192,384]{3,2,1,0:T(8,128)(2,1)}, u32[]{:S(2)}, u32[]{:S(2)}) async-start(bf16[4,1,192,384]{3,2,1,0:T(8,128)(2,1)} %bitcast.68), calls=%async_computation.9 | async-start | bytes 1179648 | tf_op jit(solution)/shard_map/all_to_all | solution.py:610
  552.2 67.6 %all-to-all-start.11 = ((bf16[4,448,768]{2,1,0:T(8,128)(2,1)}), bf16[4,448,768]{2,1,0:T(8,128)(2,1)}, u32[]{:S(2)}, u32[]{:S(2)}) async-start(bf16[4,448,768]{2,1,0:T(8,128)(2,1)} %bitcast.376), calls=%async_computation.11 | async-start | bytes 5505024 | tf_op jit(solution)/shard_map/all_to_all | solution.py:503
  557.6 66.6 %collective-permute-start.12 = (bf16[384,1536]{1,0:T(8,128)(2,1)}, bf16[384,1536]{1,0:T(8,128)(2,1)}, u32[]{:S(2)}, u32[]{:S(2)}) collective-permute-start(bf16[384,1536]{1,0:T(8,128)(2,1)} %convolution_convert_fusion.9), channel_id=1, source_target_pairs={{0,1},{1,0},{2,3},{3,2},{4,5},{5,4},{6,7},{7,6},{8,9},{9,8},{10,11... | collective-permute-start | bytes 3538952 | tf_op jit(solution)/shard_map/ppermute | solution.py:422
  591.0 72.9 %collective-permute-start.20 = (bf16[384,3072]{1,0:T(8,128)(2,1)}, bf16[384,3072]{1,0:T(8,128)(2,1)}, u32[]{:S(2)}, u32[]{:S(2)}) collective-permute-start(bf16[384,3072]{1,0:T(8,128)(2,1)} %broadcast_select_fusion.1), channel_id=1, source_target_pairs={{0,16},{8,24},{16,0},{24,8},{1,17},{9,25},{17,1},{25,9},{2,18},{10... | collective-permute-start | bytes 7077896 | tf_op jit(solution)/shard_map/ppermute | solution.py:535
  652.3 186.4 %all-gather.11.cloned.1.call-start = ((), (), s32[]{:S(2)}) async-start(), calls=%async_computation.19 | async-start | bytes 11698176 | tf_op jit(solution)/shard_map/all_gather | solution.py:905
  679.4 94.6 %all-to-all-start.13 = ((bf16[4,96,3072]{2,1,0:T(8,128)(2,1)}), bf16[4,96,3072]{2,1,0:T(8,128)(2,1)}, u32[]{:S(2)}, u32[]{:S(2)}) async-start(bf16[4,96,3072]{2,1,0:T(8,128)(2,1)} %bitcast.377), calls=%async_computation.13 | async-start | bytes 4718592 | tf_op jit(solution)/shard_map/all_to_all | solution.py:503
  707.6 68.5 %collective-permute-start.22 = (bf16[384,1536]{1,0:T(8,128)(2,1)}, bf16[384,1536]{1,0:T(8,128)(2,1)}, u32[]{:S(2)}, u32[]{:S(2)}) collective-permute-start(bf16[384,1536]{1,0:T(8,128)(2,1)} %convolution_convert_fusion.7), channel_id=1, source_target_pairs={{0,1},{1,0},{2,3},{3,2},{4,5},{5,4},{6,7},{7,6},{8,9},{9,8},{10,11... | collective-permute-start | bytes 3538952 | tf_op jit(solution)/shard_map/ppermute | solution.py:422
  715.2 58.9 %collective-permute-start.23 = (f32[104,128]{1,0:T(8,128)}, f32[104,128]{1,0:T(8,128)}, u32[]{:S(2)}, u32[]{:S(2)}) collective-permute-start(f32[104,128]{1,0:T(8,128)} %add.607), channel_id=1, source_target_pairs={{0,16},{8,24},{16,0},{24,8},{1,17},{9,25},{17,1},{25,9},{2,18},{10... | collective-permute-start | bytes 159752 | tf_op jit(solution)/shard_map/ppermute | solution.py:489
  730.3 77.3 %collective-permute-start.25 = (bf16[384,2048]{1,0:T(8,128)(2,1)}, bf16[384,2048]{1,0:T(8,128)(2,1)}, u32[]{:S(2)}, u32[]{:S(2)}) collective-permute-start(bf16[384,2048]{1,0:T(8,128)(2,1)} %broadcast_select_fusion.4), channel_id=1, source_target_pairs={{0,16},{8,24},{16,0},{24,8},{1,17},{9,25},{17,1},{25,9},{2,18},{10... | collective-permute-start | bytes 4718600 | tf_op jit(solution)/shard_map/ppermute | solution.py:535
  783.6 38.2 %all-to-all-start.15 = ((f32[4,1,896]{2,1,0:T(1,128)}), f32[4,1,896]{2,1,0:T(1,128)}, u32[]{:S(2)}, u32[]{:S(2)}) async-start(f32[4,1,896]{2,1,0:T(1,128)} %broadcast_in_dim.32), calls=%async_computation.15 | async-start | bytes 28672 | tf_op jit(solution)/shard_map/all_to_all | solution.py:1032
  821.8 42.6 %all-to-all-start.14 = ((bf16[4,96,2048]{2,1,0:T(8,128)(2,1)}), bf16[4,96,2048]{2,1,0:T(8,128)(2,1)S(1)}, u32[]{:S(2)}, u32[]{:S(2)}) async-start(bf16[4,96,2048]{2,1,0:T(8,128)(2,1)} %bitcast.88), calls=%async_computation.14 | async-start | bytes 3145728 | tf_op jit(solution)/shard_map/all_to_all | solution.py:503
  (240 other events, 2370.5 us)
Sparse Core Ops, SparseCore 0:
  42.9 24.9 all-gather.4
  102.8 58.1 all-gather.8
  170.3 26.8 all-gather.6
  679.5 137.3 all-gather.10
